TPU v7x, 32 devices: a whole 2x2x4 slice. The times are simulated.
32 devices in a mesh: row: 4 (over y, core), col: 8 (over z, x).
Axes of the slice: x: 2, y: 2, z: 4, core: 2. Of those that a mesh axis runs over, the one named last changes fastest.
Arguments:
- fock_tiles: bfloat16 [256, 15, 128, 128], P(('row', 'col')), may hold values from -6 to 6
- fock_pattern: int32 [256, 15], replicated, may hold values from -1 to 255, as said below
- basis_tiles: bfloat16 [256, 15, 128, 128], P(('row', 'col')), may hold values from -0.25 to 0.25
- basis_pattern: int32 [256, 15], replicated, may hold values from -1 to 255, as said below
- product_pattern: int32 [256, 15], replicated, may hold values from -1 to 255, as said below
- result_pattern: int32 [256, 15], replicated, may hold values from -1 to 255, as said below
- new_index: int32 [256], replicated, may hold values from 0 to 255, as said below
Outputs:
- fock_orth: bfloat16 [256, 15, 128, 128], P(('row', 'col'))
Inputs may be any that keep to these rules, and one draw needn't show every extreme that they name: `fock_pattern`: the filled slots of a tile row i come first and hold distinct tile columns within the (16) columns starting at min(max(i - 8, 0), 240); slot 0 holds column i; from 10 to 15 slots of a row are filled, and the rest hold -1. `basis_pattern`: as for fock_pattern. `product_pattern`: as for fock_pattern. `result_pattern`: as for fock_pattern. `new_index`: A permutation; each tile row's new index lies in the same block of 64 consecutive tile rows and has the same remainder modulo 8; the 8 consecutive tile rows starting at a multiple of 8 move into 8 different blocks of 8 rows.
All inputs are finite; a program needn't handle non-finite values.
Results may differ from a plain program's by a relative error of at most 0.0065.
Values may be sent and summed in bfloat16 or wider, within the bound.
No kernel may reach another device: no remote copies, remote signals or barrier semaphores. Data moves between devices by JAX's collectives and lax.ppermute only.
A program may use at most 192 MiB of HBM per device.

v0:
```python
import jax
import jax.numpy as jnp
from jax import lax
from jax.sharding import PartitionSpec as P

H = 8


def padded(block, sides, width):
    for axis, dim in sides:
        count = lax.axis_size(axis)
        forward = [(i, i + 1) for i in range(count - 1)]
        backward = [(target, source) for source, target in forward]
        low = lax.ppermute(
            lax.slice_in_dim(block, block.shape[dim] - width, None, axis=dim), axis, forward
        )
        high = lax.ppermute(lax.slice_in_dim(block, 0, width, axis=dim), axis, backward)
        block = jnp.concatenate([low, block, high], axis=dim)
    return block


def body(
    fock_tiles, fock_pattern, basis_tiles, basis_pattern, product_pattern, result_pattern, new_index
):
    rows_dev = fock_tiles.shape[0]
    total_rows = fock_pattern.shape[0]
    reach = H
    near_count = rows_dev + 2 * reach
    device = lax.axis_index(("row", "col"))
    first_row = device * rows_dev
    near_start = first_row - reach
    fock_cols = lax.dynamic_slice_in_dim(fock_pattern, first_row, rows_dev, 0)
    prod_cols = lax.dynamic_slice_in_dim(product_pattern, first_row, rows_dev, 0)
    basis_near = padded(basis_tiles, ((("row", "col"), 0),), reach)

    def first_product(inputs):
        row_fock_cols, row_prod_cols, row_fock = inputs
        near_index = jnp.clip(row_fock_cols - near_start, 0, near_count - 1)
        gathered = basis_near[near_index]
        gathered_cols = basis_pattern[jnp.clip(row_fock_cols, 0, total_rows - 1)]
        match = (
            (gathered_cols[:, None, :] == row_prod_cols[None, :, None])
            & (row_prod_cols[None, :, None] >= 0)
            & (row_fock_cols[:, None, None] >= 0)
        )
        chosen = jnp.einsum(
            "kps,ksab->kpab",
            match.astype(jnp.bfloat16),
            gathered,
            preferred_element_type=jnp.float32,
        ).astype(jnp.bfloat16)
        return jnp.einsum(
            "kab,kpbc->pac", row_fock, chosen, preferred_element_type=jnp.float32
        ).astype(jnp.bfloat16)

    product = lax.map(first_product, (fock_cols, prod_cols, fock_tiles))
    product_near = padded(product, ((("row", "col"), 0),), reach)
    near_rows = near_start + jnp.arange(near_count, dtype=jnp.int32)
    inside = (near_rows >= 0) & (near_rows < total_rows)
    clipped = jnp.clip(near_rows, 0, total_rows - 1)
    near_basis_cols = jnp.where(inside[:, None], basis_pattern[clipped], -1)
    near_prod_cols = jnp.where(inside[:, None], product_pattern[clipped], -1)
    own_result_cols = lax.dynamic_slice_in_dim(result_pattern, first_row, rows_dev, 0)

    def pull_row(local_row, owned):
        target = first_row + local_row
        pick_basis = (near_basis_cols == target).astype(jnp.bfloat16)
        column_tiles = jnp.einsum(
            "js,jsab->jab", pick_basis, basis_near, preferred_element_type=jnp.float32
        ).astype(jnp.bfloat16)
        row_result_cols = lax.dynamic_index_in_dim(own_result_cols, local_row, 0, keepdims=False)
        second = (near_prod_cols[:, None, :] == row_result_cols[None, :, None]) & (
            row_result_cols[None, :, None] >= 0
        )
        picked = jnp.einsum(
            "jrp,jpab->jrab",
            second.astype(jnp.bfloat16),
            product_near,
            preferred_element_type=jnp.float32,
        ).astype(jnp.bfloat16)
        tiles_row = jnp.einsum(
            "jba,jrbc->rac", column_tiles, picked, preferred_element_type=jnp.float32
        )
        return lax.dynamic_update_index_in_dim(owned, tiles_row, local_row, 0)

    owned = lax.fori_loop(0, rows_dev, pull_row, jnp.zeros(fock_tiles.shape, jnp.float32))
    orth = owned.astype(jnp.bfloat16)
    width = lax.axis_size("col")
    own_new = lax.dynamic_slice_in_dim(new_index, first_row, rows_dev, 0)
    destinations = own_new // rows_dev % width
    select = destinations[None, :] == jnp.arange(width, dtype=jnp.int32)[:, None]
    source_slot = jnp.sum(
        select.astype(jnp.int32) * jnp.arange(rows_dev, dtype=jnp.int32)[None, :], axis=1
    )
    present = jnp.sum(select.astype(jnp.int32), axis=1) > 0
    outgoing = orth[source_slot] * present.astype(jnp.bfloat16)[:, None, None, None]
    incoming = lax.all_to_all(outgoing, "col", split_axis=0, concat_axis=0, tiled=True)
    wanted = first_row + jnp.arange(rows_dev, dtype=jnp.int32)
    found = new_index[None, :] == wanted[:, None]
    anchor = jnp.sum(
        found.astype(jnp.int32) * jnp.arange(total_rows, dtype=jnp.int32)[None, :], axis=1
    )
    anchor_col = anchor // rows_dev % width
    return incoming[anchor_col]


def solution(mesh):
    placed = (
        P(("row", "col"), None, None, None),
        P(),
        P(("row", "col"), None, None, None),
        P(),
        P(),
        P(),
        P(),
    )
    return jax.shard_map(
        body,
        mesh=mesh,
        in_specs=placed,
        out_specs=P(("row", "col"), None, None, None),
        check_vma=False,
    )
```

profile of v0, /device:TPU:14, one launch (start us, length us, event | category | flops | bytes accessed | tf_op | source)
XLA Modules:
  0.0 901.3 jit_solution(421615313505187610)
XLA Ops:
  0.0 3.6 collective-permute-start
  7.9 165.4 %collective-permute-done = bf16[8,15,128,128]{3,2,1,0:T(8,128)(2,1)} collective-permute-done((bf16[8,15,128,128]{3,2,1,0:T(8,128)(2,1)}, bf16[8,15,128,128]{3,2,1,0:T(8,128)(2,1)}, u32[]{:S(2)}, u32[]{:S(2)}) %collective-permute-start) | collective-permute-done | bytes 3932192 | tf_op jit(solution)/shard_map/ppermute | solution.py:14
  176.3 2.9 constant_dynamic-update-slice_fusion.2
  179.2 4.3 copy-done.2
  183.5 182.4 %while.23 = (s32[]{:T(128)}, bf16[8,15,128,128]{3,2,1,0:T(8,128)(2,1)}, s32[8,15]{1,0:T(8,128)S(1)}, s32[256,15]{1,0:T(8,128)S(1)}, s32[8,15]{1,0:T(8,128)S(1)},...) while((s32[]{:T(128)}, ...), condition=%wide.region_1.2_spmd, body=%wide.region_0.1_spmd.sunk | while | flops 1058254912 | bytes 39825864 | solution.py:56
  183.5 8.8 gather_fusion
  192.9 8.1 fusion.73
  201.0 4.1 fusion.74
  206.3 8.8 gather_fusion
  215.7 8.1 fusion.73
  223.8 4.2 fusion.74
  229.1 8.8 gather_fusion
  238.5 8.1 fusion.73
  246.6 4.2 fusion.74
  251.9 8.8 gather_fusion
  261.3 8.1 fusion.73
  269.4 4.1 fusion.74
  274.7 8.8 gather_fusion
  284.1 8.1 fusion.73
  292.2 4.1 fusion.74
  297.5 8.8 gather_fusion
  306.9 8.1 fusion.73
  315.0 4.2 fusion.74
  320.3 8.8 gather_fusion
  329.7 8.1 fusion.73
  337.8 4.1 fusion.74
  343.1 8.8 gather_fusion
  352.5 8.1 fusion.73
  360.6 4.1 fusion.74
  365.9 2.4 collective-permute-start.2
  368.3 3.4 collective-permute-start.3
  373.5 164.7 %collective-permute-done.2 = bf16[8,15,128,128]{3,2,1,0:T(8,128)(2,1)} collective-permute-done((bf16[8,15,128,128]{3,2,1,0:T(8,128)(2,1)}, bf16[8,15,128,128]{3,2,1,0:T(8,128)(2,1)}, u32[]{:S(2)}, u32[]{:S(2)}) %collective-permute-start.2) | collective-permute-done | bytes 3932192 | tf_op jit(solution)/shard_map/ppermute | solution.py:14
  538.2 6.0 pad_maximum_fusion
  544.2 9.5 %copy.73 = bf16[24,15,128,128]{3,1,2,0:T(8,128)(2,1)} copy(bf16[24,15,128,128]{3,2,1,0:T(8,128)(2,1)S(1)} %pad_maximum_fusion) | data formatting | bytes 23592960 | tf_op jit(solution)/shard_map/while | solution.py:86
  553.7 243.3 %while.24 = (s32[]{:T(128)}, bf16[8,15,128,128]{3,2,1,0:T(8,128)(2,1)}, s32[24,15]{1,0:T(8,128)S(1)}, s32[8,15]{1,0:T(8,128)S(1)}, bf16[24,15,128,128]{3,1,2,0:T...) while((s32[]{:T(128)}, ...), condition=%wide.region_3.4_spmd, body=%wide.region_2.3_spmd.sunk | while | flops 1704995712 | bytes 99980360 | solution.py:86
  553.7 12.5 %convolution_convert_fusion.2 = bf16[24,15,128,128]{3,1,2,0:T(8,128)(2,1)} fusion(bf16[24,15,128,128]{3,1,2,0:T(8,128)(2,1)} %get-tuple-element.477, s32[24,15]{1,0:T(8,128)S(1)} %get-tuple-element.475, s32[15]{0:T(128)S(1)} %get-tuple-element.426, pred[15]{0:T(512)(128)(4,1)S(1)} %get-tuple-element.427), kind=kOutput, calls=%fused_computation.10.clone.1 | convolution fusion | flops 182856240 | bytes 23594476 | tf_op jit(solution)/shard_map/while/body/eval_jaxpr/jrp,jpab->jrab/dot_general | solution.py:75
  566.3 11.6 %fusion.81 = f32[24,1,128,128]{3,1,2,0:T(1,128)S(1)} fusion(pred[24,15,1,1]{1,2,3,0:T(4,128)(4,1)S(1)} %copy.119, bf16[24,15,128,128]{3,2,1,0:T(8,128)(2,1)} %get-tuple-element.480), kind=kOutput, calls=%fused_computation.6.clone.1 | convolution fusion | flops 11796480 | bytes 13369704 | tf_op jit(solution)/shard_map/while/body/eval_jaxpr/js,jsab->jab/dot_general | solution.py:68
  578.0 5.0 fusion.82
  584.1 12.5 %convolution_convert_fusion.2 = bf16[24,15,128,128]{3,1,2,0:T(8,128)(2,1)} fusion(bf16[24,15,128,128]{3,1,2,0:T(8,128)(2,1)} %get-tuple-element.477, s32[24,15]{1,0:T(8,128)S(1)} %get-tuple-element.475, s32[15]{0:T(128)S(1)} %get-tuple-element.426, pred[15]{0:T(512)(128)(4,1)S(1)} %get-tuple-element.427), kind=kOutput, calls=%fused_computation.10.clone.1 | convolution fusion | flops 182856240 | bytes 23594476 | tf_op jit(solution)/shard_map/while/body/eval_jaxpr/jrp,jpab->jrab/dot_general | solution.py:75
  596.8 11.6 %fusion.81 = f32[24,1,128,128]{3,1,2,0:T(1,128)S(1)} fusion(pred[24,15,1,1]{1,2,3,0:T(4,128)(4,1)S(1)} %copy.119, bf16[24,15,128,128]{3,2,1,0:T(8,128)(2,1)} %get-tuple-element.480), kind=kOutput, calls=%fused_computation.6.clone.1 | convolution fusion | flops 11796480 | bytes 13369704 | tf_op jit(solution)/shard_map/while/body/eval_jaxpr/js,jsab->jab/dot_general | solution.py:68
  608.4 5.0 fusion.82
  614.5 12.5 %convolution_convert_fusion.2 = bf16[24,15,128,128]{3,1,2,0:T(8,128)(2,1)} fusion(bf16[24,15,128,128]{3,1,2,0:T(8,128)(2,1)} %get-tuple-element.477, s32[24,15]{1,0:T(8,128)S(1)} %get-tuple-element.475, s32[15]{0:T(128)S(1)} %get-tuple-element.426, pred[15]{0:T(512)(128)(4,1)S(1)} %get-tuple-element.427), kind=kOutput, calls=%fused_computation.10.clone.1 | convolution fusion | flops 182856240 | bytes 23594476 | tf_op jit(solution)/shard_map/while/body/eval_jaxpr/jrp,jpab->jrab/dot_general | solution.py:75
  627.2 11.6 %fusion.81 = f32[24,1,128,128]{3,1,2,0:T(1,128)S(1)} fusion(pred[24,15,1,1]{1,2,3,0:T(4,128)(4,1)S(1)} %copy.119, bf16[24,15,128,128]{3,2,1,0:T(8,128)(2,1)} %get-tuple-element.480), kind=kOutput, calls=%fused_computation.6.clone.1 | convolution fusion | flops 11796480 | bytes 13369704 | tf_op jit(solution)/shard_map/while/body/eval_jaxpr/js,jsab->jab/dot_general | solution.py:68
  638.8 5.0 fusion.82
  644.9 12.5 %convolution_convert_fusion.2 = bf16[24,15,128,128]{3,1,2,0:T(8,128)(2,1)} fusion(bf16[24,15,128,128]{3,1,2,0:T(8,128)(2,1)} %get-tuple-element.477, s32[24,15]{1,0:T(8,128)S(1)} %get-tuple-element.475, s32[15]{0:T(128)S(1)} %get-tuple-element.426, pred[15]{0:T(512)(128)(4,1)S(1)} %get-tuple-element.427), kind=kOutput, calls=%fused_computation.10.clone.1 | convolution fusion | flops 182856240 | bytes 23594476 | tf_op jit(solution)/shard_map/while/body/eval_jaxpr/jrp,jpab->jrab/dot_general | solution.py:75
  657.6 11.6 %fusion.81 = f32[24,1,128,128]{3,1,2,0:T(1,128)S(1)} fusion(pred[24,15,1,1]{1,2,3,0:T(4,128)(4,1)S(1)} %copy.119, bf16[24,15,128,128]{3,2,1,0:T(8,128)(2,1)} %get-tuple-element.480), kind=kOutput, calls=%fused_computation.6.clone.1 | convolution fusion | flops 11796480 | bytes 13369704 | tf_op jit(solution)/shard_map/while/body/eval_jaxpr/js,jsab->jab/dot_general | solution.py:68
  669.2 5.0 fusion.82
  675.4 12.5 %convolution_convert_fusion.2 = bf16[24,15,128,128]{3,1,2,0:T(8,128)(2,1)} fusion(bf16[24,15,128,128]{3,1,2,0:T(8,128)(2,1)} %get-tuple-element.477, s32[24,15]{1,0:T(8,128)S(1)} %get-tuple-element.475, s32[15]{0:T(128)S(1)} %get-tuple-element.426, pred[15]{0:T(512)(128)(4,1)S(1)} %get-tuple-element.427), kind=kOutput, calls=%fused_computation.10.clone.1 | convolution fusion | flops 182856240 | bytes 23594476 | tf_op jit(solution)/shard_map/while/body/eval_jaxpr/jrp,jpab->jrab/dot_general | solution.py:75
  688.0 11.6 %fusion.81 = f32[24,1,128,128]{3,1,2,0:T(1,128)S(1)} fusion(pred[24,15,1,1]{1,2,3,0:T(4,128)(4,1)S(1)} %copy.119, bf16[24,15,128,128]{3,2,1,0:T(8,128)(2,1)} %get-tuple-element.480), kind=kOutput, calls=%fused_computation.6.clone.1 | convolution fusion | flops 11796480 | bytes 13369704 | tf_op jit(solution)/shard_map/while/body/eval_jaxpr/js,jsab->jab/dot_general | solution.py:68
  699.6 5.0 fusion.82
  705.8 12.5 %convolution_convert_fusion.2 = bf16[24,15,128,128]{3,1,2,0:T(8,128)(2,1)} fusion(bf16[24,15,128,128]{3,1,2,0:T(8,128)(2,1)} %get-tuple-element.477, s32[24,15]{1,0:T(8,128)S(1)} %get-tuple-element.475, s32[15]{0:T(128)S(1)} %get-tuple-element.426, pred[15]{0:T(512)(128)(4,1)S(1)} %get-tuple-element.427), kind=kOutput, calls=%fused_computation.10.clone.1 | convolution fusion | flops 182856240 | bytes 23594476 | tf_op jit(solution)/shard_map/while/body/eval_jaxpr/jrp,jpab->jrab/dot_general | solution.py:75
  718.4 11.6 %fusion.81 = f32[24,1,128,128]{3,1,2,0:T(1,128)S(1)} fusion(pred[24,15,1,1]{1,2,3,0:T(4,128)(4,1)S(1)} %copy.119, bf16[24,15,128,128]{3,2,1,0:T(8,128)(2,1)} %get-tuple-element.480), kind=kOutput, calls=%fused_computation.6.clone.1 | convolution fusion | flops 11796480 | bytes 13369704 | tf_op jit(solution)/shard_map/while/body/eval_jaxpr/js,jsab->jab/dot_general | solution.py:68
  730.1 5.0 fusion.82
  736.2 12.5 %convolution_convert_fusion.2 = bf16[24,15,128,128]{3,1,2,0:T(8,128)(2,1)} fusion(bf16[24,15,128,128]{3,1,2,0:T(8,128)(2,1)} %get-tuple-element.477, s32[24,15]{1,0:T(8,128)S(1)} %get-tuple-element.475, s32[15]{0:T(128)S(1)} %get-tuple-element.426, pred[15]{0:T(512)(128)(4,1)S(1)} %get-tuple-element.427), kind=kOutput, calls=%fused_computation.10.clone.1 | convolution fusion | flops 182856240 | bytes 23594476 | tf_op jit(solution)/shard_map/while/body/eval_jaxpr/jrp,jpab->jrab/dot_general | solution.py:75
  748.8 11.6 %fusion.81 = f32[24,1,128,128]{3,1,2,0:T(1,128)S(1)} fusion(pred[24,15,1,1]{1,2,3,0:T(4,128)(4,1)S(1)} %copy.119, bf16[24,15,128,128]{3,2,1,0:T(8,128)(2,1)} %get-tuple-element.480), kind=kOutput, calls=%fused_computation.6.clone.1 | convolution fusion | flops 11796480 | bytes 13369704 | tf_op jit(solution)/shard_map/while/body/eval_jaxpr/js,jsab->jab/dot_general | solution.py:68
  760.5 5.0 fusion.82
  766.6 12.5 %convolution_convert_fusion.2 = bf16[24,15,128,128]{3,1,2,0:T(8,128)(2,1)} fusion(bf16[24,15,128,128]{3,1,2,0:T(8,128)(2,1)} %get-tuple-element.477, s32[24,15]{1,0:T(8,128)S(1)} %get-tuple-element.475, s32[15]{0:T(128)S(1)} %get-tuple-element.426, pred[15]{0:T(512)(128)(4,1)S(1)} %get-tuple-element.427), kind=kOutput, calls=%fused_computation.10.clone.1 | convolution fusion | flops 182856240 | bytes 23594476 | tf_op jit(solution)/shard_map/while/body/eval_jaxpr/jrp,jpab->jrab/dot_general | solution.py:75
  779.3 11.6 %fusion.81 = f32[24,1,128,128]{3,1,2,0:T(1,128)S(1)} fusion(pred[24,15,1,1]{1,2,3,0:T(4,128)(4,1)S(1)} %copy.119, bf16[24,15,128,128]{3,2,1,0:T(8,128)(2,1)} %get-tuple-element.480), kind=kOutput, calls=%fused_computation.6.clone.1 | convolution fusion | flops 11796480 | bytes 13369704 | tf_op jit(solution)/shard_map/while/body/eval_jaxpr/js,jsab->jab/dot_general | solution.py:68
  790.9 5.0 fusion.82
  797.0 5.0 gather_fusion.4
  802.0 4.4 broadcast_multiply_fusion
  806.4 6.3 all-to-all-start
  812.9 83.3 %all-to-all-done = bf16[8,15,128,128]{3,2,1,0:T(8,128)(2,1)} async-done(((bf16[8,15,128,128]{3,2,1,0:T(8,128)(2,1)}), bf16[8,15,128,128]{3,2,1,0:T(8,128)(2,1)}, u32[]{:S(2)}, u32[]{:S(2)}) %all-to-all-start) | async-done | bytes 3932192 | tf_op jit(solution)/shard_map/all_to_all | solution.py:97
  896.2 5.1 gather_fusion.5
  (154 shorter events, 32.6 us)
Async XLA Ops:
  0.0 6.8 copy-start
  0.0 173.3 %collective-permute-start = (bf16[8,15,128,128]{3,2,1,0:T(8,128)(2,1)}, bf16[8,15,128,128]{3,2,1,0:T(8,128)(2,1)}, u32[]{:S(2)}, u32[]{:S(2)}) collective-permute-start(bf16[8,15,128,128]{3,2,1,0:T(8,128)(2,1)} %param.13), channel_id=1, source_target_pairs={{0,1},{1,2},{2,3},{3,4},{4,5},{5,6},{6,7},{7,8},{8,9},{9,10},{10,1... | collective-permute-start | bytes 11796488 | tf_op jit(solution)/shard_map/ppermute | solution.py:14
  3.6 172.7 %collective-permute-start.1 = (bf16[8,15,128,128]{3,2,1,0:T(8,128)(2,1)}, bf16[8,15,128,128]{3,2,1,0:T(8,128)(2,1)}, u32[]{:S(2)}, u32[]{:S(2)}) collective-permute-start(bf16[8,15,128,128]{3,2,1,0:T(8,128)(2,1)} %param.13), channel_id=1, source_target_pairs={{1,0},{2,1},{3,2},{4,3},{5,4},{6,5},{7,6},{8,7},{9,8},{10,9},{11,1... | collective-permute-start | bytes 11796488 | tf_op jit(solution)/shard_map/ppermute | solution.py:17
  7.8 167.9 %copy-start.4 = (bf16[8,15,128,128]{3,2,1,0:T(8,128)(2,1)S(1)}, bf16[8,15,128,128]{3,2,1,0:T(8,128)(2,1)}, u32[]{:S(2)}) copy-start(bf16[8,15,128,128]{3,2,1,0:T(8,128)(2,1)} %param.13) | copy-start | bytes 11796484
  179.2 4.3 copy-start.2
  183.5 188.3 %copy-start.6 = (s32[256]{0:T(256)S(1)}, s32[256]{0:T(256)}, u32[]{:S(2)}) copy-start(s32[256]{0:T(256)} %param.17) | copy-start | bytes 3076
  183.5 189.9 %copy-start.5 = (s32[256,15]{0,1:T(8,128)S(1)}, s32[256,15]{0,1:T(8,128)}, u32[]{:S(2)}) copy-start(s32[256,15]{0,1:T(8,128)} %param.16) | copy-start | bytes 46084
  365.9 172.3 %collective-permute-start.2 = (bf16[8,15,128,128]{3,2,1,0:T(8,128)(2,1)}, bf16[8,15,128,128]{3,2,1,0:T(8,128)(2,1)}, u32[]{:S(2)}, u32[]{:S(2)}) collective-permute-start(bf16[8,15,128,128]{3,2,1,0:T(8,128)(2,1)} %get-tuple-element.186), channel_id=1, source_target_pairs={{0,1},{1,2},{2,3},{3,4},{4,5},{5,6},{6,7},{7,8},{8,9},{9,10},{10,1... | collective-permute-start | bytes 11796488 | tf_op jit(solution)/shard_map/ppermute | solution.py:14
  368.3 169.9 %collective-permute-start.3 = (bf16[8,15,128,128]{3,2,1,0:T(8,128)(2,1)}, bf16[8,15,128,128]{3,2,1,0:T(8,128)(2,1)}, u32[]{:S(2)}, u32[]{:S(2)}) collective-permute-start(bf16[8,15,128,128]{3,2,1,0:T(8,128)(2,1)} %get-tuple-element.186), channel_id=1, source_target_pairs={{1,0},{2,1},{3,2},{4,3},{5,4},{6,5},{7,6},{8,7},{9,8},{10,9},{11,1... | collective-permute-start | bytes 11796488 | tf_op jit(solution)/shard_map/ppermute | solution.py:17
  566.3 11.6 %copy-start.3 = (bf16[24,15,128,128]{3,1,2,0:T(8,128)(2,1)S(1)}, bf16[24,15,128,128]{3,1,2,0:T(8,128)(2,1)}, u32[]{:S(2)}) copy-start(bf16[24,15,128,128]{3,1,2,0:T(8,128)(2,1)} %convolution_convert_fusion.2) | copy-start | bytes 35389444 | tf_op jit(solution)/shard_map/while
  596.7 11.6 %copy-start.3 = (bf16[24,15,128,128]{3,1,2,0:T(8,128)(2,1)S(1)}, bf16[24,15,128,128]{3,1,2,0:T(8,128)(2,1)}, u32[]{:S(2)}) copy-start(bf16[24,15,128,128]{3,1,2,0:T(8,128)(2,1)} %convolution_convert_fusion.2) | copy-start | bytes 35389444 | tf_op jit(solution)/shard_map/while
  627.2 11.6 %copy-start.3 = (bf16[24,15,128,128]{3,1,2,0:T(8,128)(2,1)S(1)}, bf16[24,15,128,128]{3,1,2,0:T(8,128)(2,1)}, u32[]{:S(2)}) copy-start(bf16[24,15,128,128]{3,1,2,0:T(8,128)(2,1)} %convolution_convert_fusion.2) | copy-start | bytes 35389444 | tf_op jit(solution)/shard_map/while
  657.6 11.6 %copy-start.3 = (bf16[24,15,128,128]{3,1,2,0:T(8,128)(2,1)S(1)}, bf16[24,15,128,128]{3,1,2,0:T(8,128)(2,1)}, u32[]{:S(2)}) copy-start(bf16[24,15,128,128]{3,1,2,0:T(8,128)(2,1)} %convolution_convert_fusion.2) | copy-start | bytes 35389444 | tf_op jit(solution)/shard_map/while
  688.0 11.6 %copy-start.3 = (bf16[24,15,128,128]{3,1,2,0:T(8,128)(2,1)S(1)}, bf16[24,15,128,128]{3,1,2,0:T(8,128)(2,1)}, u32[]{:S(2)}) copy-start(bf16[24,15,128,128]{3,1,2,0:T(8,128)(2,1)} %convolution_convert_fusion.2) | copy-start | bytes 35389444 | tf_op jit(solution)/shard_map/while
  718.4 11.6 %copy-start.3 = (bf16[24,15,128,128]{3,1,2,0:T(8,128)(2,1)S(1)}, bf16[24,15,128,128]{3,1,2,0:T(8,128)(2,1)}, u32[]{:S(2)}) copy-start(bf16[24,15,128,128]{3,1,2,0:T(8,128)(2,1)} %convolution_convert_fusion.2) | copy-start | bytes 35389444 | tf_op jit(solution)/shard_map/while
  748.8 11.6 %copy-start.3 = (bf16[24,15,128,128]{3,1,2,0:T(8,128)(2,1)S(1)}, bf16[24,15,128,128]{3,1,2,0:T(8,128)(2,1)}, u32[]{:S(2)}) copy-start(bf16[24,15,128,128]{3,1,2,0:T(8,128)(2,1)} %convolution_convert_fusion.2) | copy-start | bytes 35389444 | tf_op jit(solution)/shard_map/while
  779.2 11.6 %copy-start.3 = (bf16[24,15,128,128]{3,1,2,0:T(8,128)(2,1)S(1)}, bf16[24,15,128,128]{3,1,2,0:T(8,128)(2,1)}, u32[]{:S(2)}) copy-start(bf16[24,15,128,128]{3,1,2,0:T(8,128)(2,1)} %convolution_convert_fusion.2) | copy-start | bytes 35389444 | tf_op jit(solution)/shard_map/while
  806.4 6.3 copy-start.7
  806.4 89.8 %all-to-all-start = ((bf16[8,15,128,128]{3,2,1,0:T(8,128)(2,1)}), bf16[8,15,128,128]{3,2,1,0:T(8,128)(2,1)}, u32[]{:S(2)}, u32[]{:S(2)}) async-start(bf16[8,15,128,128]{3,2,1,0:T(8,128)(2,1)} %broadcast_multiply_fusion), calls=%async_computation | async-start | bytes 7864320 | tf_op jit(solution)/shard_map/all_to_all | solution.py:97
  812.9 88.4 %copy-start.1 = (s32[256,15]{0,1:T(8,128)S(1)}, s32[256,15]{0,1:T(8,128)}, u32[]{:S(2)}) copy-start(s32[256,15]{0,1:T(8,128)} %param.12) | copy-start | bytes 46084
where the time goes:
time: 910 us; the launch traced here: 901 us
  waiting for transfers between devices  413 us (45%)
  matrix products  331 us (36%)
  local copies, waits for them, and re-layouts  126 us (14%)
  starting transfers between devices  18.1 us (2%)
  other arithmetic  11.4 us (1%)
    ppermute x2, waiting for transfers between devices, padded(): lax.ppermute(lax.slice_in_dim(block, block.shape[dim] - width, None, axis...  330 us
    dot_general x8, matrix products, pull_row(): jnp.einsum('jrp,jpab->jrab', second.astype(jnp.bfloat16), product_near, p...  100 us
    dot_general x8, matrix products, pull_row(): jnp.einsum('js,jsab->jab', pick_basis, basis_near, preferred_element_type...  93.1 us
    all_to_all x1, waiting for transfers between devices, body(): lax.all_to_all(outgoing, 'col', split_axis=0, concat_axis=0, tiled=True)  83.3 us
    gather x8, local copies, waits for them, and re-layouts, first_product(): gathered = basis_near[near_index]  70.4 us
    dot_general x8, matrix products, first_product(): jnp.einsum('kps,ksab->kpab', match.astype(jnp.bfloat16), gathered, prefer...  64.7 us
    dot_general x8, matrix products, pull_row(): jnp.einsum('jba,jrbc->rac', column_tiles, picked, preferred_element_type=...  40.2 us
    dot_general x8, matrix products, first_product(): jnp.einsum('kab,kpbc->pac', row_fock, chosen, preferred_element_type=jnp....  33.2 us
  transfers between devices with their start and end apart: 5, of which 3 were waited for; matrix products, arithmetic and copies ran while one was open for 1% of the time, Pallas kernels for 0%

commit v1 on v0

v1 whole, which is shorter than its diff:
```python
import functools

import jax
import jax.numpy as jnp
from jax import lax
from jax.experimental import pallas as pl
from jax.experimental.pallas import tpu as pltpu
from jax.sharding import PartitionSpec as P

H = 8
AXES = ("row", "col")
COST_SCALE = 3_000_000


def layout(rows, cols):
    def place(v):
        g, n = divmod(v, cols)
        return (2 * (g // 2) + n % 2) * cols + 2 * (n // 2) + g % 2

    def beside(v):
        return v + 1 if v % 2 else v - 1

    total = rows * cols
    moved = [place(v) != v for v in range(total)]
    edge = [v % cols in (0, cols - 1) for v in range(total)]
    has_outer = [0 <= beside(v) < total for v in range(total)]
    return {
        "swap": [(v, place(v)) for v in range(total) if moved[v]],
        "mate_a": [(place(v), place(v ^ 1)) for v in range(total) if not moved[v]],
        "mate_b": [(place(v), place(v ^ 1)) for v in range(total) if moved[v]],
        "pair": [(place(v), place(v ^ 1)) for v in range(total)],
        "far_a": [(v, place(beside(v))) for v in range(total) if has_outer[v] and (edge[v] or not moved[v])],
        "far_b": [(place(v), place(beside(v))) for v in range(total) if has_outer[v] and moved[v] and not edge[v]],
        "outer": [(place(v), place(beside(v))) for v in range(total) if has_outer[v]],
        "shifts": [[(place(v), v // cols * cols + (v + s) % cols) for v in range(total)] for s in range(cols)],
    }


BASE, ODD, MOVED, FAR_A = range(4)


def widths(slots, rows, low):
    return [min(slots, 2 * H - 1 - t if low else H + t) for t in range(rows)]


def pack_tables(pattern, base, low, packed_tiles):
    rows, slots = pattern.shape[1:]
    tables = [widths(slots, rows, side) for side in (False, True)]
    width = jnp.where(low[:, None], jnp.array(tables[1]), jnp.array(tables[0]))
    starts = [[sum(table[:t]) for t in range(rows)] for table in tables]
    offset = jnp.where(low[:, None], jnp.array(starts[1]), jnp.array(starts[0]))
    beyond = jnp.where(low[:, None, None], pattern <= base[:, None, None] + H - 2, pattern >= base[:, None, None])
    wanted = (pattern >= 0) & beyond
    earlier = jnp.arange(slots)[None, :] < jnp.arange(slots)[:, None]
    rank = jnp.sum((wanted[:, :, None, :] & earlier).astype(jnp.int32), axis=-1)
    place = jnp.where(wanted & (rank < width[:, :, None]), offset[:, :, None] + rank, -1)
    hit = place.reshape(-1, 1, rows * slots) == jnp.arange(packed_tiles)[None, :, None]
    col_of = jnp.max(jnp.where(hit, pattern.reshape(-1, 1, rows * slots), 0), axis=-1)
    return place, col_of


def spread(pattern, values, origin, span, empty):
    at = pattern[:, :, None] - origin == jnp.arange(span)
    found = jnp.max(jnp.where(at & (pattern >= 0)[:, :, None], values[:, :, None], -1), axis=1)
    return jnp.where(found >= 0, found, empty).astype(jnp.int32)


def either(flag, first, second, act):
    @pl.when(flag != 0)
    def _():
        act(first)

    @pl.when(flag == 0)
    def _():
        act(second)


def tiles_of(ref, row, col, tile):
    return ref.at[pl.ds(pl.multiple_of(row * tile, tile), tile), pl.ds(pl.multiple_of(col * tile, tile), tile)]


def pair_cols(first, count, tile):
    return pl.ds(pl.multiple_of(first * tile, 2 * tile), count * tile)


def pair_rows(first, tile):
    return pl.ds(pl.multiple_of(first * tile, 2 * tile), 2 * tile)


def window(base, rows, r, total):
    low = jnp.clip(base + 2 * r - H, 0, total - 2 * H) - (base - rows)
    return jnp.clip(low // 2 * 2, 0, 3 * rows - 2 * H - 2)


def densify(pool, table, dense, row, count):
    tile = pool.shape[1]

    def one(t, carry):
        for c in range(table.shape[1]):
            dense[pl.ds(pl.multiple_of((row + t) * tile, tile), tile), c * tile : (c + 1) * tile] = pool[table[t, c]]
        return carry

    lax.fori_loop(0, count, one, 0)


def pack_kernel(rows, meta, first, pattern, tiles, packed, held, sem, osem):
    count = tiles.shape[0]
    slots = count // rows
    inward = pltpu.make_async_copy(tiles, held, sem)
    inward.start()
    start = first[0]
    low = first[1] == 0
    tables = [widths(slots, rows, side) for side in (False, True)]
    starts = [[sum(table[:t]) for t in range(rows)] for table in tables]
    inward.wait()
    for t in range(rows):
        offset = jnp.where(low, starts[1][t], starts[0][t])
        end = offset + jnp.where(low, tables[1][t], tables[0][t])

        def one(k, place, t=t, end=end):
            col = pattern[start + t, k]
            take = (col >= 0) & jnp.where(low, col <= start + H - 2, col >= start) & (place < end)

            @pl.when(take)
            def _():
                pltpu.make_async_copy(held.at[t * slots + k], packed.at[place], osem).start()

            return place + take.astype(jnp.int32)

        place = offset
        for k in range(slots):
            place = one(k, place)

        def wait(k, carry):
            pltpu.make_async_copy(held.at[0], packed.at[0], osem).wait()
            return carry

        lax.fori_loop(0, place - offset, wait, 0)


def near_kernel(rows, meta, table, z_home, z_came, mate_a, mate_b, znear, turned_far, turned_own, pool, zd, zf, zo, sem, osem):
    count, tile = z_home.shape[:2]
    odd = meta[ODD]
    own_at = odd * count
    either(meta[MOVED], z_came, z_home, lambda own: pltpu.make_async_copy(own, pool.at[pl.ds(own_at, count)], sem).start())
    either(meta[MOVED], mate_a, mate_b, lambda mate: pltpu.make_async_copy(mate, pool.at[pl.ds(count - own_at, count)], sem).start())
    pool[2 * count] = jnp.zeros(pool.shape[1:], pool.dtype)
    for _ in range(2):
        pltpu.make_async_copy(z_home, z_home, sem).wait()
    densify(pool, table, zd, 0, 2 * rows)
    copies = [pltpu.make_async_copy(zd, znear, osem.at[0])]
    copies[0].start()
    own_rows = pl.ds(pl.multiple_of(odd * rows * tile, rows * tile), rows * tile)

    def far_one(i, carry):
        at = pl.ds(pl.multiple_of((odd * 2 * rows + i) * tile, tile), tile)
        zf[pl.ds(pl.multiple_of(i * tile, tile), tile), :] = zd[own_rows, at].T
        return carry

    def own_one(i, carry):
        at = pl.ds(pl.multiple_of((rows + i) * tile, tile), tile)
        zo[pl.ds(pl.multiple_of(i * tile, tile), tile), :] = zd[:, at].T
        return carry

    lax.fori_loop(0, rows, far_one, 0)
    lax.fori_loop(0, rows, own_one, 0)
    copies += [pltpu.make_async_copy(zf, turned_far, osem.at[1]), pltpu.make_async_copy(zo, turned_own, osem.at[2])]
    copies[1].start()
    copies[2].start()
    for copy in copies:
        copy.wait()


def product_kernel(
    total, rows, meta, ftab, ztab, keep, col_of, f_home, f_came, far_a, far_b, znear, turned,
    prod, lent, packed, fd, zd, pd, zt, fpool, zpool, part, fsem, zsem, tsem, nsem, psem, osem,
):
    count, tile = f_home.shape[:2]
    span, wide = 3 * rows, 2 * H + 2
    base, odd = meta[BASE], meta[ODD]
    far_row = jnp.where(odd == 0, 0, 2 * rows)
    near_rows = pl.ds(pl.multiple_of(rows * tile * (1 - odd), rows * tile), 2 * rows * tile)
    either(meta[MOVED], f_came, f_home, lambda fock: pltpu.make_async_copy(fock, fpool.at[:count], fsem).start())
    either(meta[FAR_A], far_a, far_b, lambda far: pltpu.make_async_copy(far, zpool.at[: far.shape[0]], zsem).start())
    near_in = pltpu.make_async_copy(znear, zd.at[near_rows], nsem)
    near_in.start()
    turn_in = pltpu.make_async_copy(turned, zt, tsem)
    turn_in.start()
    fpool[count] = jnp.zeros(fpool.shape[1:], fpool.dtype)
    zpool[far_a.shape[0]] = jnp.zeros(zpool.shape[1:], zpool.dtype)

    def clear(i, carry):
        pd[pl.ds(pl.multiple_of(i * tile, tile), tile), :] = jnp.zeros((tile, pd.shape[1]), pd.dtype)
        return carry

    lax.fori_loop(0, rows, clear, 0)
    pltpu.make_async_copy(f_home, fpool.at[:count], fsem).wait()
    densify(fpool, ftab, fd, 0, rows)
    pltpu.make_async_copy(far_a, zpool.at[: far_a.shape[0]], zsem).wait()
    densify(zpool, ztab, zd, far_row, rows)
    near_in.wait()
    step = 6 if wide % 6 == 0 else 2
    for r in range(rows // 2):
        k0 = window(base, rows, r, total)
        kcols = pair_cols(k0, wide, tile)

        def block(nb, carry, r=r, k0=k0, kcols=kcols):
            first = k0 + step * nb
            acc = jnp.dot(
                fd[2 * r * tile : (2 * r + 2) * tile, kcols],
                zd[kcols, pair_cols(first, step, tile)],
                preferred_element_type=jnp.float32,
            )
            for i in range(2):
                for j in range(step):
                    piece = acc[i * tile : (i + 1) * tile, j * tile : (j + 1) * tile]
                    piece = jnp.where(keep[2 * r + i, first + j] != 0, piece, 0.0)
                    tiles_of(pd, 2 * r + i, first + j, tile)[...] = piece.astype(pd.dtype)
            return carry

        lax.fori_loop(0, wide // step, block, 0)
    lent_cols = pl.ds(pl.multiple_of((1 - odd) * rows * tile, rows * tile), 2 * rows * tile)
    writes = [pltpu.make_async_copy(pd, prod, psem.at[0]), pltpu.make_async_copy(pd.at[:, lent_cols], lent, psem.at[1])]
    for write in writes:
        write.start()
    turn_in.wait()
    start = jnp.where(odd == 0, 0, rows)
    pairs = rows // 2
    for m in range(pairs):
        r = jnp.where(odd == 0, m, pairs - 1 - m)
        deep = 2 * (m + 1) * tile
        k_at = pl.ds(pl.multiple_of(jnp.where(odd == 0, 0, rows * tile - deep), 2 * tile), deep)
        n_wide = H + 2 * (m + 1)
        n_at = jnp.where(odd == 0, 0, 2 * H - n_wide)
        acc = jnp.dot(
            zt[pair_rows(2 * r, tile), k_at],
            pd[k_at, pair_cols(start + n_at, n_wide, tile)],
            preferred_element_type=jnp.float32,
        )
        part[pair_rows(2 * r, tile), pair_cols(n_at, n_wide, tile)] = acc.astype(part.dtype)
    low_rows = [t for t, w in enumerate(widths(count // rows, rows, True)) for _ in range(w)]
    high_rows = [t for t, w in enumerate(widths(count // rows, rows, False)) for _ in range(w)]
    for p in range(packed.shape[0]):
        t = jnp.where(odd == 1, low_rows[p], high_rows[p])
        pltpu.make_async_copy(tiles_of(part, t, col_of[p], tile), packed.at[p], osem).start()
    pltpu.make_async_copy(packed, packed, osem).wait()
    for write in writes:
        write.wait()


def own_kernel(total, rows, meta, col_of, turned, prod, lent, near, zt, pd, acc_ref, out, sem, osem):
    count, tile = near.shape[:2]
    slots = count // rows
    base, odd = meta[BASE], meta[ODD]
    wide = 2 * H + 2
    own = rows * tile

    def part(index, n):
        return pl.ds(pl.multiple_of(index * own, own), n * own)

    copies = [
        pltpu.make_async_copy(turned, zt, sem.at[0]),
        pltpu.make_async_copy(prod, pd.at[part(odd, 1)], sem.at[1]),
        pltpu.make_async_copy(lent, pd.at[part(1 - odd, 1), part(1 - odd, 2)], sem.at[2]),
    ]
    for copy in copies:
        copy.start()
    pd[part(1 - odd, 1), part(2 * odd, 1)] = jnp.zeros((own, own), pd.dtype)
    acc_ref[:, 3 * own :] = jnp.zeros((own, tile), acc_ref.dtype)
    for copy in copies:
        copy.wait()
    step = 6 if wide % 6 == 0 else 2
    for r in range(rows // 2):
        k0 = window(base, rows, r, total)

        def block(nb, carry, r=r, k0=k0):
            cols = pair_cols(k0 + step * nb, step, tile)
            acc = jnp.dot(zt[2 * r * tile : (2 * r + 2) * tile, :], pd[:, cols], preferred_element_type=jnp.float32)
            acc_ref[2 * r * tile : (2 * r + 2) * tile, cols] = acc.astype(acc_ref.dtype)
            return carry

        lax.fori_loop(0, wide // step, block, 0)

    def one(t, carry):
        for s in range(slots):
            out[t * slots + s] = tiles_of(acc_ref, t, col_of[t, s], tile)[...]
        return carry

    lax.fori_loop(0, rows, one, 0)
    outward = pltpu.make_async_copy(out, near, osem)
    outward.start()
    outward.wait()


def join_kernel(rows, place, where, near, far, *rest):
    outs, (a, b, out, sem, far_sem, osem) = rest[:-6], rest[-6:]
    slots = near.shape[0] // rows
    tiles = far.shape[0]
    inward = pltpu.make_async_copy(far, b.at[:tiles], far_sem)
    inward.start()
    copies = [pltpu.make_async_copy(near.at[pl.ds(where[n] * slots, slots)], a.at[n], sem.at[n]) for n in range(len(outs))]
    for copy in copies:
        copy.start()
    b[tiles] = jnp.zeros(b.shape[1:], b.dtype)
    inward.wait()
    for n, target in enumerate(outs):
        row = where[n]
        copies[n].wait()
        for s in range(slots):
            out[n, s] = (a[n, s].astype(jnp.float32) + b[place[row, s]].astype(jnp.float32)).astype(out.dtype)
        pltpu.make_async_copy(out.at[n], target, osem.at[n]).start()
    for n, target in enumerate(outs):
        pltpu.make_async_copy(out.at[n], target, osem.at[n]).wait()


def gather_kernel(slot, present, *rest):
    parts, (out, held, isem, osem) = rest[:-4], rest[-4:]
    for s, part in enumerate(parts):
        pltpu.make_async_copy(part, held.at[s], isem.at[s]).start()
    for s, part in enumerate(parts):
        pltpu.make_async_copy(part, held.at[s], isem.at[s]).wait()

        @pl.when(present[s] != 0)
        def _(s=s):
            pltpu.make_async_copy(held.at[s], out.at[slot[s]], osem).start()

    pltpu.make_async_copy(out, out, osem).wait()


def call(kernel, scalars, arrays, outs, scratch, name=None, limit=60, cost=1.0):
    any_spec = pl.BlockSpec(memory_space=pl.ANY)
    smem = pl.BlockSpec(memory_space=pltpu.SMEM)
    return pl.pallas_call(
        kernel,
        in_specs=[smem] * len(scalars) + [any_spec] * len(arrays),
        out_specs=[any_spec] * len(outs),
        out_shape=outs,
        scratch_shapes=scratch,
        compiler_params=pltpu.CompilerParams(vmem_limit_bytes=limit * 1024 * 1024),
        cost_estimate=pl.CostEstimate(flops=0, bytes_accessed=int(cost * COST_SCALE), transcendentals=0),
        name=name,
    )(*scalars, *arrays)


def body(fock_tiles, fock_pattern, basis_tiles, basis_pattern, product_pattern, result_pattern, new_index):
    rows, slots, tile = fock_tiles.shape[:3]
    total = fock_pattern.shape[0]
    count = rows * slots
    count_rows, count_cols = lax.axis_size("row"), lax.axis_size("col")
    plan = layout(count_rows, count_cols)
    my_row, my_col = lax.axis_index("row"), lax.axis_index("col")
    group = 2 * (my_row // 2) + my_col % 2
    number = 2 * (my_col // 2) + my_row % 2
    block = group * count_cols + number
    base = block * rows
    odd = number % 2
    moved = (my_row + my_col) % 2
    at_edge = (number == 0) | (number == count_cols - 1)
    home = (my_row * count_cols + my_col) * rows
    meta = jnp.stack([jnp.asarray(m, jnp.int32) for m in (base, odd, moved, (moved == 1) | at_edge)])
    dtype = fock_tiles.dtype
    packed_tiles = max(sum(widths(slots, rows, side)) for side in (False, True))
    span = 3 * rows

    framed = jnp.pad(
        jnp.concatenate([basis_pattern, result_pattern, fock_pattern, product_pattern], axis=1),
        ((rows, rows), (0, 0)),
        constant_values=-1,
    )
    near = lax.dynamic_slice_in_dim(framed, base, span, 0)
    zpat, rpat, fpat, ppat = (near[:, i * slots : (i + 1) * slots] for i in range(4))
    mid = slice(rows, 2 * rows)
    far_side = jnp.where(odd == 0, jnp.concatenate([zpat, rpat], 1)[:rows], jnp.concatenate([zpat, rpat], 1)[2 * rows :])
    far_base = jnp.where(odd == 0, base - rows, base + rows)
    place, col_of = pack_tables(
        jnp.stack([far_side[:, :slots], far_side[:, slots:], rpat[mid]]),
        jnp.stack([far_base, far_base, base]),
        jnp.stack([odd == 1, odd == 1, odd == 0]),
        packed_tiles,
    )
    origin = base - rows
    slot_ids = jnp.arange(2 * count, dtype=jnp.int32).reshape(2 * rows, slots)
    znear_pat = jnp.where(odd == 0, zpat[rows:], zpat[: 2 * rows])
    near_table = spread(znear_pat, slot_ids, origin, span, 2 * count)
    fock_table = spread(fpat[mid], slot_ids[:rows], origin, span, count)
    far_table = spread(far_side[:, :slots], place[0], origin, span, packed_tiles)
    keep = spread(ppat[mid], jnp.ones((rows, slots), jnp.int32), origin, span, 0)
    far_start = jnp.where(odd == 0, 0, rows)
    far_cols = jnp.clip(col_of[1] - origin - far_start, 0, 2 * H - 1)
    own_cols = jnp.where(rpat[mid] >= 0, rpat[mid] - origin, span)
    own_place = jnp.where(place[2] >= 0, place[2], packed_tiles)

    def permute(x, name):
        return lax.ppermute(x, AXES, plan[name])

    def dense(n_rows, n_cols, kind=dtype):
        return pltpu.VMEM((n_rows * tile, n_cols * tile), kind)

    def pool(n):
        return pltpu.VMEM((n, tile, tile), dtype)

    def shape(*dims):
        return jax.ShapeDtypeStruct(dims, dtype)

    dma = pltpu.SemaphoreType.DMA
    packed_shape = shape(packed_tiles, tile, tile)
    block_shape = shape(count, tile, tile)
    z_home, f_home = basis_tiles.reshape(count, tile, tile), fock_tiles.reshape(count, tile, tile)

    def pack(first, tiles):
        kernel = functools.partial(pack_kernel, rows)
        scalars = [meta, jnp.stack([jnp.asarray(f, jnp.int32) for f in first]), basis_pattern]
        return call(kernel, scalars, [tiles], [packed_shape], [pool(count), dma, dma], name="pack", limit=8, cost=5)[0]

    z_came = permute(z_home, "swap")
    mate_a = permute(z_home, "mate_a")
    far_a = permute(pack((home, my_col % 2), z_home), "far_a")
    f_came = permute(f_home, "swap")
    z_came, far_a = lax.optimization_barrier((z_came, far_a))
    far_b = permute(pack((base, odd), z_came), "far_b")
    mate_b = permute(z_came, "mate_b")
    znear, turned_far, turned_own = call(
        functools.partial(near_kernel, rows),
        [meta, near_table],
        [z_home, z_came, mate_a, mate_b],
        [shape(2 * rows * tile, span * tile), shape(rows * tile, rows * tile), shape(rows * tile, 2 * rows * tile)],
        [pool(2 * count + 1), dense(2 * rows, span), dense(rows, rows), dense(rows, 2 * rows), dma, dma((3,))],
        name="near",
        limit=40,
        cost=14,
    )
    prod, lent, packed = call(
        functools.partial(product_kernel, total, rows),
        [meta, fock_table, far_table, keep, far_cols],
        [f_home, f_came, far_a, far_b, znear, turned_far],
        [shape(rows * tile, span * tile), shape(rows * tile, 2 * rows * tile), packed_shape],
        [dense(rows, span), dense(span, span), dense(rows, span), dense(rows, rows)]
        + [pool(count + 1), pool(packed_tiles + 1), dense(rows, 2 * H)]
        + [dma] * 4
        + [dma((2,)), dma],
        name="product",
        cost=27,
    )
    far = permute(packed, "outer")
    lent = permute(lent, "pair")
    (near_sum,) = call(
        functools.partial(own_kernel, total, rows),
        [meta, own_cols],
        [turned_own, prod, lent],
        [block_shape],
        [dense(rows, 2 * rows), dense(2 * rows, span), dense(rows, span + 1), pool(count), dma((3,)), dma],
        name="own",
        limit=40,
        cost=20,
    )
    shift = (lax.dynamic_slice_in_dim(new_index, base, rows, 0) // rows - number) % count_cols
    hit = shift[None, :] == jnp.arange(count_cols, dtype=jnp.int32)[:, None]
    where = jnp.sum(hit.astype(jnp.int32) * jnp.arange(rows, dtype=jnp.int32)[None, :], axis=1)
    outs = call(
        functools.partial(join_kernel, rows),
        [own_place, where],
        [near_sum, far],
        [shape(slots, tile, tile)] * count_cols,
        [pltpu.VMEM((count_cols, slots, tile, tile), dtype), pool(packed_tiles + 1), pltpu.VMEM((count_cols, slots, tile, tile), dtype)]
        + [dma((count_cols,)), dma, dma((count_cols,))],
        name="join",
        limit=24,
        cost=5,
    )
    parts = [lax.ppermute(out, AXES, plan["shifts"][s]) for s, out in enumerate(outs)]
    wanted = home + jnp.arange(rows, dtype=jnp.int32)
    found = new_index[None, :] == wanted[:, None]
    anchor = jnp.sum(found.astype(jnp.int32) * jnp.arange(total, dtype=jnp.int32)[None, :], axis=1)
    came = (my_col - anchor // rows) % count_cols
    hit = came[None, :] == jnp.arange(count_cols, dtype=jnp.int32)[:, None]
    slot = jnp.sum(hit.astype(jnp.int32) * jnp.arange(rows, dtype=jnp.int32)[None, :], axis=1)
    present = jnp.sum(hit.astype(jnp.int32), axis=1)
    (out,) = call(
        gather_kernel,
        [slot, present],
        parts,
        [shape(rows, slots, tile, tile)],
        [pltpu.VMEM((count_cols, slots, tile, tile), dtype), dma((count_cols,)), dma],
        name="gather",
        limit=16,
        cost=4,
    )
    return out


def solution(mesh):
    placed = P(AXES, None, None, None)
    return jax.shard_map(
        body,
        mesh=mesh,
        in_specs=(placed, P(), placed, P(), P(), P(), P()),
        out_specs=placed,
        check_vma=False,
    )
```

time: 910 us -> 335 us (0.37)
  matrix products: 331 us -> 0 us
  waiting for transfers between devices: 413 us -> 137 us
  local copies, waits for them, and re-layouts: 126 us -> 7.37 us
  Pallas kernels: 0 us -> 89.9 us
  starting transfers between devices: 18.1 us -> 91.4 us
    dot_general x40 -> x0, matrix products: 331 us -> none  [the longest x8 100 us: pull_row(): jnp.einsum('jrp,jpab->jrab', second.astype(jnp.bfloat16), product_near, p...]
    ppermute x4 -> x16, waiting for transfers between devices: 330 us -> 137 us  [the longest x8 75.9 us: body(): lax.ppermute(out, AXES, plan['shifts'][s])]
    pallas_call x0 -> x7, Pallas kernels: none -> 89.9 us  [call(): pl.pallas_call(kernel, in_specs=[smem] * len(scalars) + [any_spec] * len(...]
    gather x20 -> x0, local copies, waits for them, and re-layouts: 86.1 us -> none  [the longest x8 70.4 us: first_product(): gathered = basis_near[near_index]]
    all_to_all x1 -> x0, waiting for transfers between devices: 83.3 us -> none  [body(): lax.all_to_all(outgoing, 'col', split_axis=0, concat_axis=0, tiled=True)]
    ppermute x4 -> x16, starting transfers between devices: 11.8 us -> 91.4 us  [the longest x8 71.4 us: body(): lax.ppermute(out, AXES, plan['shifts'][s])]
    dynamic_update_slice x32 -> x0, local copies, waits for them, and re-layouts: 17.7 us -> none  [the longest x16 8.92 us: body(): product = lax.map(first_product, (fock_cols, prod_cols, fock_tiles))]
    while x19 -> x0, local copies, waits for them, and re-layouts: 10.4 us -> none  [the longest x2 9.54 us: body(): lax.fori_loop(0, rows_dev, pull_row, jnp.zeros(fock_tiles.shape, jnp.floa...]
  transfers between devices with their start and end apart: 5 -> 16, of which waited for: 3 -> 12; matrix products, arithmetic and copies ran while one was open for 1% -> 3% of each run, Pallas kernels for 0% -> 15%
where the time goes in v1:
time: 335 us; the launch traced here: 333 us
  waiting for transfers between devices  137 us (41%)
  starting transfers between devices  91.4 us (27%)
  Pallas kernels  89.9 us (27%)
  local copies, waits for them, and re-layouts  7.37 us (2%)
  other arithmetic  6.5 us (2%)
    pallas_call x7, Pallas kernels, call(): pl.pallas_call(kernel, in_specs=[smem] * len(scalars) + [any_spec] * len(...  89.9 us
    ppermute x8, waiting for transfers between devices, body(): lax.ppermute(out, AXES, plan['shifts'][s])  75.9 us
    ppermute x8, starting transfers between devices, body(): lax.ppermute(out, AXES, plan['shifts'][s])  71.4 us
    ppermute x8, waiting for transfers between devices, permute(): return lax.ppermute(x, AXES, plan[name])  61.3 us
    ppermute x8, starting transfers between devices, permute(): return lax.ppermute(x, AXES, plan[name])  20.1 us
  transfers between devices with their start and end apart: 16, of which 12 were waited for; matrix products, arithmetic and copies ran while one was open for 3% of the time, Pallas kernels for 15%

profile of v1, /device:TPU:14, one launch (start us, length us, event | category | flops | bytes accessed | tf_op | source)
XLA Modules:
  0.0 332.9 jit_solution(8192617908620450827)
XLA Ops:
  0.0 2.1 collective-permute-start
  2.1 0.8 copy.39.pattern
  3.1 8.9 %pack.2 = bf16[92,128,128]{2,1,0:T(8,128)(2,1)S(1)} custom-call(s32[4]{0:T(128)S(1)} %pad_add_fusion.6.meta, s32[2]{0:T(128)S(1)} %pad_add_fusion.7.first, s32[256,15]{1,0:T(8,128)S(1)} %copy.39.pattern, bf16[120,128,128]{2,1,0:T(8,128)(2,1)} %bitcast.11.tiles.z_home), custom_call_target="tpu_custom_call" | custom-call | bytes 15000000 | tf_op jit(solution)/shard_map/pack/pallas_call | solution.py:333
  12.0 1.3 collective-permute-start.1
  13.3 1.3 collective-permute-start.2
  14.6 5.0 %collective-permute-start.4 = (bf16[120,128,128]{2,1,0:T(8,128)(2,1)}, bf16[120,128,128]{2,1,0:T(8,128)(2,1)}, u32[]{:S(2)}, u32[]{:S(2)}) collective-permute-start(bf16[120,128,128]{2,1,0:T(8,128)(2,1)} %bitcast.16.f_home), channel_id=1, source_target_pairs={{1,8},{3,10},{5,12},{7,14},{8,1},{10,3},{12,5},{14,7},{17,24},{19,... | collective-permute-start | bytes 11796488 | tf_op jit(solution)/shard_map/ppermute | solution.py:394
  19.6 0.1 copy.41
  19.8 0.1 copy.42
  19.9 0.8 copy.40
  20.6 1.1 pad_add_fusion
  21.7 0.1 subtract_select_fusion
  22.7 0.1 broadcast_compare_fusion.2
  22.7 26.6 %collective-permute-done.1.far_a = bf16[92,128,128]{2,1,0:T(8,128)(2,1)} collective-permute-done((bf16[92,128,128]{2,1,0:T(8,128)(2,1)S(1)}, bf16[92,128,128]{2,1,0:T(8,128)(2,1)}, u32[]{:S(2)}, u32[]{:S(2)}) %collective-permute-start.1) | collective-permute-done | bytes 3014688 | tf_op jit(solution)/shard_map/ppermute | solution.py:394
  49.3 3.2 collective-permute-start.3
  52.6 10.2 %pack.3 = bf16[92,128,128]{2,1,0:T(8,128)(2,1)S(1)} custom-call(s32[4]{0:T(128)S(1)} %pad_add_fusion.6.meta, s32[2]{0:T(128)S(1)} %pad_add_fusion.8.first, s32[256,15]{1,0:T(8,128)S(1)} %copy.39.pattern, bf16[120,128,128]{2,1,0:T(8,128)(2,1)} %collective-permute-done.z_came.tiles), custom_call_target="tpu_custom_call" | custom-call | bytes 15000000 | tf_op jit(solution)/shard_map/pack/pallas_call | solution.py:333
  62.8 2.9 collective-permute-start.5
  65.9 0.1 copy.54
  66.0 0.1 copy.49
  66.1 0.1 copy.58
  66.2 0.1 copy.52
  66.6 0.1 copy.46
  66.8 0.9 convert_reduce_fusion
  67.8 0.1 and_select_fusion
  67.8 0.1 copy.59
  68.0 0.1 lt.78
  68.0 0.1 copy.60
  68.3 0.2 select_reduce_fusion
  68.5 0.1 select_reduce_fusion.2
  68.6 0.2 select_reduce_fusion.1
  68.7 0.1 select_reduce_fusion.4
  68.9 0.1 select_reduce_fusion.3
  69.0 0.6 clamp_bitcast_fusion.col_of
  69.6 0.6 compare_select_fusion.1.keep
  70.1 0.6 compare_select_fusion.3.ftab
  70.7 0.6 compare_select_fusion.2.ztab
  71.4 13.2 %near.1 = (bf16[2048,3072]{1,0:T(8,128)(2,1)}, bf16[1024,1024]{1,0:T(8,128)(2,1)S(1)}, bf16[1024,2048]{1,0:T(8,128)(2,1)}) custom-call(s32[4]{0:T(128)S(1)} %pad_add_fusion.6.meta, s32[16,24]{1,0:T(8,128)S(1)} %compare_select_fusion.table, bf16[120,128,128]{2,1,0:T(8,128)(2,1)} %bitcast.11.tiles.z_home, ...), custom_call_target="tpu_custom_call" | custom-call | bytes 42000000 | tf_op jit(solution)/shard_map/near/pallas_call | solution.py:333
  84.6 1.3 copy-done.1
  85.9 3.7 %collective-permute-done.4.f_came = bf16[120,128,128]{2,1,0:T(8,128)(2,1)} collective-permute-done((bf16[120,128,128]{2,1,0:T(8,128)(2,1)}, bf16[120,128,128]{2,1,0:T(8,128)(2,1)}, u32[]{:S(2)}, u32[]{:S(2)}) %collective-permute-start.4) | collective-permute-done | bytes 3932192 | tf_op jit(solution)/shard_map/ppermute | solution.py:394
  89.6 7.9 %collective-permute-done.5.far_b = bf16[92,128,128]{2,1,0:T(8,128)(2,1)} collective-permute-done((bf16[92,128,128]{2,1,0:T(8,128)(2,1)S(1)}, bf16[92,128,128]{2,1,0:T(8,128)(2,1)}, u32[]{:S(2)}, u32[]{:S(2)}) %collective-permute-start.5) | collective-permute-done | bytes 3014688 | tf_op jit(solution)/shard_map/ppermute | solution.py:394
  97.5 27.0 %product.1 = (bf16[1024,3072]{1,0:T(8,128)(2,1)}, bf16[1024,2048]{1,0:T(8,128)(2,1)}, bf16[92,128,128]{2,1,0:T(8,128)(2,1)}) custom-call(s32[4]{0:T(128)} %copy-done.2, s32[8,24]{1,0:T(8,128)} %compare_select_fusion.3.ftab, s32[8,24]{1,0:T(8,128)} %compare_select_fusion.2.ztab, s32[8,24]{1,0:T(8,128)} %compare_select_fusion.1.keep, ...), custom_call_target="tpu_custom_call" | custom-call | bytes 81000000 | tf_op jit(solution)/shard_map/product/pallas_call | solution.py:333
  124.5 2.3 collective-permute-start.6
  126.8 2.1 collective-permute-start.7
  129.1 0.1 and_select_fusion.2
  129.1 0.1 select_reduce_fusion.6.where
  129.3 4.7 %collective-permute-done.6.lent = bf16[1024,2048]{1,0:T(8,128)(2,1)} collective-permute-done((bf16[1024,2048]{1,0:T(8,128)(2,1)}, bf16[1024,2048]{1,0:T(8,128)(2,1)}, u32[]{:S(2)}, u32[]{:S(2)}) %collective-permute-start.6) | collective-permute-done | bytes 4194336 | tf_op jit(solution)/shard_map/ppermute | solution.py:394
  134.0 2.2 copy-done
  136.1 18.4 %own.1.near = bf16[120,128,128]{2,1,0:T(8,128)(2,1)S(1)} custom-call(s32[4]{0:T(128)S(1)} %copy-done.3, s32[8,15]{1,0:T(8,128)S(1)} %get-tuple-element.45.col_of, bf16[1024,2048]{1,0:T(8,128)(2,1)S(1)} %copy-done, bf16[1024,3072]{1,0:T(8,128)(2,1)} %get-tuple-element.26.prod, bf16[1024,2048]{1,0:T(8,128)(2,1)} %collective-permute-done.6.lent), custom_call_target="tpu_custom_call" | custom-call | bytes 60000000 | tf_op jit(solution)/shard_map/own/pallas_call | solution.py:333
  154.5 18.4 %collective-permute-done.7.far = bf16[92,128,128]{2,1,0:T(8,128)(2,1)S(1)} collective-permute-done((bf16[92,128,128]{2,1,0:T(8,128)(2,1)}, bf16[92,128,128]{2,1,0:T(8,128)(2,1)S(1)}, u32[]{:S(2)}, u32[]{:S(2)}) %collective-permute-start.7) | collective-permute-done | bytes 3014688 | tf_op jit(solution)/shard_map/ppermute | solution.py:394
  172.9 7.1 %join.1 = (bf16[15,128,128]{2,1,0:T(8,128)(2,1)S(1)}, bf16[15,128,128]{2,1,0:T(8,128)(2,1)S(1)}, bf16[15,128,128]{2,1,0:T(8,128)(2,1)S(1)}, bf16[15,128,128]{2,1...) custom-call(s32[8,15]{1,0:T(8,128)S(1)} %compare_select_fusion.4.pla, ...), custom_call_target="tpu_custom_call" | custom-call | bytes 15000000 | tf_op jit(solution)/shard_map/join/pallas_call | solution.py:333
  180.0 54.2 %collective-permute-start.8 = (bf16[15,128,128]{2,1,0:T(8,128)(2,1)S(1)}, bf16[15,128,128]{2,1,0:T(8,128)(2,1)S(1)}, u32[]{:S(2)}, u32[]{:S(2)}) collective-permute-start(bf16[15,128,128]{2,1,0:T(8,128)(2,1)S(1)} %get-tuple-element.29), channel_id=1, source_target_pairs={{0,0},{8,1},{2,2},{10,3},{4,4},{12,5},{6,6},{14,7},{1,8},{9,9},{3,... | collective-permute-start | bytes 1474568 | tf_op jit(solution)/shard_map/ppermute | solution.py:470
  234.4 4.1 %collective-permute-start.11 = (bf16[15,128,128]{2,1,0:T(8,128)(2,1)S(1)}, bf16[15,128,128]{2,1,0:T(8,128)(2,1)S(1)}, u32[]{:S(2)}, u32[]{:S(2)}) collective-permute-start(bf16[15,128,128]{2,1,0:T(8,128)(2,1)S(1)} %get-tuple-element.32), channel_id=1, source_target_pairs={{0,3},{8,4},{2,5},{10,6},{4,7},{12,0},{6,1},{14,2},{1,11},{9,12},{... | collective-permute-start | bytes 1474568 | tf_op jit(solution)/shard_map/ppermute | solution.py:470
  238.5 4.4 %collective-permute-start.12 = (bf16[15,128,128]{2,1,0:T(8,128)(2,1)S(1)}, bf16[15,128,128]{2,1,0:T(8,128)(2,1)S(1)}, u32[]{:S(2)}, u32[]{:S(2)}) collective-permute-start(bf16[15,128,128]{2,1,0:T(8,128)(2,1)S(1)} %get-tuple-element.33), channel_id=1, source_target_pairs={{0,4},{8,5},{2,6},{10,7},{4,0},{12,1},{6,2},{14,3},{1,12},{9,13},{... | collective-permute-start | bytes 1474568 | tf_op jit(solution)/shard_map/ppermute | solution.py:470
  243.0 8.2 %collective-permute-done.8.rest_0_ = bf16[15,128,128]{2,1,0:T(8,128)(2,1)S(1)} collective-permute-done((bf16[15,128,128]{2,1,0:T(8,128)(2,1)S(1)}, bf16[15,128,128]{2,1,0:T(8,128)(2,1)S(1)}, u32[]{:S(2)}, u32[]{:S(2)}) %collective-permute-start.8) | collective-permute-done | bytes 491552 | tf_op jit(solution)/shard_map/ppermute | solution.py:470
  251.2 4.1 %collective-permute-start.14 = (bf16[15,128,128]{2,1,0:T(8,128)(2,1)S(1)}, bf16[15,128,128]{2,1,0:T(8,128)(2,1)S(1)}, u32[]{:S(2)}, u32[]{:S(2)}) collective-permute-start(bf16[15,128,128]{2,1,0:T(8,128)(2,1)S(1)} %get-tuple-element.35), channel_id=1, source_target_pairs={{0,6},{8,7},{2,0},{10,1},{4,2},{12,3},{6,4},{14,5},{1,14},{9,15},{... | collective-permute-start | bytes 1474568 | tf_op jit(solution)/shard_map/ppermute | solution.py:470
  255.3 0.4 collective-permute-done.10.rest_2_
  255.7 4.4 %collective-permute-start.15 = (bf16[15,128,128]{2,1,0:T(8,128)(2,1)S(1)}, bf16[15,128,128]{2,1,0:T(8,128)(2,1)S(1)}, u32[]{:S(2)}, u32[]{:S(2)}) collective-permute-start(bf16[15,128,128]{2,1,0:T(8,128)(2,1)S(1)} %get-tuple-element.36), channel_id=1, source_target_pairs={{0,7},{8,0},{2,1},{10,2},{4,3},{12,4},{6,5},{14,6},{1,15},{9,8},{3... | collective-permute-start | bytes 1474568 | tf_op jit(solution)/shard_map/ppermute | solution.py:470
  260.0 0.2 select_reduce_fusion.5
  260.2 0.1 convert_reduce_fusion.1
  260.4 3.2 collective-permute-done.11.rest_3_
  263.6 45.7 %collective-permute-done.12.rest_4_ = bf16[15,128,128]{2,1,0:T(8,128)(2,1)S(1)} collective-permute-done((bf16[15,128,128]{2,1,0:T(8,128)(2,1)S(1)}, bf16[15,128,128]{2,1,0:T(8,128)(2,1)S(1)}, u32[]{:S(2)}, u32[]{:S(2)}) %collective-permute-start.12) | collective-permute-done | bytes 491552 | tf_op jit(solution)/shard_map/ppermute | solution.py:470
  309.3 7.5 %collective-permute-done.13.rest_5_ = bf16[15,128,128]{2,1,0:T(8,128)(2,1)S(1)} collective-permute-done((bf16[15,128,128]{2,1,0:T(8,128)(2,1)S(1)}, bf16[15,128,128]{2,1,0:T(8,128)(2,1)S(1)}, u32[]{:S(2)}, u32[]{:S(2)}) %collective-permute-start.13) | collective-permute-done | bytes 491552 | tf_op jit(solution)/shard_map/ppermute | solution.py:470
  316.8 10.3 %collective-permute-done.14.rest_6_ = bf16[15,128,128]{2,1,0:T(8,128)(2,1)S(1)} collective-permute-done((bf16[15,128,128]{2,1,0:T(8,128)(2,1)S(1)}, bf16[15,128,128]{2,1,0:T(8,128)(2,1)S(1)}, u32[]{:S(2)}, u32[]{:S(2)}) %collective-permute-start.14) | collective-permute-done | bytes 491552 | tf_op jit(solution)/shard_map/ppermute | solution.py:470
  327.1 0.6 collective-permute-done.15.rest_7_
  327.7 5.0 %gather.1 = bf16[8,15,128,128]{3,2,1,0:T(8,128)(2,1)} custom-call(s32[8]{0:T(128)S(1)} %get-tuple-element.38.slot, s32[8]{0:T(128)S(1)} %get-tuple-element.37.present, bf16[15,128,128]{2,1,0:T(8,128)(2,1)S(1)} %collective-permute-done.8.rest_0_, bf16[15,128,128]{2,1,0:T(8,128)(2,1)S(1)} %collective-permute-done.9.rest_1_, ...), custom_call_target="tpu_custom_call" | custom-call | bytes 12000000 | tf_op jit(solution)/shard_map/gather/pallas_call | solution.py:333
  (67 shorter events, 2.2 us)
Async XLA Ops:
  0.0 19.6 %copy-start.4 = (s32[256,15]{0,1:T(8,128)S(1)}, s32[256,15]{0,1:T(8,128)}, u32[]{:S(2)}) copy-start(s32[256,15]{0,1:T(8,128)} %param.12) | copy-start | bytes 46084
  0.0 19.7 %copy-start.5 = (s32[256,15]{0,1:T(8,128)S(1)}, s32[256,15]{0,1:T(8,128)}, u32[]{:S(2)}) copy-start(s32[256,15]{0,1:T(8,128)} %param.15) | copy-start | bytes 46084
  0.0 19.9 %copy-start.6 = (s32[256,15]{0,1:T(8,128)S(1)}, s32[256,15]{0,1:T(8,128)}, u32[]{:S(2)}) copy-start(s32[256,15]{0,1:T(8,128)} %param.16) | copy-start | bytes 46084
  0.0 49.3 %collective-permute-start = (bf16[120,128,128]{2,1,0:T(8,128)(2,1)}, bf16[120,128,128]{2,1,0:T(8,128)(2,1)}, u32[]{:S(2)}, u32[]{:S(2)}) collective-permute-start(bf16[120,128,128]{2,1,0:T(8,128)(2,1)} %bitcast.11.tiles.z_home), channel_id=1, source_target_pairs={{1,8},{3,10},{5,12},{7,14},{8,1},{10,3},{12,5},{14,7},{17,24},{19,... | collective-permute-start | bytes 11796488 | tf_op jit(solution)/shard_map/ppermute | solution.py:394
  3.1 68.2 %copy-start.2 = (s32[4]{0:T(128)}, s32[4]{0:T(128)S(1)}, u32[]{:S(2)}) copy-start(s32[4]{0:T(128)S(1)} %pad_add_fusion.6.meta) | copy-start | bytes 52
  12.0 37.3 %collective-permute-start.1 = (bf16[92,128,128]{2,1,0:T(8,128)(2,1)S(1)}, bf16[92,128,128]{2,1,0:T(8,128)(2,1)}, u32[]{:S(2)}, u32[]{:S(2)}) collective-permute-start(bf16[92,128,128]{2,1,0:T(8,128)(2,1)S(1)} %pack.2), channel_id=1, source_target_pairs={{2,8},{4,10},{6,12},{7,1},{8,14},{9,3},{11,5},{13,7},{15,16},{16,1... | collective-permute-start | bytes 9043976 | tf_op jit(solution)/shard_map/ppermute | solution.py:394
  13.3 58.0 %collective-permute-start.2 = (bf16[120,128,128]{2,1,0:T(8,128)(2,1)}, bf16[120,128,128]{2,1,0:T(8,128)(2,1)}, u32[]{:S(2)}, u32[]{:S(2)}) collective-permute-start(bf16[120,128,128]{2,1,0:T(8,128)(2,1)} %bitcast.11.tiles.z_home), channel_id=1, source_target_pairs={{0,8},{2,10},{4,12},{6,14},{9,1},{11,3},{13,5},{15,7},{16,24},{18,... | collective-permute-start | bytes 11796488 | tf_op jit(solution)/shard_map/ppermute | solution.py:394
  14.6 75.0 %collective-permute-start.4 = (bf16[120,128,128]{2,1,0:T(8,128)(2,1)}, bf16[120,128,128]{2,1,0:T(8,128)(2,1)}, u32[]{:S(2)}, u32[]{:S(2)}) collective-permute-start(bf16[120,128,128]{2,1,0:T(8,128)(2,1)} %bitcast.16.f_home), channel_id=1, source_target_pairs={{1,8},{3,10},{5,12},{7,14},{8,1},{10,3},{12,5},{14,7},{17,24},{19,... | collective-permute-start | bytes 11796488 | tf_op jit(solution)/shard_map/ppermute | solution.py:394
  21.8 45.8 %copy-start.8 = (s32[8]{0:T(128)S(1)}, s32[8]{0:T(128)}, u32[]{:S(2)}) copy-start(s32[8]{0:T(128)} %constant.139.clone) | copy-start | bytes 100
  21.8 45.8 %copy-start.9 = (s32[8]{0:T(128)S(1)}, s32[8]{0:T(128)}, u32[]{:S(2)}) copy-start(s32[8]{0:T(128)} %constant.138.clone) | copy-start | bytes 100
  21.8 45.9 %copy-start.10 = (s32[8]{0:T(128)S(1)}, s32[8]{0:T(128)}, u32[]{:S(2)}) copy-start(s32[8]{0:T(128)} %constant.137.clone) | copy-start | bytes 100
  21.8 45.9 %copy-start.11 = (s32[8]{0:T(128)S(1)}, s32[8]{0:T(128)}, u32[]{:S(2)}) copy-start(s32[8]{0:T(128)} %constant.136.clone) | copy-start | bytes 100
  49.3 22.0 %collective-permute-start.3 = (bf16[120,128,128]{2,1,0:T(8,128)(2,1)}, bf16[120,128,128]{2,1,0:T(8,128)(2,1)}, u32[]{:S(2)}, u32[]{:S(2)}) collective-permute-start(bf16[120,128,128]{2,1,0:T(8,128)(2,1)} %collective-permute-done.z_came.tiles), channel_id=1, source_target_pairs={{8,0},{10,2},{12,4},{14,6},{1,9},{3,11},{5,13},{7,15},{24,16},{26,... | collective-permute-start | bytes 11796488 | tf_op jit(solution)/shard_map/ppermute | solution.py:394
  62.8 34.7 %collective-permute-start.5 = (bf16[92,128,128]{2,1,0:T(8,128)(2,1)S(1)}, bf16[92,128,128]{2,1,0:T(8,128)(2,1)}, u32[]{:S(2)}, u32[]{:S(2)}) collective-permute-start(bf16[92,128,128]{2,1,0:T(8,128)(2,1)S(1)} %pack.3), channel_id=1, source_target_pairs={{8,2},{10,4},{12,6},{3,9},{5,11},{7,13},{24,18},{26,20},{28,22},{1... | collective-permute-start | bytes 9043976 | tf_op jit(solution)/shard_map/ppermute | solution.py:394
  84.6 1.3 copy-start.1
  97.5 31.6 %copy-start.7 = (s32[256]{0:T(256)S(1)}, s32[256]{0:T(256)}, u32[]{:S(2)}) copy-start(s32[256]{0:T(256)} %param.17) | copy-start | bytes 3076
  97.5 36.5 %copy-start.3 = (s32[4]{0:T(128)S(1)}, s32[4]{0:T(128)}, u32[]{:S(2)}) copy-start(s32[4]{0:T(128)} %copy-done.2) | copy-start | bytes 52
  124.5 9.4 %collective-permute-start.6 = (bf16[1024,2048]{1,0:T(8,128)(2,1)}, bf16[1024,2048]{1,0:T(8,128)(2,1)}, u32[]{:S(2)}, u32[]{:S(2)}) collective-permute-start(bf16[1024,2048]{1,0:T(8,128)(2,1)} %get-tuple-element.27), channel_id=1, source_target_pairs={{0,8},{8,0},{2,10},{10,2},{4,12},{12,4},{6,14},{14,6},{1,9},{9,1},... | collective-permute-start | bytes 12582920 | tf_op jit(solution)/shard_map/ppermute | solution.py:394
  126.8 46.1 %collective-permute-start.7 = (bf16[92,128,128]{2,1,0:T(8,128)(2,1)}, bf16[92,128,128]{2,1,0:T(8,128)(2,1)S(1)}, u32[]{:S(2)}, u32[]{:S(2)}) collective-permute-start(bf16[92,128,128]{2,1,0:T(8,128)(2,1)} %get-tuple-element.28), channel_id=1, source_target_pairs={{8,2},{2,8},{10,4},{4,10},{12,6},{6,12},{14,1},{1,14},{9,3},{3,9},... | collective-permute-start | bytes 9043976 | tf_op jit(solution)/shard_map/ppermute | solution.py:394
  134.0 2.2 copy-start
  180.0 71.1 %collective-permute-start.8 = (bf16[15,128,128]{2,1,0:T(8,128)(2,1)S(1)}, bf16[15,128,128]{2,1,0:T(8,128)(2,1)S(1)}, u32[]{:S(2)}, u32[]{:S(2)}) collective-permute-start(bf16[15,128,128]{2,1,0:T(8,128)(2,1)S(1)} %get-tuple-element.29), channel_id=1, source_target_pairs={{0,0},{8,1},{2,2},{10,3},{4,4},{12,5},{6,6},{14,7},{1,8},{9,9},{3,... | collective-permute-start | bytes 1474568 | tf_op jit(solution)/shard_map/ppermute | solution.py:470
  234.3 16.9 %collective-permute-start.9 = (bf16[15,128,128]{2,1,0:T(8,128)(2,1)S(1)}, bf16[15,128,128]{2,1,0:T(8,128)(2,1)S(1)}, u32[]{:S(2)}, u32[]{:S(2)}) collective-permute-start(bf16[15,128,128]{2,1,0:T(8,128)(2,1)S(1)} %get-tuple-element.30), channel_id=1, source_target_pairs={{0,1},{8,2},{2,3},{10,4},{4,5},{12,6},{6,7},{14,0},{1,9},{9,10},{3... | collective-permute-start | bytes 1474568 | tf_op jit(solution)/shard_map/ppermute | solution.py:470
  234.4 21.3 %collective-permute-start.10 = (bf16[15,128,128]{2,1,0:T(8,128)(2,1)S(1)}, bf16[15,128,128]{2,1,0:T(8,128)(2,1)S(1)}, u32[]{:S(2)}, u32[]{:S(2)}) collective-permute-start(bf16[15,128,128]{2,1,0:T(8,128)(2,1)S(1)} %get-tuple-element.31), channel_id=1, source_target_pairs={{0,2},{8,3},{2,4},{10,5},{4,6},{12,7},{6,0},{14,1},{1,10},{9,11},{... | collective-permute-start | bytes 1474568 | tf_op jit(solution)/shard_map/ppermute | solution.py:470
  234.4 29.1 %collective-permute-start.11 = (bf16[15,128,128]{2,1,0:T(8,128)(2,1)S(1)}, bf16[15,128,128]{2,1,0:T(8,128)(2,1)S(1)}, u32[]{:S(2)}, u32[]{:S(2)}) collective-permute-start(bf16[15,128,128]{2,1,0:T(8,128)(2,1)S(1)} %get-tuple-element.32), channel_id=1, source_target_pairs={{0,3},{8,4},{2,5},{10,6},{4,7},{12,0},{6,1},{14,2},{1,11},{9,12},{... | collective-permute-start | bytes 1474568 | tf_op jit(solution)/shard_map/ppermute | solution.py:470
  238.5 70.8 %collective-permute-start.12 = (bf16[15,128,128]{2,1,0:T(8,128)(2,1)S(1)}, bf16[15,128,128]{2,1,0:T(8,128)(2,1)S(1)}, u32[]{:S(2)}, u32[]{:S(2)}) collective-permute-start(bf16[15,128,128]{2,1,0:T(8,128)(2,1)S(1)} %get-tuple-element.33), channel_id=1, source_target_pairs={{0,4},{8,5},{2,6},{10,7},{4,0},{12,1},{6,2},{14,3},{1,12},{9,13},{... | collective-permute-start | bytes 1474568 | tf_op jit(solution)/shard_map/ppermute | solution.py:470
  251.2 65.6 %collective-permute-start.13 = (bf16[15,128,128]{2,1,0:T(8,128)(2,1)S(1)}, bf16[15,128,128]{2,1,0:T(8,128)(2,1)S(1)}, u32[]{:S(2)}, u32[]{:S(2)}) collective-permute-start(bf16[15,128,128]{2,1,0:T(8,128)(2,1)S(1)} %get-tuple-element.34), channel_id=1, source_target_pairs={{0,5},{8,6},{2,7},{10,0},{4,1},{12,2},{6,3},{14,4},{1,13},{9,14},{... | collective-permute-start | bytes 1474568 | tf_op jit(solution)/shard_map/ppermute | solution.py:470
  251.2 75.9 %collective-permute-start.14 = (bf16[15,128,128]{2,1,0:T(8,128)(2,1)S(1)}, bf16[15,128,128]{2,1,0:T(8,128)(2,1)S(1)}, u32[]{:S(2)}, u32[]{:S(2)}) collective-permute-start(bf16[15,128,128]{2,1,0:T(8,128)(2,1)S(1)} %get-tuple-element.35), channel_id=1, source_target_pairs={{0,6},{8,7},{2,0},{10,1},{4,2},{12,3},{6,4},{14,5},{1,14},{9,15},{... | collective-permute-start | bytes 1474568 | tf_op jit(solution)/shard_map/ppermute | solution.py:470
  255.7 72.1 %collective-permute-start.15 = (bf16[15,128,128]{2,1,0:T(8,128)(2,1)S(1)}, bf16[15,128,128]{2,1,0:T(8,128)(2,1)S(1)}, u32[]{:S(2)}, u32[]{:S(2)}) collective-permute-start(bf16[15,128,128]{2,1,0:T(8,128)(2,1)S(1)} %get-tuple-element.36), channel_id=1, source_target_pairs={{0,7},{8,0},{2,1},{10,2},{4,3},{12,4},{6,5},{14,6},{1,15},{9,8},{3... | collective-permute-start | bytes 1474568 | tf_op jit(solution)/shard_map/ppermute | solution.py:470

commit v2 on v1

--- a/solution.py
+++ b/solution.py
@@ -29,14 +29,15 @@
         "mate_a": [(place(v), place(v ^ 1)) for v in range(total) if not moved[v]],
         "mate_b": [(place(v), place(v ^ 1)) for v in range(total) if moved[v]],
         "pair": [(place(v), place(v ^ 1)) for v in range(total)],
-        "far_a": [(v, place(beside(v))) for v in range(total) if has_outer[v] and (edge[v] or not moved[v])],
+        "far_a": [(v, place(beside(v))) for v in range(total) if has_outer[v] and moved[v] == edge[v]],
         "far_b": [(place(v), place(beside(v))) for v in range(total) if has_outer[v] and moved[v] and not edge[v]],
+        "far_c": [(v, place(beside(v))) for v in range(total) if has_outer[v] and edge[v] and not moved[v]],
         "outer": [(place(v), place(beside(v))) for v in range(total) if has_outer[v]],
         "shifts": [[(place(v), v // cols * cols + (v + s) % cols) for v in range(total)] for s in range(cols)],
     }
 
 
-BASE, ODD, MOVED, FAR_A = range(4)
+BASE, ODD, MOVED, FAR = range(4)
 
 
 def widths(slots, rows, low):
@@ -103,39 +104,29 @@
     lax.fori_loop(0, count, one, 0)
 
 
-def pack_kernel(rows, meta, first, pattern, tiles, packed, held, sem, osem):
+def pack_kernel(rows, first, pattern, tiles, packed, held, table, sem):
     count = tiles.shape[0]
     slots = count // rows
     inward = pltpu.make_async_copy(tiles, held, sem)
     inward.start()
     start = first[0]
     low = first[1] == 0
+    trash = packed.shape[0]
+    for p in range(trash):
+        table[p] = 0
     tables = [widths(slots, rows, side) for side in (False, True)]
     starts = [[sum(table[:t]) for t in range(rows)] for table in tables]
-    inward.wait()
     for t in range(rows):
-        offset = jnp.where(low, starts[1][t], starts[0][t])
-        end = offset + jnp.where(low, tables[1][t], tables[0][t])
-
-        def one(k, place, t=t, end=end):
+        place = jnp.where(low, starts[1][t], starts[0][t])
+        end = place + jnp.where(low, tables[1][t], tables[0][t])
+        for k in range(slots):
             col = pattern[start + t, k]
             take = (col >= 0) & jnp.where(low, col <= start + H - 2, col >= start) & (place < end)
-
-            @pl.when(take)
-            def _():
-                pltpu.make_async_copy(held.at[t * slots + k], packed.at[place], osem).start()
-
-            return place + take.astype(jnp.int32)
-
-        place = offset
-        for k in range(slots):
-            place = one(k, place)
-
-        def wait(k, carry):
-            pltpu.make_async_copy(held.at[0], packed.at[0], osem).wait()
-            return carry
-
-        lax.fori_loop(0, place - offset, wait, 0)
+            table[jnp.where(take, place, trash)] = t * slots + k
+            place = place + take.astype(jnp.int32)
+    inward.wait()
+    for p in range(trash):
+        packed[p] = held[table[p]]
 
 
 def near_kernel(rows, meta, table, z_home, z_came, mate_a, mate_b, znear, turned_far, turned_own, pool, zd, zf, zo, sem, osem):
@@ -172,8 +163,8 @@
 
 
 def product_kernel(
-    total, rows, meta, ftab, ztab, keep, col_of, f_home, f_came, far_a, far_b, znear, turned,
-    prod, lent, packed, fd, zd, pd, zt, fpool, zpool, part, fsem, zsem, tsem, nsem, psem, osem,
+    total, rows, meta, ftab, ztab, keep, col_of, f_home, f_came, far_a, far_b, far_c, znear, turned,
+    prod, lent_0, lent_1, packed, fd, zd, pd, zt, fpool, zpool, part, fsem, zsem, tsem, nsem, psem, osem,
 ):
     count, tile = f_home.shape[:2]
     span, wide = 3 * rows, 2 * H + 2
@@ -181,7 +172,12 @@
     far_row = jnp.where(odd == 0, 0, 2 * rows)
     near_rows = pl.ds(pl.multiple_of(rows * tile * (1 - odd), rows * tile), 2 * rows * tile)
     either(meta[MOVED], f_came, f_home, lambda fock: pltpu.make_async_copy(fock, fpool.at[:count], fsem).start())
-    either(meta[FAR_A], far_a, far_b, lambda far: pltpu.make_async_copy(far, zpool.at[: far.shape[0]], zsem).start())
+    for kind, far in enumerate((far_b, far_a, far_c)):
+
+        @pl.when(meta[FAR] == kind)
+        def _(far=far):
+            pltpu.make_async_copy(far, zpool.at[: far.shape[0]], zsem).start()
+
     near_in = pltpu.make_async_copy(znear, zd.at[near_rows], nsem)
     near_in.start()
     turn_in = pltpu.make_async_copy(turned, zt, tsem)
@@ -219,8 +215,10 @@
             return carry
 
         lax.fori_loop(0, wide // step, block, 0)
-    lent_cols = pl.ds(pl.multiple_of((1 - odd) * rows * tile, rows * tile), 2 * rows * tile)
-    writes = [pltpu.make_async_copy(pd, prod, psem.at[0]), pltpu.make_async_copy(pd.at[:, lent_cols], lent, psem.at[1])]
+    writes = [pltpu.make_async_copy(pd, prod, psem.at[0])]
+    for i, lent in enumerate((lent_0, lent_1)):
+        cols = pl.ds(pl.multiple_of((1 - odd + i) * rows * tile, rows * tile), rows * tile)
+        writes.append(pltpu.make_async_copy(pd.at[:, cols], lent, psem.at[1 + i]))
     for write in writes:
         write.start()
     turn_in.wait()
@@ -248,7 +246,7 @@
         write.wait()
 
 
-def own_kernel(total, rows, meta, col_of, turned, prod, lent, near, zt, pd, acc_ref, out, sem, osem):
+def own_kernel(total, rows, meta, col_of, turned, prod, lent_0, lent_1, near, zt, pd, acc_ref, out, sem, osem):
     count, tile = near.shape[:2]
     slots = count // rows
     base, odd = meta[BASE], meta[ODD]
@@ -261,7 +259,8 @@
     copies = [
         pltpu.make_async_copy(turned, zt, sem.at[0]),
         pltpu.make_async_copy(prod, pd.at[part(odd, 1)], sem.at[1]),
-        pltpu.make_async_copy(lent, pd.at[part(1 - odd, 1), part(1 - odd, 2)], sem.at[2]),
+        pltpu.make_async_copy(lent_0, pd.at[part(1 - odd, 1), part(1 - odd, 1)], sem.at[2]),
+        pltpu.make_async_copy(lent_1, pd.at[part(1 - odd, 1), part(2 - odd, 1)], sem.at[3]),
     ]
     for copy in copies:
         copy.start()
@@ -293,47 +292,47 @@
 
 
 def join_kernel(rows, place, where, near, far, *rest):
-    outs, (a, b, out, sem, far_sem, osem) = rest[:-6], rest[-6:]
+    outs = rest
     slots = near.shape[0] // rows
     tiles = far.shape[0]
-    inward = pltpu.make_async_copy(far, b.at[:tiles], far_sem)
-    inward.start()
-    copies = [pltpu.make_async_copy(near.at[pl.ds(where[n] * slots, slots)], a.at[n], sem.at[n]) for n in range(len(outs))]
-    for copy in copies:
-        copy.start()
-    b[tiles] = jnp.zeros(b.shape[1:], b.dtype)
-    inward.wait()
-    for n, target in enumerate(outs):
+    for n, out in enumerate(outs):
         row = where[n]
-        copies[n].wait()
-        for s in range(slots):
-            out[n, s] = (a[n, s].astype(jnp.float32) + b[place[row, s]].astype(jnp.float32)).astype(out.dtype)
-        pltpu.make_async_copy(out.at[n], target, osem.at[n]).start()
-    for n, target in enumerate(outs):
-        pltpu.make_async_copy(out.at[n], target, osem.at[n]).wait()
+
+        def one(s, carry, out=out, row=row):
+            at = place[row, s]
+
+            @pl.when(at < tiles)
+            def _():
+                out[s] = near[row * slots + s] + far[at]
+
+            @pl.when(at >= tiles)
+            def _():
+                out[s] = near[row * slots + s]
+
+            return carry
+
+        lax.fori_loop(0, slots, one, 0)
 
 
 def gather_kernel(slot, present, *rest):
-    parts, (out, held, isem, osem) = rest[:-4], rest[-4:]
+    parts, (out, sem) = rest[:-2], rest[-2:]
     for s, part in enumerate(parts):
-        pltpu.make_async_copy(part, held.at[s], isem.at[s]).start()
-    for s, part in enumerate(parts):
-        pltpu.make_async_copy(part, held.at[s], isem.at[s]).wait()
 
         @pl.when(present[s] != 0)
-        def _(s=s):
-            pltpu.make_async_copy(held.at[s], out.at[slot[s]], osem).start()
-
-    pltpu.make_async_copy(out, out, osem).wait()
-
-
-def call(kernel, scalars, arrays, outs, scratch, name=None, limit=60, cost=1.0):
+        def _(s=s, part=part):
+            pltpu.make_async_copy(part, out.at[slot[s]], sem).start()
+
+    pltpu.make_async_copy(out, out, sem).wait()
+
+
+def call(kernel, scalars, arrays, outs, scratch, name=None, limit=60, cost=1.0, held_in=False, held_out=False):
     any_spec = pl.BlockSpec(memory_space=pl.ANY)
     smem = pl.BlockSpec(memory_space=pltpu.SMEM)
+    vmem = pl.BlockSpec(memory_space=pltpu.VMEM)
     return pl.pallas_call(
         kernel,
-        in_specs=[smem] * len(scalars) + [any_spec] * len(arrays),
-        out_specs=[any_spec] * len(outs),
+        in_specs=[smem] * len(scalars) + [vmem if held_in else any_spec] * len(arrays),
+        out_specs=[vmem if held_out else any_spec] * len(outs),
         out_shape=outs,
         scratch_shapes=scratch,
         compiler_params=pltpu.CompilerParams(vmem_limit_bytes=limit * 1024 * 1024),
@@ -355,9 +354,9 @@
     base = block * rows
     odd = number % 2
     moved = (my_row + my_col) % 2
-    at_edge = (number == 0) | (number == count_cols - 1)
+    at_edge = ((number == 0) | (number == count_cols - 1)).astype(jnp.int32)
     home = (my_row * count_cols + my_col) * rows
-    meta = jnp.stack([jnp.asarray(m, jnp.int32) for m in (base, odd, moved, (moved == 1) | at_edge)])
+    meta = jnp.stack([jnp.asarray(m, jnp.int32) for m in (base, odd, moved, jnp.where(moved == 1, 1, 2 * at_edge))])
     dtype = fock_tiles.dtype
     packed_tiles = max(sum(widths(slots, rows, side)) for side in (False, True))
     span = 3 * rows
@@ -409,12 +408,14 @@
 
     def pack(first, tiles):
         kernel = functools.partial(pack_kernel, rows)
-        scalars = [meta, jnp.stack([jnp.asarray(f, jnp.int32) for f in first]), basis_pattern]
-        return call(kernel, scalars, [tiles], [packed_shape], [pool(count), dma, dma], name="pack", limit=8, cost=5)[0]
+        scalars = [jnp.stack([jnp.asarray(f, jnp.int32) for f in first]), basis_pattern]
+        scratch = [pool(count), pltpu.SMEM((packed_tiles + 1,), jnp.int32), dma]
+        return call(kernel, scalars, [tiles], [packed_shape], scratch, name="pack", limit=12, cost=4, held_out=True)[0]
 
     z_came = permute(z_home, "swap")
     mate_a = permute(z_home, "mate_a")
-    far_a = permute(pack((home, my_col % 2), z_home), "far_a")
+    packed_a = pack((home, my_col % 2), z_home)
+    far_a = permute(packed_a, "far_a")
     f_came = permute(f_home, "swap")
     z_came, far_a = lax.optimization_barrier((z_came, far_a))
     far_b = permute(pack((base, odd), z_came), "far_b")
@@ -429,29 +430,32 @@
         limit=40,
         cost=14,
     )
-    prod, lent, packed = call(
+    packed_a, turned_far = lax.optimization_barrier((packed_a, turned_far))
+    far_c = permute(packed_a, "far_c")
+    prod, lent_0, lent_1, packed = call(
         functools.partial(product_kernel, total, rows),
         [meta, fock_table, far_table, keep, far_cols],
-        [f_home, f_came, far_a, far_b, znear, turned_far],
-        [shape(rows * tile, span * tile), shape(rows * tile, 2 * rows * tile), packed_shape],
+        [f_home, f_came, far_a, far_b, far_c, znear, turned_far],
+        [shape(rows * tile, span * tile), shape(rows * tile, rows * tile), shape(rows * tile, rows * tile), packed_shape],
         [dense(rows, span), dense(span, span), dense(rows, span), dense(rows, rows)]
         + [pool(count + 1), pool(packed_tiles + 1), dense(rows, 2 * H)]
         + [dma] * 4
-        + [dma((2,)), dma],
+        + [dma((3,)), dma],
         name="product",
+        limit=50,
         cost=27,
     )
     far = permute(packed, "outer")
-    lent = permute(lent, "pair")
+    lent_0, lent_1 = permute(lent_0, "pair"), permute(lent_1, "pair")
     (near_sum,) = call(
         functools.partial(own_kernel, total, rows),
         [meta, own_cols],
-        [turned_own, prod, lent],
+        [turned_own, prod, lent_0, lent_1],
         [block_shape],
-        [dense(rows, 2 * rows), dense(2 * rows, span), dense(rows, span + 1), pool(count), dma((3,)), dma],
+        [dense(rows, 2 * rows), dense(2 * rows, span), dense(rows, span + 1), pool(count), dma((4,)), dma],
         name="own",
         limit=40,
-        cost=20,
+        cost=0.1,
     )
     shift = (lax.dynamic_slice_in_dim(new_index, base, rows, 0) // rows - number) % count_cols
     hit = shift[None, :] == jnp.arange(count_cols, dtype=jnp.int32)[:, None]
@@ -461,11 +465,12 @@
         [own_place, where],
         [near_sum, far],
         [shape(slots, tile, tile)] * count_cols,
-        [pltpu.VMEM((count_cols, slots, tile, tile), dtype), pool(packed_tiles + 1), pltpu.VMEM((count_cols, slots, tile, tile), dtype)]
-        + [dma((count_cols,)), dma, dma((count_cols,))],
+        [],
         name="join",
-        limit=24,
-        cost=5,
+        limit=16,
+        cost=4,
+        held_in=True,
+        held_out=True,
     )
     parts = [lax.ppermute(out, AXES, plan["shifts"][s]) for s, out in enumerate(outs)]
     wanted = home + jnp.arange(rows, dtype=jnp.int32)
@@ -480,10 +485,11 @@
         [slot, present],
         parts,
         [shape(rows, slots, tile, tile)],
-        [pltpu.VMEM((count_cols, slots, tile, tile), dtype), dma((count_cols,)), dma],
+        [dma],
         name="gather",
         limit=16,
-        cost=4,
+        cost=3,
+        held_in=True,
     )
     return out
 

time: 335 us -> 322 us (0.961)
  Pallas kernels: 89.9 us -> 76 us
  waiting for transfers between devices: 137 us -> 146 us
  starting transfers between devices: 91.4 us -> 85.7 us
    pallas_call x7, Pallas kernels: 89.9 us -> 76 us  [call(): pl.pallas_call(kernel, in_specs=[smem] * len(scalars) + [vmem if held_in...]
    ppermute x8 -> x10, waiting for transfers between devices: 61.3 us -> 71.6 us  [permute(): return lax.ppermute(x, AXES, plan[name])]
    ppermute x8, starting transfers between devices: 71.4 us -> 65.1 us  [body(): lax.ppermute(out, AXES, plan['shifts'][s])]
    unnamed x29 -> x27, local copies, waits for them, and re-layouts: 5.37 us -> 7.01 us
    ppermute x8 -> x10, starting transfers between devices: 20.1 us -> 20.6 us  [permute(): return lax.ppermute(x, AXES, plan[name])]
  transfers between devices with their start and end apart: 16 -> 18, of which waited for: 12 -> 14; matrix products, arithmetic and copies ran while one was open for 3% -> 2% of each run, Pallas kernels for 15% -> 13%
where the time goes in v2:
time: 322 us
  waiting for transfers between devices  146 us (45%)
  starting transfers between devices  85.7 us (27%)
  Pallas kernels  76 us (24%)
  local copies, waits for them, and re-layouts  9.02 us (3%)
  other arithmetic  4.19 us (1%)
    pallas_call x7, Pallas kernels, call(): pl.pallas_call(kernel, in_specs=[smem] * len(scalars) + [vmem if held_in...  76 us
    ppermute x8, waiting for transfers between devices, body(): lax.ppermute(out, AXES, plan['shifts'][s])  74.6 us
    ppermute x10, waiting for transfers between devices, permute(): return lax.ppermute(x, AXES, plan[name])  71.6 us
    ppermute x8, starting transfers between devices, body(): lax.ppermute(out, AXES, plan['shifts'][s])  65.1 us
    ppermute x10, starting transfers between devices, permute(): return lax.ppermute(x, AXES, plan[name])  20.6 us
    unnamed x27, local copies, waits for them, and re-layouts  7.01 us
  transfers between devices with their start and end apart: 18, of which 14 were waited for; matrix products, arithmetic and copies ran while one was open for 2% of the time, Pallas kernels for 13%

profile of v2, /device:TPU:14, one launch (start us, length us, event | category | flops | bytes accessed | tf_op | source)
XLA Modules:
  0.0 321.7 jit_solution(16872226018245909680)
XLA Ops:
  0.0 1.9 collective-permute-start
  1.9 0.8 copy.39.pattern
  2.8 5.0 %pack.2 = bf16[92,128,128]{2,1,0:T(8,128)(2,1)S(1)} custom-call(s32[2]{0:T(128)S(1)} %pad_add_fusion.7.first, s32[256,15]{1,0:T(8,128)S(1)} %copy.39.pattern, bf16[120,128,128]{2,1,0:T(8,128)(2,1)} %bitcast.11.tiles.z_home), custom_call_target="tpu_custom_call" | custom-call | bytes 12000000 | tf_op jit(solution)/shard_map/pack/pallas_call | solution.py:332
  7.9 1.3 collective-permute-start.1
  9.2 1.3 collective-permute-start.2
  10.5 34.6 %collective-permute-done.1.far_a = bf16[92,128,128]{2,1,0:T(8,128)(2,1)S(1)} collective-permute-done((bf16[92,128,128]{2,1,0:T(8,128)(2,1)S(1)}, bf16[92,128,128]{2,1,0:T(8,128)(2,1)S(1)}, u32[]{:S(2)}, u32[]{:S(2)}) %collective-permute-start.1) | collective-permute-done | bytes 3014688 | tf_op jit(solution)/shard_map/ppermute | solution.py:393
  45.0 1.6 copy-done.2
  46.7 0.7 collective-permute-done.z_came.tiles
  47.3 3.2 collective-permute-start.3
  50.5 3.0 collective-permute-start.4
  53.6 0.1 copy.41
  53.7 0.1 copy.42
  53.8 0.8 copy.40
  54.6 1.1 pad_add_fusion
  55.6 0.1 subtract_select_fusion
  56.3 0.1 copy.54
  56.5 0.1 copy.49
  56.7 0.1 copy.58
  56.8 0.1 copy.52
  57.0 0.1 copy.57
  57.3 0.2 select_reduce_fusion.1
  57.5 6.6 %pack.3 = bf16[92,128,128]{2,1,0:T(8,128)(2,1)} custom-call(s32[2]{0:T(128)S(1)} %pad_add_fusion.8.first, s32[256,15]{1,0:T(8,128)S(1)} %copy.39.pattern, bf16[120,128,128]{2,1,0:T(8,128)(2,1)} %collective-permute-done.z_came.tiles), custom_call_target="tpu_custom_call" | custom-call | bytes 12000000 | tf_op jit(solution)/shard_map/pack/pallas_call | solution.py:332
  64.1 3.1 collective-permute-start.5
  67.2 13.0 %near.1 = (bf16[2048,3072]{1,0:T(8,128)(2,1)}, bf16[1024,1024]{1,0:T(8,128)(2,1)S(1)}, bf16[1024,2048]{1,0:T(8,128)(2,1)}) custom-call(s32[4]{0:T(128)S(1)} %pad_add_fusion.6.meta, s32[16,24]{1,0:T(8,128)S(1)} %compare_select_fusion.table, bf16[120,128,128]{2,1,0:T(8,128)(2,1)} %bitcast.11.tiles.z_home, ...), custom_call_target="tpu_custom_call" | custom-call | bytes 42000000 | tf_op jit(solution)/shard_map/near/pallas_call | solution.py:332
  80.3 1.3 copy-done.1
  81.6 2.3 collective-permute-start.6
  84.3 0.1 copy.46
  84.5 0.9 convert_reduce_fusion
  85.5 0.1 and_select_fusion
  85.6 0.1 copy.59
  85.7 0.1 lt.78
  85.8 0.1 copy.60
  86.0 0.2 select_reduce_fusion
  86.2 0.1 select_reduce_fusion.2
  86.3 0.1 select_reduce_fusion.4
  86.4 0.1 select_reduce_fusion.3
  86.6 11.2 %collective-permute-done.4.f_came = bf16[120,128,128]{2,1,0:T(8,128)(2,1)} collective-permute-done((bf16[120,128,128]{2,1,0:T(8,128)(2,1)}, bf16[120,128,128]{2,1,0:T(8,128)(2,1)}, u32[]{:S(2)}, u32[]{:S(2)}) %collective-permute-start.4) | collective-permute-done | bytes 3932192 | tf_op jit(solution)/shard_map/ppermute | solution.py:393
  97.8 1.5 collective-permute-done.5.far_b
  99.3 26.8 %product.1 = (bf16[1024,3072]{1,0:T(8,128)(2,1)}, bf16[1024,1024]{1,0:T(8,128)(2,1)}, bf16[1024,1024]{1,0:T(8,128)(2,1)}, bf16[92,128,128]{2,1,0:T(8,128)(2,1)}) custom-call(s32[4]{0:T(128)S(1)} %pad_add_fusion.6.meta, s32[8,24]{1,0:T(8,128)S(1)} %compare_select_fusion.3.ftab, s32[8,24]{1,0:T(8,128)S(1)} %compare_select_fusion.2.ztab, ...), custom_call_target="tpu_custom_call" | custom-call | bytes 81000000 | tf_op jit(solution)/shard_map/product/pallas_call | solution.py:332
  126.1 4.0 %collective-permute-start.9 = (bf16[92,128,128]{2,1,0:T(8,128)(2,1)}, bf16[92,128,128]{2,1,0:T(8,128)(2,1)S(1)}, u32[]{:S(2)}, u32[]{:S(2)}) collective-permute-start(bf16[92,128,128]{2,1,0:T(8,128)(2,1)} %get-tuple-element.34), channel_id=1, source_target_pairs={{8,2},{2,8},{10,4},{4,10},{12,6},{6,12},{14,1},{1,14},{9,3},{3,9},... | collective-permute-start | bytes 9043976 | tf_op jit(solution)/shard_map/ppermute | solution.py:393
  130.2 0.5 collective-permute-start.8
  130.8 0.1 and_select_fusion.2
  130.9 0.1 select_reduce_fusion.6.where
  131.0 3.7 %collective-permute-done.7.lent_0 = bf16[1024,1024]{1,0:T(8,128)(2,1)} collective-permute-done((bf16[1024,1024]{1,0:T(8,128)(2,1)}, bf16[1024,1024]{1,0:T(8,128)(2,1)}, u32[]{:S(2)}, u32[]{:S(2)}) %collective-permute-start.7) | collective-permute-done | bytes 2097184 | tf_op jit(solution)/shard_map/ppermute | solution.py:393
  134.7 3.0 collective-permute-done.8.lent_1
  137.7 2.2 copy-done
  139.9 18.5 %own.1.near = bf16[120,128,128]{2,1,0:T(8,128)(2,1)S(1)} custom-call(s32[4]{0:T(128)S(1)} %pad_add_fusion.6.meta, s32[8,15]{1,0:T(8,128)S(1)} %get-tuple-element.51.col_of, bf16[1024,2048]{1,0:T(8,128)(2,1)S(1)} %copy-done, bf16[1024,3072]{1,0:T(8,128)(2,1)} %get-tuple-element.31.prod, bf16[1024,1024]{1,0:T(8,128)(2,1)} %collective-permute-done.7.lent_0, ...), custom_call_target="tpu_custom_call" | custom-call | bytes 300000 | tf_op jit(solution)/shard_map/own/pallas_call | solution.py:332
  158.4 17.0 %collective-permute-done.9.far = bf16[92,128,128]{2,1,0:T(8,128)(2,1)S(1)} collective-permute-done((bf16[92,128,128]{2,1,0:T(8,128)(2,1)}, bf16[92,128,128]{2,1,0:T(8,128)(2,1)S(1)}, u32[]{:S(2)}, u32[]{:S(2)}) %collective-permute-start.9) | collective-permute-done | bytes 3014688 | tf_op jit(solution)/shard_map/ppermute | solution.py:393
  175.4 3.6 %join.1 = (bf16[15,128,128]{2,1,0:T(8,128)(2,1)S(1)}, bf16[15,128,128]{2,1,0:T(8,128)(2,1)S(1)}, bf16[15,128,128]{2,1,0:T(8,128)(2,1)S(1)}, bf16[15,128,128]{2,1...) custom-call(s32[8,15]{1,0:T(8,128)S(1)} %compare_select_fusion.4.pla, ...), custom_call_target="tpu_custom_call" | custom-call | bytes 12000000 | tf_op jit(solution)/shard_map/join/pallas_call | solution.py:332
  179.0 41.3 %collective-permute-start.10 = (bf16[15,128,128]{2,1,0:T(8,128)(2,1)S(1)}, bf16[15,128,128]{2,1,0:T(8,128)(2,1)S(1)}, u32[]{:S(2)}, u32[]{:S(2)}) collective-permute-start(bf16[15,128,128]{2,1,0:T(8,128)(2,1)S(1)} %get-tuple-element.35), channel_id=1, source_target_pairs={{0,0},{8,1},{2,2},{10,3},{4,4},{12,5},{6,6},{14,7},{1,8},{9,9},{3,... | collective-permute-start | bytes 1474568 | tf_op jit(solution)/shard_map/ppermute | solution.py:475
  220.5 4.5 %collective-permute-start.13 = (bf16[15,128,128]{2,1,0:T(8,128)(2,1)S(1)}, bf16[15,128,128]{2,1,0:T(8,128)(2,1)S(1)}, u32[]{:S(2)}, u32[]{:S(2)}) collective-permute-start(bf16[15,128,128]{2,1,0:T(8,128)(2,1)S(1)} %get-tuple-element.38), channel_id=1, source_target_pairs={{0,3},{8,4},{2,5},{10,6},{4,7},{12,0},{6,1},{14,2},{1,11},{9,12},{... | collective-permute-start | bytes 1474568 | tf_op jit(solution)/shard_map/ppermute | solution.py:475
  225.0 9.4 %collective-permute-start.14 = (bf16[15,128,128]{2,1,0:T(8,128)(2,1)S(1)}, bf16[15,128,128]{2,1,0:T(8,128)(2,1)S(1)}, u32[]{:S(2)}, u32[]{:S(2)}) collective-permute-start(bf16[15,128,128]{2,1,0:T(8,128)(2,1)S(1)} %get-tuple-element.39), channel_id=1, source_target_pairs={{0,4},{8,5},{2,6},{10,7},{4,0},{12,1},{6,2},{14,3},{1,12},{9,13},{... | collective-permute-start | bytes 1474568 | tf_op jit(solution)/shard_map/ppermute | solution.py:475
  234.3 2.8 collective-permute-done.10.rest_0_
  237.2 0.2 collective-permute-done.11.rest_1_
  237.4 3.8 %collective-permute-start.16 = (bf16[15,128,128]{2,1,0:T(8,128)(2,1)S(1)}, bf16[15,128,128]{2,1,0:T(8,128)(2,1)S(1)}, u32[]{:S(2)}, u32[]{:S(2)}) collective-permute-start(bf16[15,128,128]{2,1,0:T(8,128)(2,1)S(1)} %get-tuple-element.41), channel_id=1, source_target_pairs={{0,6},{8,7},{2,0},{10,1},{4,2},{12,3},{6,4},{14,5},{1,14},{9,15},{... | collective-permute-start | bytes 1474568 | tf_op jit(solution)/shard_map/ppermute | solution.py:475
  241.1 6.0 %collective-permute-start.17 = (bf16[15,128,128]{2,1,0:T(8,128)(2,1)S(1)}, bf16[15,128,128]{2,1,0:T(8,128)(2,1)S(1)}, u32[]{:S(2)}, u32[]{:S(2)}) collective-permute-start(bf16[15,128,128]{2,1,0:T(8,128)(2,1)S(1)} %get-tuple-element.42), channel_id=1, source_target_pairs={{0,7},{8,0},{2,1},{10,2},{4,3},{12,4},{6,5},{14,6},{1,15},{9,8},{3... | collective-permute-start | bytes 1474568 | tf_op jit(solution)/shard_map/ppermute | solution.py:475
  247.1 0.2 select_reduce_fusion.5
  247.4 0.1 convert_reduce_fusion.1
  247.5 7.4 %collective-permute-done.13.rest_3_ = bf16[15,128,128]{2,1,0:T(8,128)(2,1)S(1)} collective-permute-done((bf16[15,128,128]{2,1,0:T(8,128)(2,1)S(1)}, bf16[15,128,128]{2,1,0:T(8,128)(2,1)S(1)}, u32[]{:S(2)}, u32[]{:S(2)}) %collective-permute-start.13) | collective-permute-done | bytes 491552 | tf_op jit(solution)/shard_map/ppermute | solution.py:475
  254.9 40.3 %collective-permute-done.14.rest_4_ = bf16[15,128,128]{2,1,0:T(8,128)(2,1)S(1)} collective-permute-done((bf16[15,128,128]{2,1,0:T(8,128)(2,1)S(1)}, bf16[15,128,128]{2,1,0:T(8,128)(2,1)S(1)}, u32[]{:S(2)}, u32[]{:S(2)}) %collective-permute-start.14) | collective-permute-done | bytes 491552 | tf_op jit(solution)/shard_map/ppermute | solution.py:475
  295.3 9.8 %collective-permute-done.15.rest_5_ = bf16[15,128,128]{2,1,0:T(8,128)(2,1)S(1)} collective-permute-done((bf16[15,128,128]{2,1,0:T(8,128)(2,1)S(1)}, bf16[15,128,128]{2,1,0:T(8,128)(2,1)S(1)}, u32[]{:S(2)}, u32[]{:S(2)}) %collective-permute-start.15) | collective-permute-done | bytes 491552 | tf_op jit(solution)/shard_map/ppermute | solution.py:475
  305.1 13.4 %collective-permute-done.16.rest_6_ = bf16[15,128,128]{2,1,0:T(8,128)(2,1)S(1)} collective-permute-done((bf16[15,128,128]{2,1,0:T(8,128)(2,1)S(1)}, bf16[15,128,128]{2,1,0:T(8,128)(2,1)S(1)}, u32[]{:S(2)}, u32[]{:S(2)}) %collective-permute-start.16) | collective-permute-done | bytes 491552 | tf_op jit(solution)/shard_map/ppermute | solution.py:475
  318.5 0.6 collective-permute-done.17.rest_7_
  319.1 2.5 gather.1
  (69 shorter events, 2.3 us)
Async XLA Ops:
  0.0 47.3 %collective-permute-start = (bf16[120,128,128]{2,1,0:T(8,128)(2,1)}, bf16[120,128,128]{2,1,0:T(8,128)(2,1)}, u32[]{:S(2)}, u32[]{:S(2)}) collective-permute-start(bf16[120,128,128]{2,1,0:T(8,128)(2,1)} %bitcast.11.tiles.z_home), channel_id=1, source_target_pairs={{1,8},{3,10},{5,12},{7,14},{8,1},{10,3},{12,5},{14,7},{17,24},{19,... | collective-permute-start | bytes 11796488 | tf_op jit(solution)/shard_map/ppermute | solution.py:393
  2.8 50.7 %copy-start.3 = (s32[256,15]{0,1:T(8,128)S(1)}, s32[256,15]{0,1:T(8,128)}, u32[]{:S(2)}) copy-start(s32[256,15]{0,1:T(8,128)} %param.12) | copy-start | bytes 46084
  2.8 50.8 %copy-start.4 = (s32[256,15]{0,1:T(8,128)S(1)}, s32[256,15]{0,1:T(8,128)}, u32[]{:S(2)}) copy-start(s32[256,15]{0,1:T(8,128)} %param.15) | copy-start | bytes 46084
  2.8 51.0 %copy-start.5 = (s32[256,15]{0,1:T(8,128)S(1)}, s32[256,15]{0,1:T(8,128)}, u32[]{:S(2)}) copy-start(s32[256,15]{0,1:T(8,128)} %param.16) | copy-start | bytes 46084
  7.9 37.2 %collective-permute-start.1 = (bf16[92,128,128]{2,1,0:T(8,128)(2,1)S(1)}, bf16[92,128,128]{2,1,0:T(8,128)(2,1)S(1)}, u32[]{:S(2)}, u32[]{:S(2)}) collective-permute-start(bf16[92,128,128]{2,1,0:T(8,128)(2,1)S(1)} %pack.2), channel_id=1, source_target_pairs={{2,8},{4,10},{6,12},{7,1},{8,14},{9,3},{11,5},{13,7},{18,24},{20,2... | collective-permute-start | bytes 9043976 | tf_op jit(solution)/shard_map/ppermute | solution.py:393
  9.2 58.0 %collective-permute-start.2 = (bf16[120,128,128]{2,1,0:T(8,128)(2,1)}, bf16[120,128,128]{2,1,0:T(8,128)(2,1)}, u32[]{:S(2)}, u32[]{:S(2)}) collective-permute-start(bf16[120,128,128]{2,1,0:T(8,128)(2,1)} %bitcast.11.tiles.z_home), channel_id=1, source_target_pairs={{0,8},{2,10},{4,12},{6,14},{9,1},{11,3},{13,5},{15,7},{16,24},{18,... | collective-permute-start | bytes 11796488 | tf_op jit(solution)/shard_map/ppermute | solution.py:393
  45.0 1.6 copy-start.2
  47.3 19.9 %collective-permute-start.3 = (bf16[120,128,128]{2,1,0:T(8,128)(2,1)}, bf16[120,128,128]{2,1,0:T(8,128)(2,1)}, u32[]{:S(2)}, u32[]{:S(2)}) collective-permute-start(bf16[120,128,128]{2,1,0:T(8,128)(2,1)} %collective-permute-done.z_came.tiles), channel_id=1, source_target_pairs={{8,0},{10,2},{12,4},{14,6},{1,9},{3,11},{5,13},{7,15},{24,16},{26,... | collective-permute-start | bytes 11796488 | tf_op jit(solution)/shard_map/ppermute | solution.py:393
  50.5 47.3 %collective-permute-start.4 = (bf16[120,128,128]{2,1,0:T(8,128)(2,1)}, bf16[120,128,128]{2,1,0:T(8,128)(2,1)}, u32[]{:S(2)}, u32[]{:S(2)}) collective-permute-start(bf16[120,128,128]{2,1,0:T(8,128)(2,1)} %bitcast.16.f_home), channel_id=1, source_target_pairs={{1,8},{3,10},{5,12},{7,14},{8,1},{10,3},{12,5},{14,7},{17,24},{19,... | collective-permute-start | bytes 11796488 | tf_op jit(solution)/shard_map/ppermute | solution.py:393
  64.1 21.3 %copy-start.7 = (s32[8]{0:T(128)S(1)}, s32[8]{0:T(128)}, u32[]{:S(2)}) copy-start(s32[8]{0:T(128)} %constant.140.clone) | copy-start | bytes 100
  64.1 21.3 %copy-start.8 = (s32[8]{0:T(128)S(1)}, s32[8]{0:T(128)}, u32[]{:S(2)}) copy-start(s32[8]{0:T(128)} %constant.139.clone) | copy-start | bytes 100
  64.1 21.3 %copy-start.9 = (s32[8]{0:T(128)S(1)}, s32[8]{0:T(128)}, u32[]{:S(2)}) copy-start(s32[8]{0:T(128)} %constant.138.clone) | copy-start | bytes 100
  64.1 21.3 %copy-start.10 = (s32[8]{0:T(128)S(1)}, s32[8]{0:T(128)}, u32[]{:S(2)}) copy-start(s32[8]{0:T(128)} %constant.137.clone) | copy-start | bytes 100
  64.1 35.1 %collective-permute-start.5 = (bf16[92,128,128]{2,1,0:T(8,128)(2,1)}, bf16[92,128,128]{2,1,0:T(8,128)(2,1)}, u32[]{:S(2)}, u32[]{:S(2)}) collective-permute-start(bf16[92,128,128]{2,1,0:T(8,128)(2,1)} %pack.3), channel_id=1, source_target_pairs={{8,2},{10,4},{12,6},{3,9},{5,11},{7,13},{24,18},{26,20},{28,22},{1... | collective-permute-start | bytes 9043976 | tf_op jit(solution)/shard_map/ppermute | solution.py:393
  80.2 1.3 copy-start.1
  81.6 17.7 %collective-permute-start.6 = (bf16[92,128,128]{2,1,0:T(8,128)(2,1)S(1)}, bf16[92,128,128]{2,1,0:T(8,128)(2,1)}, u32[]{:S(2)}, u32[]{:S(2)}) collective-permute-start(bf16[92,128,128]{2,1,0:T(8,128)(2,1)S(1)} %pack.2), channel_id=1, source_target_pairs={{15,16},{16,15}} | collective-permute-start | bytes 9043976 | tf_op jit(solution)/shard_map/ppermute | solution.py:393
  99.3 31.5 %copy-start.6 = (s32[256]{0:T(256)S(1)}, s32[256]{0:T(256)}, u32[]{:S(2)}) copy-start(s32[256]{0:T(256)} %param.17) | copy-start | bytes 3076
  126.1 49.3 %collective-permute-start.9 = (bf16[92,128,128]{2,1,0:T(8,128)(2,1)}, bf16[92,128,128]{2,1,0:T(8,128)(2,1)S(1)}, u32[]{:S(2)}, u32[]{:S(2)}) collective-permute-start(bf16[92,128,128]{2,1,0:T(8,128)(2,1)} %get-tuple-element.34), channel_id=1, source_target_pairs={{8,2},{2,8},{10,4},{4,10},{12,6},{6,12},{14,1},{1,14},{9,3},{3,9},... | collective-permute-start | bytes 9043976 | tf_op jit(solution)/shard_map/ppermute | solution.py:393
  130.1 4.6 %collective-permute-start.7 = (bf16[1024,1024]{1,0:T(8,128)(2,1)}, bf16[1024,1024]{1,0:T(8,128)(2,1)}, u32[]{:S(2)}, u32[]{:S(2)}) collective-permute-start(bf16[1024,1024]{1,0:T(8,128)(2,1)} %get-tuple-element.32), channel_id=1, source_target_pairs={{0,8},{8,0},{2,10},{10,2},{4,12},{12,4},{6,14},{14,6},{1,9},{9,1},... | collective-permute-start | bytes 6291464 | tf_op jit(solution)/shard_map/ppermute | solution.py:393
  130.2 7.5 %collective-permute-start.8 = (bf16[1024,1024]{1,0:T(8,128)(2,1)}, bf16[1024,1024]{1,0:T(8,128)(2,1)}, u32[]{:S(2)}, u32[]{:S(2)}) collective-permute-start(bf16[1024,1024]{1,0:T(8,128)(2,1)} %get-tuple-element.33), channel_id=1, source_target_pairs={{0,8},{8,0},{2,10},{10,2},{4,12},{12,4},{6,14},{14,6},{1,9},{9,1},... | collective-permute-start | bytes 6291464 | tf_op jit(solution)/shard_map/ppermute | solution.py:393
  137.7 2.2 copy-start
  179.0 58.2 %collective-permute-start.10 = (bf16[15,128,128]{2,1,0:T(8,128)(2,1)S(1)}, bf16[15,128,128]{2,1,0:T(8,128)(2,1)S(1)}, u32[]{:S(2)}, u32[]{:S(2)}) collective-permute-start(bf16[15,128,128]{2,1,0:T(8,128)(2,1)S(1)} %get-tuple-element.35), channel_id=1, source_target_pairs={{0,0},{8,1},{2,2},{10,3},{4,4},{12,5},{6,6},{14,7},{1,8},{9,9},{3,... | collective-permute-start | bytes 1474568 | tf_op jit(solution)/shard_map/ppermute | solution.py:475
  220.3 17.0 %collective-permute-start.11 = (bf16[15,128,128]{2,1,0:T(8,128)(2,1)S(1)}, bf16[15,128,128]{2,1,0:T(8,128)(2,1)S(1)}, u32[]{:S(2)}, u32[]{:S(2)}) collective-permute-start(bf16[15,128,128]{2,1,0:T(8,128)(2,1)S(1)} %get-tuple-element.36), channel_id=1, source_target_pairs={{0,1},{8,2},{2,3},{10,4},{4,5},{12,6},{6,7},{14,0},{1,9},{9,10},{3... | collective-permute-start | bytes 1474568 | tf_op jit(solution)/shard_map/ppermute | solution.py:475
  220.4 20.8 %collective-permute-start.12 = (bf16[15,128,128]{2,1,0:T(8,128)(2,1)S(1)}, bf16[15,128,128]{2,1,0:T(8,128)(2,1)S(1)}, u32[]{:S(2)}, u32[]{:S(2)}) collective-permute-start(bf16[15,128,128]{2,1,0:T(8,128)(2,1)S(1)} %get-tuple-element.37), channel_id=1, source_target_pairs={{0,2},{8,3},{2,4},{10,5},{4,6},{12,7},{6,0},{14,1},{1,10},{9,11},{... | collective-permute-start | bytes 1474568 | tf_op jit(solution)/shard_map/ppermute | solution.py:475
  220.5 34.5 %collective-permute-start.13 = (bf16[15,128,128]{2,1,0:T(8,128)(2,1)S(1)}, bf16[15,128,128]{2,1,0:T(8,128)(2,1)S(1)}, u32[]{:S(2)}, u32[]{:S(2)}) collective-permute-start(bf16[15,128,128]{2,1,0:T(8,128)(2,1)S(1)} %get-tuple-element.38), channel_id=1, source_target_pairs={{0,3},{8,4},{2,5},{10,6},{4,7},{12,0},{6,1},{14,2},{1,11},{9,12},{... | collective-permute-start | bytes 1474568 | tf_op jit(solution)/shard_map/ppermute | solution.py:475
  225.0 70.3 %collective-permute-start.14 = (bf16[15,128,128]{2,1,0:T(8,128)(2,1)S(1)}, bf16[15,128,128]{2,1,0:T(8,128)(2,1)S(1)}, u32[]{:S(2)}, u32[]{:S(2)}) collective-permute-start(bf16[15,128,128]{2,1,0:T(8,128)(2,1)S(1)} %get-tuple-element.39), channel_id=1, source_target_pairs={{0,4},{8,5},{2,6},{10,7},{4,0},{12,1},{6,2},{14,3},{1,12},{9,13},{... | collective-permute-start | bytes 1474568 | tf_op jit(solution)/shard_map/ppermute | solution.py:475
  237.2 67.9 %collective-permute-start.15 = (bf16[15,128,128]{2,1,0:T(8,128)(2,1)S(1)}, bf16[15,128,128]{2,1,0:T(8,128)(2,1)S(1)}, u32[]{:S(2)}, u32[]{:S(2)}) collective-permute-start(bf16[15,128,128]{2,1,0:T(8,128)(2,1)S(1)} %get-tuple-element.40), channel_id=1, source_target_pairs={{0,5},{8,6},{2,7},{10,0},{4,1},{12,2},{6,3},{14,4},{1,13},{9,14},{... | collective-permute-start | bytes 1474568 | tf_op jit(solution)/shard_map/ppermute | solution.py:475
  237.4 81.1 %collective-permute-start.16 = (bf16[15,128,128]{2,1,0:T(8,128)(2,1)S(1)}, bf16[15,128,128]{2,1,0:T(8,128)(2,1)S(1)}, u32[]{:S(2)}, u32[]{:S(2)}) collective-permute-start(bf16[15,128,128]{2,1,0:T(8,128)(2,1)S(1)} %get-tuple-element.41), channel_id=1, source_target_pairs={{0,6},{8,7},{2,0},{10,1},{4,2},{12,3},{6,4},{14,5},{1,14},{9,15},{... | collective-permute-start | bytes 1474568 | tf_op jit(solution)/shard_map/ppermute | solution.py:475
  241.1 77.9 %collective-permute-start.17 = (bf16[15,128,128]{2,1,0:T(8,128)(2,1)S(1)}, bf16[15,128,128]{2,1,0:T(8,128)(2,1)S(1)}, u32[]{:S(2)}, u32[]{:S(2)}) collective-permute-start(bf16[15,128,128]{2,1,0:T(8,128)(2,1)S(1)} %get-tuple-element.42), channel_id=1, source_target_pairs={{0,7},{8,0},{2,1},{10,2},{4,3},{12,4},{6,5},{14,6},{1,15},{9,8},{3... | collective-permute-start | bytes 1474568 | tf_op jit(solution)/shard_map/ppermute | solution.py:475

commit v3 on v2

--- a/solution.py
+++ b/solution.py
@@ -44,12 +44,26 @@
     return [min(slots, 2 * H - 1 - t if low else H + t) for t in range(rows)]
 
 
-def pack_tables(pattern, base, low, packed_tiles):
+def pack_order(rows, low, small_first):
+    half = rows // 2
+    if low and small_first:
+        return [*range(half, rows), *range(half)]
+    return list(range(rows))
+
+
+def pack_starts(slots, rows, low, small_first):
+    table, starts, at = widths(slots, rows, low), [0] * rows, 0
+    for t in pack_order(rows, low, small_first):
+        starts[t] = at
+        at += table[t]
+    return starts
+
+
+def pack_tables(pattern, base, low, small_first, packed_tiles):
     rows, slots = pattern.shape[1:]
-    tables = [widths(slots, rows, side) for side in (False, True)]
-    width = jnp.where(low[:, None], jnp.array(tables[1]), jnp.array(tables[0]))
-    starts = [[sum(table[:t]) for t in range(rows)] for table in tables]
-    offset = jnp.where(low[:, None], jnp.array(starts[1]), jnp.array(starts[0]))
+    width = jnp.where(low[:, None], jnp.array(widths(slots, rows, True)), jnp.array(widths(slots, rows, False)))
+    starts = [jnp.array([pack_starts(slots, rows, side, first) for first in small_first]) for side in (False, True)]
+    offset = jnp.where(low[:, None], starts[1], starts[0])
     beyond = jnp.where(low[:, None, None], pattern <= base[:, None, None] + H - 2, pattern >= base[:, None, None])
     wanted = (pattern >= 0) & beyond
     earlier = jnp.arange(slots)[None, :] < jnp.arange(slots)[:, None]
@@ -162,16 +176,23 @@
         copy.wait()
 
 
-def product_kernel(
-    total, rows, meta, ftab, ztab, keep, col_of, f_home, f_came, far_a, far_b, far_c, znear, turned,
-    prod, lent_0, lent_1, packed, fd, zd, pd, zt, fpool, zpool, part, fsem, zsem, tsem, nsem, psem, osem,
-):
+def product_kernel(total, rows, half, meta, ftab, ztab, keep, col_of, f_home, f_came, far_a, far_b, far_c, znear, turned, *rest):
+    if half:
+        earlier, rest = rest[0], rest[1:]
+    prod, lent_0, lent_1, packed, fd, zd, pd, zt, fpool, zpool, part, fsem, zsem, tsem, nsem, esem, psem, osem = rest
     count, tile = f_home.shape[:2]
+    slots = count // rows
     span, wide = 3 * rows, 2 * H + 2
     base, odd = meta[BASE], meta[ODD]
+    few = rows // 2
+    here = odd if half == 0 else 1 - odd
+    mine = pl.ds(pl.multiple_of(here * few * tile, few * tile), few * tile)
     far_row = jnp.where(odd == 0, 0, 2 * rows)
     near_rows = pl.ds(pl.multiple_of(rows * tile * (1 - odd), rows * tile), 2 * rows * tile)
-    either(meta[MOVED], f_came, f_home, lambda fock: pltpu.make_async_copy(fock, fpool.at[:count], fsem).start())
+    f_part = pl.ds(here * (count // 2), count // 2)
+    either(
+        meta[MOVED], f_came, f_home, lambda fock: pltpu.make_async_copy(fock.at[f_part], fpool.at[: count // 2], fsem).start()
+    )
     for kind, far in enumerate((far_b, far_a, far_c)):
 
         @pl.when(meta[FAR] == kind)
@@ -182,49 +203,57 @@
     near_in.start()
     turn_in = pltpu.make_async_copy(turned, zt, tsem)
     turn_in.start()
-    fpool[count] = jnp.zeros(fpool.shape[1:], fpool.dtype)
+    if half:
+        others = pl.ds(pl.multiple_of(odd * few * tile, few * tile), few * tile)
+        early_in = pltpu.make_async_copy(earlier, pd.at[others], esem)
+        early_in.start()
+    fpool[count // 2] = jnp.zeros(fpool.shape[1:], fpool.dtype)
     zpool[far_a.shape[0]] = jnp.zeros(zpool.shape[1:], zpool.dtype)
 
     def clear(i, carry):
-        pd[pl.ds(pl.multiple_of(i * tile, tile), tile), :] = jnp.zeros((tile, pd.shape[1]), pd.dtype)
+        at = pl.ds(pl.multiple_of((here * few + i) * tile, tile), tile)
+        pd[at, :] = jnp.zeros((tile, pd.shape[1]), pd.dtype)
         return carry
 
-    lax.fori_loop(0, rows, clear, 0)
-    pltpu.make_async_copy(f_home, fpool.at[:count], fsem).wait()
-    densify(fpool, ftab, fd, 0, rows)
+    lax.fori_loop(0, few, clear, 0)
+    pltpu.make_async_copy(f_home.at[f_part], fpool.at[: count // 2], fsem).wait()
+    densify(fpool, ftab, fd, 0, few)
     pltpu.make_async_copy(far_a, zpool.at[: far_a.shape[0]], zsem).wait()
     densify(zpool, ztab, zd, far_row, rows)
     near_in.wait()
     step = 6 if wide % 6 == 0 else 2
-    for r in range(rows // 2):
+    for q in range(few // 2):
+        r = here * (few // 2) + q
         k0 = window(base, rows, r, total)
         kcols = pair_cols(k0, wide, tile)
 
-        def block(nb, carry, r=r, k0=k0, kcols=kcols):
+        def block(nb, carry, q=q, r=r, k0=k0, kcols=kcols):
             first = k0 + step * nb
             acc = jnp.dot(
-                fd[2 * r * tile : (2 * r + 2) * tile, kcols],
+                fd[2 * q * tile : (2 * q + 2) * tile, kcols],
                 zd[kcols, pair_cols(first, step, tile)],
                 preferred_element_type=jnp.float32,
             )
             for i in range(2):
                 for j in range(step):
                     piece = acc[i * tile : (i + 1) * tile, j * tile : (j + 1) * tile]
-                    piece = jnp.where(keep[2 * r + i, first + j] != 0, piece, 0.0)
+                    piece = jnp.where(keep[2 * q + i, first + j] != 0, piece, 0.0)
                     tiles_of(pd, 2 * r + i, first + j, tile)[...] = piece.astype(pd.dtype)
             return carry
 
         lax.fori_loop(0, wide // step, block, 0)
-    writes = [pltpu.make_async_copy(pd, prod, psem.at[0])]
+    writes = [pltpu.make_async_copy(pd.at[mine], prod, psem.at[0])]
     for i, lent in enumerate((lent_0, lent_1)):
         cols = pl.ds(pl.multiple_of((1 - odd + i) * rows * tile, rows * tile), rows * tile)
-        writes.append(pltpu.make_async_copy(pd.at[:, cols], lent, psem.at[1 + i]))
+        writes.append(pltpu.make_async_copy(pd.at[mine, cols], lent, psem.at[1 + i]))
     for write in writes:
         write.start()
     turn_in.wait()
+    if half:
+        early_in.wait()
     start = jnp.where(odd == 0, 0, rows)
     pairs = rows // 2
-    for m in range(pairs):
+    for m in range(half * pairs // 2, (half + 1) * pairs // 2):
         r = jnp.where(odd == 0, m, pairs - 1 - m)
         deep = 2 * (m + 1) * tile
         k_at = pl.ds(pl.multiple_of(jnp.where(odd == 0, 0, rows * tile - deep), 2 * tile), deep)
@@ -236,32 +265,40 @@
             preferred_element_type=jnp.float32,
         )
         part[pair_rows(2 * r, tile), pair_cols(n_at, n_wide, tile)] = acc.astype(part.dtype)
-    low_rows = [t for t, w in enumerate(widths(count // rows, rows, True)) for _ in range(w)]
-    high_rows = [t for t, w in enumerate(widths(count // rows, rows, False)) for _ in range(w)]
+    low_rows, high_rows = (
+        [t for t in pack_order(rows, low, True) for _ in range(widths(slots, rows, low)[t])] for low in (True, False)
+    )
+    skipped = half * (len(low_rows) - packed.shape[0])
     for p in range(packed.shape[0]):
-        t = jnp.where(odd == 1, low_rows[p], high_rows[p])
+        t = jnp.where(odd == 1, low_rows[skipped + p], high_rows[skipped + p])
         pltpu.make_async_copy(tiles_of(part, t, col_of[p], tile), packed.at[p], osem).start()
     pltpu.make_async_copy(packed, packed, osem).wait()
     for write in writes:
         write.wait()
 
 
-def own_kernel(total, rows, meta, col_of, turned, prod, lent_0, lent_1, near, zt, pd, acc_ref, out, sem, osem):
+def own_kernel(total, rows, meta, col_of, turned, prod_0, prod_1, *rest):
+    lent, (near, zt, pd, acc_ref, out, sem, osem) = rest[:-7], rest[-7:]
     count, tile = near.shape[:2]
     slots = count // rows
     base, odd = meta[BASE], meta[ODD]
     wide = 2 * H + 2
     own = rows * tile
+    few = own // 2
 
     def part(index, n):
         return pl.ds(pl.multiple_of(index * own, own), n * own)
 
-    copies = [
-        pltpu.make_async_copy(turned, zt, sem.at[0]),
-        pltpu.make_async_copy(prod, pd.at[part(odd, 1)], sem.at[1]),
-        pltpu.make_async_copy(lent_0, pd.at[part(1 - odd, 1), part(1 - odd, 1)], sem.at[2]),
-        pltpu.make_async_copy(lent_1, pd.at[part(1 - odd, 1), part(2 - odd, 1)], sem.at[3]),
-    ]
+    def half_rows(block, index):
+        return pl.ds(pl.multiple_of(block * own + index * few, few), few)
+
+    copies = [pltpu.make_async_copy(turned, zt, sem.at[0])]
+    for h, prod in enumerate((prod_0, prod_1)):
+        mine = half_rows(odd, odd if h == 0 else 1 - odd)
+        copies.append(pltpu.make_async_copy(prod, pd.at[mine], sem.at[len(copies)]))
+        theirs = half_rows(1 - odd, 1 - odd if h == 0 else odd)
+        for i in range(2):
+            copies.append(pltpu.make_async_copy(lent[2 * h + i], pd.at[theirs, part(1 - odd + i, 1)], sem.at[len(copies)]))
     for copy in copies:
         copy.start()
     pd[part(1 - odd, 1), part(2 * odd, 1)] = jnp.zeros((own, own), pd.dtype)
@@ -291,19 +328,22 @@
     outward.wait()
 
 
-def join_kernel(rows, place, where, near, far, *rest):
-    outs = rest
+def join_kernel(rows, place, where, near, far_0, far_1, *outs):
     slots = near.shape[0] // rows
-    tiles = far.shape[0]
+    few, tiles = far_0.shape[0], far_0.shape[0] + far_1.shape[0]
     for n, out in enumerate(outs):
         row = where[n]
 
         def one(s, carry, out=out, row=row):
             at = place[row, s]
 
-            @pl.when(at < tiles)
+            @pl.when(at < few)
             def _():
-                out[s] = near[row * slots + s] + far[at]
+                out[s] = near[row * slots + s] + far_0[at]
+
+            @pl.when((at >= few) & (at < tiles))
+            def _():
+                out[s] = near[row * slots + s] + far_1[at - few]
 
             @pl.when(at >= tiles)
             def _():
@@ -375,6 +415,7 @@
         jnp.stack([far_side[:, :slots], far_side[:, slots:], rpat[mid]]),
         jnp.stack([far_base, far_base, base]),
         jnp.stack([odd == 1, odd == 1, odd == 0]),
+        (False, True, True),
         packed_tiles,
     )
     origin = base - rows
@@ -432,27 +473,39 @@
     )
     packed_a, turned_far = lax.optimization_barrier((packed_a, turned_far))
     far_c = permute(packed_a, "far_c")
-    prod, lent_0, lent_1, packed = call(
-        functools.partial(product_kernel, total, rows),
-        [meta, fock_table, far_table, keep, far_cols],
-        [f_home, f_came, far_a, far_b, far_c, znear, turned_far],
-        [shape(rows * tile, span * tile), shape(rows * tile, rows * tile), shape(rows * tile, rows * tile), packed_shape],
-        [dense(rows, span), dense(span, span), dense(rows, span), dense(rows, rows)]
-        + [pool(count + 1), pool(packed_tiles + 1), dense(rows, 2 * H)]
-        + [dma] * 4
-        + [dma((3,)), dma],
-        name="product",
-        limit=50,
-        cost=27,
-    )
-    far = permute(packed, "outer")
-    lent_0, lent_1 = permute(lent_0, "pair"), permute(lent_1, "pair")
+    few = sum(widths(slots, rows, False)[: rows // 2])
+    half_count, half_rows = count // 2, rows // 2
+    prods, lents, fars = [], [], []
+    for half in range(2):
+        here = odd if half == 0 else 1 - odd
+        fock_half = lax.dynamic_slice_in_dim(jnp.where(fock_table == count, count + half_count, fock_table), here * half_rows, half_rows, 0)
+        fock_half = jnp.minimum(fock_half - here * half_count, half_count)
+        keep_half = lax.dynamic_slice_in_dim(keep, here * half_rows, half_rows, 0)
+        tiles_half = few if half == 0 else packed_tiles - few
+        prod, lent_0, lent_1, packed = call(
+            functools.partial(product_kernel, total, rows, half),
+            [meta, fock_half, far_table, keep_half, far_cols[few * half : few * half + tiles_half]],
+            [f_home, f_came, far_a, far_b, far_c, znear, turned_far, *prods],
+            [shape(half_rows * tile, span * tile)] + [shape(half_rows * tile, rows * tile)] * 2 + [shape(tiles_half, tile, tile)],
+            [dense(half_rows, span), dense(span, span), dense(rows, span), dense(rows, rows)]
+            + [pool(half_count + 1), pool(packed_tiles + 1), dense(rows, 2 * H)]
+            + [dma] * 5
+            + [dma((3,)), dma],
+            name="product",
+            limit=50,
+            cost=15,
+        )
+        if fars:
+            packed, fars[0] = lax.optimization_barrier((packed, fars[0]))
+        fars.append(permute(packed, "outer"))
+        lents += [permute(lent_0, "pair"), permute(lent_1, "pair")]
+        prods.append(prod)
     (near_sum,) = call(
         functools.partial(own_kernel, total, rows),
         [meta, own_cols],
-        [turned_own, prod, lent_0, lent_1],
+        [turned_own, *prods, *lents],
         [block_shape],
-        [dense(rows, 2 * rows), dense(2 * rows, span), dense(rows, span + 1), pool(count), dma((4,)), dma],
+        [dense(rows, 2 * rows), dense(2 * rows, span), dense(rows, span + 1), pool(count), dma((7,)), dma],
         name="own",
         limit=40,
         cost=0.1,
@@ -463,7 +516,7 @@
     outs = call(
         functools.partial(join_kernel, rows),
         [own_place, where],
-        [near_sum, far],
+        [near_sum, *fars],
         [shape(slots, tile, tile)] * count_cols,
         [],
         name="join",

time: 322 us -> 315 us (0.978)
  waiting for transfers between devices: 146 us -> 131 us
  Pallas kernels: 76 us -> 84.5 us
    ppermute x10 -> x13, waiting for transfers between devices: 71.6 us -> 58.7 us  [permute(): return lax.ppermute(x, AXES, plan[name])]
    pallas_call x7 -> x8, Pallas kernels: 76 us -> 84.5 us  [call(): pl.pallas_call(kernel, in_specs=[smem] * len(scalars) + [vmem if held_in...]
    ppermute x8, starting transfers between devices: 65.1 us -> 59.5 us  [body(): lax.ppermute(out, AXES, plan['shifts'][s])]
    ppermute x10 -> x13, starting transfers between devices: 20.6 us -> 24.3 us  [permute(): return lax.ppermute(x, AXES, plan[name])]
    unnamed x27 -> x33, local copies, waits for them, and re-layouts: 7.01 us -> 7.81 us
  transfers between devices with their start and end apart: 18 -> 21, of which waited for: 14 -> 15; matrix products, arithmetic and copies ran while one was open for 2% -> 3% of each run, Pallas kernels for 13% -> 19%
where the time goes in v3:
time: 315 us; the launch traced here: 314 us
  waiting for transfers between devices  131 us (42%)
  Pallas kernels  84.5 us (27%)
  starting transfers between devices  83.8 us (27%)
  local copies, waits for them, and re-layouts  9.9 us (3%)
  other arithmetic  4.2 us (1%)
    pallas_call x8, Pallas kernels, call(): pl.pallas_call(kernel, in_specs=[smem] * len(scalars) + [vmem if held_in...  84.5 us
    ppermute x8, waiting for transfers between devices, body(): lax.ppermute(out, AXES, plan['shifts'][s])  72.3 us
    ppermute x8, starting transfers between devices, body(): lax.ppermute(out, AXES, plan['shifts'][s])  59.5 us
    ppermute x13, waiting for transfers between devices, permute(): return lax.ppermute(x, AXES, plan[name])  58.7 us
    ppermute x13, starting transfers between devices, permute(): return lax.ppermute(x, AXES, plan[name])  24.3 us
    unnamed x33, local copies, waits for them, and re-layouts  7.81 us
  transfers between devices with their start and end apart: 21, of which 15 were waited for; matrix products, arithmetic and copies ran while one was open for 3% of the time, Pallas kernels for 19%

profile of v3, /device:TPU:14, one launch (start us, length us, event | category | flops | bytes accessed | tf_op | source)
XLA Modules:
  0.0 314.1 jit_solution(919911525312452877)
XLA Ops:
  0.0 1.9 collective-permute-start
  1.9 0.8 copy.39.pattern
  2.8 5.0 %pack.2 = bf16[92,128,128]{2,1,0:T(8,128)(2,1)S(1)} custom-call(s32[2]{0:T(128)S(1)} %pad_add_fusion.7.first, s32[256,15]{1,0:T(8,128)S(1)} %copy.39.pattern, bf16[120,128,128]{2,1,0:T(8,128)(2,1)} %bitcast.11.tiles.z_home), custom_call_target="tpu_custom_call" | custom-call | bytes 12000000 | tf_op jit(solution)/shard_map/pack/pallas_call | solution.py:372
  7.9 1.3 collective-permute-start.1
  9.2 1.3 collective-permute-start.2
  10.5 34.6 %collective-permute-done.1.far_a = bf16[92,128,128]{2,1,0:T(8,128)(2,1)S(1)} collective-permute-done((bf16[92,128,128]{2,1,0:T(8,128)(2,1)S(1)}, bf16[92,128,128]{2,1,0:T(8,128)(2,1)S(1)}, u32[]{:S(2)}, u32[]{:S(2)}) %collective-permute-start.1) | collective-permute-done | bytes 3014688 | tf_op jit(solution)/shard_map/ppermute | solution.py:434
  45.0 1.6 copy-done.5
  46.7 0.6 collective-permute-done.z_came.tiles
  47.3 3.2 %collective-permute-start.3 = (bf16[120,128,128]{2,1,0:T(8,128)(2,1)}, bf16[120,128,128]{2,1,0:T(8,128)(2,1)}, u32[]{:S(2)}, u32[]{:S(2)}) collective-permute-start(bf16[120,128,128]{2,1,0:T(8,128)(2,1)} %collective-permute-done.z_came.tiles), channel_id=1, source_target_pairs={{8,0},{10,2},{12,4},{14,6},{1,9},{3,11},{5,13},{7,15},{24,16},{26,... | collective-permute-start | bytes 11796488 | tf_op jit(solution)/shard_map/ppermute | solution.py:434
  50.6 3.0 collective-permute-start.4
  53.7 0.1 copy.41
  53.8 0.1 copy.42
  53.9 0.8 copy.40
  54.7 1.1 pad_add_fusion
  56.4 0.1 copy.54
  56.6 0.1 copy.49
  56.8 0.1 copy.58
  56.9 0.1 copy.52
  57.8 0.2 select_reduce_fusion.1
  58.0 6.6 %pack.3 = bf16[92,128,128]{2,1,0:T(8,128)(2,1)} custom-call(s32[2]{0:T(128)S(1)} %pad_add_fusion.8.first, s32[256,15]{1,0:T(8,128)S(1)} %copy.39.pattern, bf16[120,128,128]{2,1,0:T(8,128)(2,1)} %collective-permute-done.z_came.tiles), custom_call_target="tpu_custom_call" | custom-call | bytes 12000000 | tf_op jit(solution)/shard_map/pack/pallas_call | solution.py:372
  64.7 3.1 collective-permute-start.5
  67.8 13.0 %near.1 = (bf16[2048,3072]{1,0:T(8,128)(2,1)}, bf16[1024,1024]{1,0:T(8,128)(2,1)S(1)}, bf16[1024,2048]{1,0:T(8,128)(2,1)}) custom-call(s32[4]{0:T(128)S(1)} %pad_add_fusion.6.meta, s32[16,24]{1,0:T(8,128)S(1)} %compare_select_fusion.table, bf16[120,128,128]{2,1,0:T(8,128)(2,1)} %bitcast.11.tiles.z_home, ...), custom_call_target="tpu_custom_call" | custom-call | bytes 42000000 | tf_op jit(solution)/shard_map/near/pallas_call | solution.py:372
  80.9 1.3 copy-done.1
  82.2 2.2 collective-permute-start.6
  84.4 0.1 copy.46
  84.6 0.9 convert_reduce_fusion
  85.7 0.1 copy.59
  86.1 0.1 select_reduce_fusion.2
  86.2 0.1 select_reduce_fusion.4
  86.5 0.1 select_reduce_fusion
  86.6 0.1 select_reduce_fusion.3
  86.8 11.1 %collective-permute-done.4.f_came = bf16[120,128,128]{2,1,0:T(8,128)(2,1)} collective-permute-done((bf16[120,128,128]{2,1,0:T(8,128)(2,1)}, bf16[120,128,128]{2,1,0:T(8,128)(2,1)}, u32[]{:S(2)}, u32[]{:S(2)}) %collective-permute-start.4) | collective-permute-done | bytes 3932192 | tf_op jit(solution)/shard_map/ppermute | solution.py:434
  97.9 2.0 collective-permute-done.5.far_b
  99.8 16.7 %product.2 = (bf16[512,3072]{1,0:T(8,128)(2,1)}, bf16[512,1024]{1,0:T(8,128)(2,1)}, bf16[512,1024]{1,0:T(8,128)(2,1)}, bf16[38,128,128]{2,1,0:T(8,128)(2,1)S(1)}) custom-call(s32[4]{0:T(128)S(1)} %pad_add_fusion.6.meta, s32[4,24]{1,0:T(4,128)S(1)} %get-tuple-element.77.ftab, s32[8,24]{1,0:T(8,128)S(1)} %compare_select_fusion.2.ztab, ...), custom_call_target="tpu_custom_call" | custom-call | bytes 45000000 | tf_op jit(solution)/shard_map/product/pallas_call | solution.py:372
  116.6 4.0 %collective-permute-start.11 = (bf16[38,128,128]{2,1,0:T(8,128)(2,1)S(1)}, bf16[38,128,128]{2,1,0:T(8,128)(2,1)S(1)}, u32[]{:S(2)}, u32[]{:S(2)}) collective-permute-start(bf16[38,128,128]{2,1,0:T(8,128)(2,1)S(1)} %get-tuple-element.44), channel_id=1, source_target_pairs={{8,2},{2,8},{10,4},{4,10},{12,6},{6,12},{14,1},{1,14},{9,3},{3,9},... | collective-permute-start | bytes 3735560 | tf_op jit(solution)/shard_map/ppermute | solution.py:434
  120.7 17.9 %product.3 = (bf16[512,3072]{1,0:T(8,128)(2,1)}, bf16[512,1024]{1,0:T(8,128)(2,1)}, bf16[512,1024]{1,0:T(8,128)(2,1)}, bf16[54,128,128]{2,1,0:T(8,128)(2,1)}) custom-call(s32[4]{0:T(128)S(1)} %pad_add_fusion.6.meta, s32[4,24]{1,0:T(4,128)S(1)} %get-tuple-element.76.ftab, s32[8,24]{1,0:T(8,128)S(1)} %compare_select_fusion.2.ztab, ...), custom_call_target="tpu_custom_call" | custom-call | bytes 45000000 | tf_op jit(solution)/shard_map/product/pallas_call | solution.py:372
  138.7 1.1 copy-done.3
  139.7 1.9 collective-permute-start.12
  141.6 1.7 collective-permute-start.7
  143.4 0.4 collective-permute-start.9
  144.1 0.1 select_reduce_fusion.6.where
  144.3 1.7 collective-permute-done.7.rest_0_
  146.0 1.5 collective-permute-done.8.rest_1_
  147.5 1.5 collective-permute-done.9.rest_2_
  149.0 1.5 collective-permute-done.10.rest_3_
  150.5 1.9 copy-done.2
  152.4 17.6 %own.1.near = bf16[120,128,128]{2,1,0:T(8,128)(2,1)S(1)} custom-call(s32[4]{0:T(128)S(1)} %pad_add_fusion.6.meta, s32[8,15]{1,0:T(8,128)S(1)} %get-tuple-element.63.col_of, bf16[1024,2048]{1,0:T(8,128)(2,1)} %get-tuple-element.31.turned, bf16[512,3072]{1,0:T(8,128)(2,1)S(1)} %copy-done, bf16[512,3072]{1,0:T(8,128)(2,1)S(1)} %copy-done.2, ...), custom_call_target="tpu_custom_call" | custom-call | bytes 300000 | tf_op jit(solution)/shard_map/own/pallas_call | solution.py:372
  170.0 4.2 %collective-permute-done.12.far_1 = bf16[54,128,128]{2,1,0:T(8,128)(2,1)} collective-permute-done((bf16[54,128,128]{2,1,0:T(8,128)(2,1)}, bf16[54,128,128]{2,1,0:T(8,128)(2,1)}, u32[]{:S(2)}, u32[]{:S(2)}) %collective-permute-start.12) | collective-permute-done | bytes 1769504 | tf_op jit(solution)/shard_map/ppermute | solution.py:434
  174.2 5.1 %join.1 = (bf16[15,128,128]{2,1,0:T(8,128)(2,1)S(1)}, bf16[15,128,128]{2,1,0:T(8,128)(2,1)S(1)}, bf16[15,128,128]{2,1,0:T(8,128)(2,1)S(1)}, bf16[15,128,128]{2,1...) custom-call(s32[8,15]{1,0:T(8,128)S(1)} %compare_select_fusion.5.pla, ...), custom_call_target="tpu_custom_call" | custom-call | bytes 12000000 | tf_op jit(solution)/shard_map/join/pallas_call | solution.py:372
  179.3 38.2 %collective-permute-start.13 = (bf16[15,128,128]{2,1,0:T(8,128)(2,1)S(1)}, bf16[15,128,128]{2,1,0:T(8,128)(2,1)S(1)}, u32[]{:S(2)}, u32[]{:S(2)}) collective-permute-start(bf16[15,128,128]{2,1,0:T(8,128)(2,1)S(1)} %get-tuple-element.47), channel_id=1, source_target_pairs={{0,0},{8,1},{2,2},{10,3},{4,4},{12,5},{6,6},{14,7},{1,8},{9,9},{3,... | collective-permute-start | bytes 1474568 | tf_op jit(solution)/shard_map/ppermute | solution.py:528
  217.6 0.1 collective-permute-start.15
  217.7 6.1 %collective-permute-start.16 = (bf16[15,128,128]{2,1,0:T(8,128)(2,1)S(1)}, bf16[15,128,128]{2,1,0:T(8,128)(2,1)S(1)}, u32[]{:S(2)}, u32[]{:S(2)}) collective-permute-start(bf16[15,128,128]{2,1,0:T(8,128)(2,1)S(1)} %get-tuple-element.50), channel_id=1, source_target_pairs={{0,3},{8,4},{2,5},{10,6},{4,7},{12,0},{6,1},{14,2},{1,11},{9,12},{... | collective-permute-start | bytes 1474568 | tf_op jit(solution)/shard_map/ppermute | solution.py:528
  223.8 2.9 collective-permute-start.17
  226.7 7.7 %collective-permute-done.13.rest_0_ = bf16[15,128,128]{2,1,0:T(8,128)(2,1)S(1)} collective-permute-done((bf16[15,128,128]{2,1,0:T(8,128)(2,1)S(1)}, bf16[15,128,128]{2,1,0:T(8,128)(2,1)S(1)}, u32[]{:S(2)}, u32[]{:S(2)}) %collective-permute-start.13) | collective-permute-done | bytes 491552 | tf_op jit(solution)/shard_map/ppermute | solution.py:528
  234.4 6.1 %collective-permute-start.19 = (bf16[15,128,128]{2,1,0:T(8,128)(2,1)S(1)}, bf16[15,128,128]{2,1,0:T(8,128)(2,1)S(1)}, u32[]{:S(2)}, u32[]{:S(2)}) collective-permute-start(bf16[15,128,128]{2,1,0:T(8,128)(2,1)S(1)} %get-tuple-element.53), channel_id=1, source_target_pairs={{0,6},{8,7},{2,0},{10,1},{4,2},{12,3},{6,4},{14,5},{1,14},{9,15},{... | collective-permute-start | bytes 1474568 | tf_op jit(solution)/shard_map/ppermute | solution.py:528
  240.5 6.0 %collective-permute-start.20 = (bf16[15,128,128]{2,1,0:T(8,128)(2,1)S(1)}, bf16[15,128,128]{2,1,0:T(8,128)(2,1)S(1)}, u32[]{:S(2)}, u32[]{:S(2)}) collective-permute-start(bf16[15,128,128]{2,1,0:T(8,128)(2,1)S(1)} %get-tuple-element.54), channel_id=1, source_target_pairs={{0,7},{8,0},{2,1},{10,2},{4,3},{12,4},{6,5},{14,6},{1,15},{9,8},{3... | collective-permute-start | bytes 1474568 | tf_op jit(solution)/shard_map/ppermute | solution.py:528
  246.5 0.2 select_reduce_fusion.5
  246.7 0.1 convert_reduce_fusion.1
  246.9 0.4 collective-permute-done.16.rest_3_
  247.3 45.2 %collective-permute-done.17.rest_4_ = bf16[15,128,128]{2,1,0:T(8,128)(2,1)S(1)} collective-permute-done((bf16[15,128,128]{2,1,0:T(8,128)(2,1)S(1)}, bf16[15,128,128]{2,1,0:T(8,128)(2,1)S(1)}, u32[]{:S(2)}, u32[]{:S(2)}) %collective-permute-start.17) | collective-permute-done | bytes 491552 | tf_op jit(solution)/shard_map/ppermute | solution.py:528
  292.5 10.0 %collective-permute-done.18.rest_5_ = bf16[15,128,128]{2,1,0:T(8,128)(2,1)S(1)} collective-permute-done((bf16[15,128,128]{2,1,0:T(8,128)(2,1)S(1)}, bf16[15,128,128]{2,1,0:T(8,128)(2,1)S(1)}, u32[]{:S(2)}, u32[]{:S(2)}) %collective-permute-start.18) | collective-permute-done | bytes 491552 | tf_op jit(solution)/shard_map/ppermute | solution.py:528
  302.5 8.4 %collective-permute-done.19.rest_6_ = bf16[15,128,128]{2,1,0:T(8,128)(2,1)S(1)} collective-permute-done((bf16[15,128,128]{2,1,0:T(8,128)(2,1)S(1)}, bf16[15,128,128]{2,1,0:T(8,128)(2,1)S(1)}, u32[]{:S(2)}, u32[]{:S(2)}) %collective-permute-start.19) | collective-permute-done | bytes 491552 | tf_op jit(solution)/shard_map/ppermute | solution.py:528
  310.8 0.6 collective-permute-done.20.rest_7_
  311.4 2.5 gather.1
  (86 shorter events, 3.0 us)
Async XLA Ops:
  0.0 47.3 %collective-permute-start = (bf16[120,128,128]{2,1,0:T(8,128)(2,1)}, bf16[120,128,128]{2,1,0:T(8,128)(2,1)}, u32[]{:S(2)}, u32[]{:S(2)}) collective-permute-start(bf16[120,128,128]{2,1,0:T(8,128)(2,1)} %bitcast.11.tiles.z_home), channel_id=1, source_target_pairs={{1,8},{3,10},{5,12},{7,14},{8,1},{10,3},{12,5},{14,7},{17,24},{19,... | collective-permute-start | bytes 11796488 | tf_op jit(solution)/shard_map/ppermute | solution.py:434
  2.8 50.8 %copy-start.6 = (s32[256,15]{0,1:T(8,128)S(1)}, s32[256,15]{0,1:T(8,128)}, u32[]{:S(2)}) copy-start(s32[256,15]{0,1:T(8,128)} %param.12) | copy-start | bytes 46084
  2.8 50.9 %copy-start.7 = (s32[256,15]{0,1:T(8,128)S(1)}, s32[256,15]{0,1:T(8,128)}, u32[]{:S(2)}) copy-start(s32[256,15]{0,1:T(8,128)} %param.15) | copy-start | bytes 46084
  2.8 51.1 %copy-start.8 = (s32[256,15]{0,1:T(8,128)S(1)}, s32[256,15]{0,1:T(8,128)}, u32[]{:S(2)}) copy-start(s32[256,15]{0,1:T(8,128)} %param.16) | copy-start | bytes 46084
  7.9 37.2 %collective-permute-start.1 = (bf16[92,128,128]{2,1,0:T(8,128)(2,1)S(1)}, bf16[92,128,128]{2,1,0:T(8,128)(2,1)S(1)}, u32[]{:S(2)}, u32[]{:S(2)}) collective-permute-start(bf16[92,128,128]{2,1,0:T(8,128)(2,1)S(1)} %pack.2), channel_id=1, source_target_pairs={{2,8},{4,10},{6,12},{7,1},{8,14},{9,3},{11,5},{13,7},{18,24},{20,2... | collective-permute-start | bytes 9043976 | tf_op jit(solution)/shard_map/ppermute | solution.py:434
  9.2 58.6 %collective-permute-start.2 = (bf16[120,128,128]{2,1,0:T(8,128)(2,1)}, bf16[120,128,128]{2,1,0:T(8,128)(2,1)}, u32[]{:S(2)}, u32[]{:S(2)}) collective-permute-start(bf16[120,128,128]{2,1,0:T(8,128)(2,1)} %bitcast.11.tiles.z_home), channel_id=1, source_target_pairs={{0,8},{2,10},{4,12},{6,14},{9,1},{11,3},{13,5},{15,7},{16,24},{18,... | collective-permute-start | bytes 11796488 | tf_op jit(solution)/shard_map/ppermute | solution.py:434
  45.0 1.6 copy-start.5
  47.3 20.5 %collective-permute-start.3 = (bf16[120,128,128]{2,1,0:T(8,128)(2,1)}, bf16[120,128,128]{2,1,0:T(8,128)(2,1)}, u32[]{:S(2)}, u32[]{:S(2)}) collective-permute-start(bf16[120,128,128]{2,1,0:T(8,128)(2,1)} %collective-permute-done.z_came.tiles), channel_id=1, source_target_pairs={{8,0},{10,2},{12,4},{14,6},{1,9},{3,11},{5,13},{7,15},{24,16},{26,... | collective-permute-start | bytes 11796488 | tf_op jit(solution)/shard_map/ppermute | solution.py:434
  50.6 47.3 %collective-permute-start.4 = (bf16[120,128,128]{2,1,0:T(8,128)(2,1)}, bf16[120,128,128]{2,1,0:T(8,128)(2,1)}, u32[]{:S(2)}, u32[]{:S(2)}) collective-permute-start(bf16[120,128,128]{2,1,0:T(8,128)(2,1)} %bitcast.16.f_home), channel_id=1, source_target_pairs={{1,8},{3,10},{5,12},{7,14},{8,1},{10,3},{12,5},{14,7},{17,24},{19,... | collective-permute-start | bytes 11796488 | tf_op jit(solution)/shard_map/ppermute | solution.py:434
  64.7 20.8 %copy-start.10 = (s32[3,8]{1,0:T(4,128)S(1)}, s32[3,8]{1,0:T(4,128)}, u32[]{:S(2)}) copy-start(s32[3,8]{1,0:T(4,128)} %constant.148.clone) | copy-start | bytes 292
  64.7 20.8 %copy-start.11 = (s32[3,8]{1,0:T(4,128)S(1)}, s32[3,8]{1,0:T(4,128)}, u32[]{:S(2)}) copy-start(s32[3,8]{1,0:T(4,128)} %constant.147.clone) | copy-start | bytes 292
  64.7 20.8 %copy-start.12 = (s32[8]{0:T(128)S(1)}, s32[8]{0:T(128)}, u32[]{:S(2)}) copy-start(s32[8]{0:T(128)} %constant.146.clone) | copy-start | bytes 100
  64.7 20.8 %copy-start.13 = (s32[8]{0:T(128)S(1)}, s32[8]{0:T(128)}, u32[]{:S(2)}) copy-start(s32[8]{0:T(128)} %constant.145.clone) | copy-start | bytes 100
  64.7 35.1 %collective-permute-start.5 = (bf16[92,128,128]{2,1,0:T(8,128)(2,1)}, bf16[92,128,128]{2,1,0:T(8,128)(2,1)}, u32[]{:S(2)}, u32[]{:S(2)}) collective-permute-start(bf16[92,128,128]{2,1,0:T(8,128)(2,1)} %pack.3), channel_id=1, source_target_pairs={{8,2},{10,4},{12,6},{3,9},{5,11},{7,13},{24,18},{26,20},{28,22},{1... | collective-permute-start | bytes 9043976 | tf_op jit(solution)/shard_map/ppermute | solution.py:434
  80.9 1.3 copy-start.1
  82.2 17.7 %collective-permute-start.6 = (bf16[92,128,128]{2,1,0:T(8,128)(2,1)S(1)}, bf16[92,128,128]{2,1,0:T(8,128)(2,1)}, u32[]{:S(2)}, u32[]{:S(2)}) collective-permute-start(bf16[92,128,128]{2,1,0:T(8,128)(2,1)S(1)} %pack.2), channel_id=1, source_target_pairs={{15,16},{16,15}} | collective-permute-start | bytes 9043976 | tf_op jit(solution)/shard_map/ppermute | solution.py:434
  116.6 22.1 %collective-permute-start.11 = (bf16[38,128,128]{2,1,0:T(8,128)(2,1)S(1)}, bf16[38,128,128]{2,1,0:T(8,128)(2,1)S(1)}, u32[]{:S(2)}, u32[]{:S(2)}) collective-permute-start(bf16[38,128,128]{2,1,0:T(8,128)(2,1)S(1)} %get-tuple-element.44), channel_id=1, source_target_pairs={{8,2},{2,8},{10,4},{4,10},{12,6},{6,12},{14,1},{1,14},{9,3},{3,9},... | collective-permute-start | bytes 3735560 | tf_op jit(solution)/shard_map/ppermute | solution.py:434
  120.7 23.4 %copy-start.9 = (s32[256]{0:T(256)S(1)}, s32[256]{0:T(256)}, u32[]{:S(2)}) copy-start(s32[256]{0:T(256)} %param.17) | copy-start | bytes 3076
  120.7 29.8 %copy-start = (bf16[512,3072]{1,0:T(8,128)(2,1)S(1)}, bf16[512,3072]{1,0:T(8,128)(2,1)}, u32[]{:S(2)}) copy-start(bf16[512,3072]{1,0:T(8,128)(2,1)} %get-tuple-element.37.rest_0_.prod_0) | copy-start | bytes 9437188
  138.7 1.1 copy-start.3
  139.7 34.5 %collective-permute-start.12 = (bf16[54,128,128]{2,1,0:T(8,128)(2,1)}, bf16[54,128,128]{2,1,0:T(8,128)(2,1)}, u32[]{:S(2)}, u32[]{:S(2)}) collective-permute-start(bf16[54,128,128]{2,1,0:T(8,128)(2,1)} %get-tuple-element.46), channel_id=1, source_target_pairs={{8,2},{2,8},{10,4},{4,10},{12,6},{6,12},{14,1},{1,14},{9,3},{3,9},... | collective-permute-start | bytes 5308424 | tf_op jit(solution)/shard_map/ppermute | solution.py:434
  141.6 4.4 %collective-permute-start.7 = (bf16[512,1024]{1,0:T(8,128)(2,1)}, bf16[512,1024]{1,0:T(8,128)(2,1)}, u32[]{:S(2)}, u32[]{:S(2)}) collective-permute-start(bf16[512,1024]{1,0:T(8,128)(2,1)} %get-tuple-element.39), channel_id=1, source_target_pairs={{0,8},{8,0},{2,10},{10,2},{4,12},{12,4},{6,14},{14,6},{1,9},{9,1},... | collective-permute-start | bytes 3145736 | tf_op jit(solution)/shard_map/ppermute | solution.py:434
  143.4 4.1 %collective-permute-start.8 = (bf16[512,1024]{1,0:T(8,128)(2,1)}, bf16[512,1024]{1,0:T(8,128)(2,1)}, u32[]{:S(2)}, u32[]{:S(2)}) collective-permute-start(bf16[512,1024]{1,0:T(8,128)(2,1)} %get-tuple-element.40), channel_id=1, source_target_pairs={{0,8},{8,0},{2,10},{10,2},{4,12},{12,4},{6,14},{14,6},{1,9},{9,1},... | collective-permute-start | bytes 3145736 | tf_op jit(solution)/shard_map/ppermute | solution.py:434
  143.4 5.5 %collective-permute-start.9 = (bf16[512,1024]{1,0:T(8,128)(2,1)}, bf16[512,1024]{1,0:T(8,128)(2,1)}, u32[]{:S(2)}, u32[]{:S(2)}) collective-permute-start(bf16[512,1024]{1,0:T(8,128)(2,1)} %get-tuple-element.41), channel_id=1, source_target_pairs={{0,8},{8,0},{2,10},{10,2},{4,12},{12,4},{6,14},{14,6},{1,9},{9,1},... | collective-permute-start | bytes 3145736 | tf_op jit(solution)/shard_map/ppermute | solution.py:434
  143.9 6.6 %collective-permute-start.10 = (bf16[512,1024]{1,0:T(8,128)(2,1)}, bf16[512,1024]{1,0:T(8,128)(2,1)}, u32[]{:S(2)}, u32[]{:S(2)}) collective-permute-start(bf16[512,1024]{1,0:T(8,128)(2,1)} %get-tuple-element.42), channel_id=1, source_target_pairs={{0,8},{8,0},{2,10},{10,2},{4,12},{12,4},{6,14},{14,6},{1,9},{9,1},... | collective-permute-start | bytes 3145736 | tf_op jit(solution)/shard_map/ppermute | solution.py:434
  150.5 1.9 copy-start.2
  152.4 21.8 %copy-start.4 = (bf16[38,128,128]{2,1,0:T(8,128)(2,1)S(1)}, bf16[38,128,128]{2,1,0:T(8,128)(2,1)}, u32[]{:S(2)}) copy-start(bf16[38,128,128]{2,1,0:T(8,128)(2,1)} %copy-done.3) | copy-start | bytes 3735556
  179.3 55.0 %collective-permute-start.13 = (bf16[15,128,128]{2,1,0:T(8,128)(2,1)S(1)}, bf16[15,128,128]{2,1,0:T(8,128)(2,1)S(1)}, u32[]{:S(2)}, u32[]{:S(2)}) collective-permute-start(bf16[15,128,128]{2,1,0:T(8,128)(2,1)S(1)} %get-tuple-element.47), channel_id=1, source_target_pairs={{0,0},{8,1},{2,2},{10,3},{4,4},{12,5},{6,6},{14,7},{1,8},{9,9},{3,... | collective-permute-start | bytes 1474568 | tf_op jit(solution)/shard_map/ppermute | solution.py:528
  217.5 16.9 %collective-permute-start.14 = (bf16[15,128,128]{2,1,0:T(8,128)(2,1)S(1)}, bf16[15,128,128]{2,1,0:T(8,128)(2,1)S(1)}, u32[]{:S(2)}, u32[]{:S(2)}) collective-permute-start(bf16[15,128,128]{2,1,0:T(8,128)(2,1)S(1)} %get-tuple-element.48), channel_id=1, source_target_pairs={{0,1},{8,2},{2,3},{10,4},{4,5},{12,6},{6,7},{14,0},{1,9},{9,10},{3... | collective-permute-start | bytes 1474568 | tf_op jit(solution)/shard_map/ppermute | solution.py:528
  217.6 22.9 %collective-permute-start.15 = (bf16[15,128,128]{2,1,0:T(8,128)(2,1)S(1)}, bf16[15,128,128]{2,1,0:T(8,128)(2,1)S(1)}, u32[]{:S(2)}, u32[]{:S(2)}) collective-permute-start(bf16[15,128,128]{2,1,0:T(8,128)(2,1)S(1)} %get-tuple-element.49), channel_id=1, source_target_pairs={{0,2},{8,3},{2,4},{10,5},{4,6},{12,7},{6,0},{14,1},{1,10},{9,11},{... | collective-permute-start | bytes 1474568 | tf_op jit(solution)/shard_map/ppermute | solution.py:528
  217.7 29.6 %collective-permute-start.16 = (bf16[15,128,128]{2,1,0:T(8,128)(2,1)S(1)}, bf16[15,128,128]{2,1,0:T(8,128)(2,1)S(1)}, u32[]{:S(2)}, u32[]{:S(2)}) collective-permute-start(bf16[15,128,128]{2,1,0:T(8,128)(2,1)S(1)} %get-tuple-element.50), channel_id=1, source_target_pairs={{0,3},{8,4},{2,5},{10,6},{4,7},{12,0},{6,1},{14,2},{1,11},{9,12},{... | collective-permute-start | bytes 1474568 | tf_op jit(solution)/shard_map/ppermute | solution.py:528
  223.8 68.7 %collective-permute-start.17 = (bf16[15,128,128]{2,1,0:T(8,128)(2,1)S(1)}, bf16[15,128,128]{2,1,0:T(8,128)(2,1)S(1)}, u32[]{:S(2)}, u32[]{:S(2)}) collective-permute-start(bf16[15,128,128]{2,1,0:T(8,128)(2,1)S(1)} %get-tuple-element.51), channel_id=1, source_target_pairs={{0,4},{8,5},{2,6},{10,7},{4,0},{12,1},{6,2},{14,3},{1,12},{9,13},{... | collective-permute-start | bytes 1474568 | tf_op jit(solution)/shard_map/ppermute | solution.py:528
  234.4 68.1 %collective-permute-start.18 = (bf16[15,128,128]{2,1,0:T(8,128)(2,1)S(1)}, bf16[15,128,128]{2,1,0:T(8,128)(2,1)S(1)}, u32[]{:S(2)}, u32[]{:S(2)}) collective-permute-start(bf16[15,128,128]{2,1,0:T(8,128)(2,1)S(1)} %get-tuple-element.52), channel_id=1, source_target_pairs={{0,5},{8,6},{2,7},{10,0},{4,1},{12,2},{6,3},{14,4},{1,13},{9,14},{... | collective-permute-start | bytes 1474568 | tf_op jit(solution)/shard_map/ppermute | solution.py:528
  234.4 76.4 %collective-permute-start.19 = (bf16[15,128,128]{2,1,0:T(8,128)(2,1)S(1)}, bf16[15,128,128]{2,1,0:T(8,128)(2,1)S(1)}, u32[]{:S(2)}, u32[]{:S(2)}) collective-permute-start(bf16[15,128,128]{2,1,0:T(8,128)(2,1)S(1)} %get-tuple-element.53), channel_id=1, source_target_pairs={{0,6},{8,7},{2,0},{10,1},{4,2},{12,3},{6,4},{14,5},{1,14},{9,15},{... | collective-permute-start | bytes 1474568 | tf_op jit(solution)/shard_map/ppermute | solution.py:528
  240.5 70.9 %collective-permute-start.20 = (bf16[15,128,128]{2,1,0:T(8,128)(2,1)S(1)}, bf16[15,128,128]{2,1,0:T(8,128)(2,1)S(1)}, u32[]{:S(2)}, u32[]{:S(2)}) collective-permute-start(bf16[15,128,128]{2,1,0:T(8,128)(2,1)S(1)} %get-tuple-element.54), channel_id=1, source_target_pairs={{0,7},{8,0},{2,1},{10,2},{4,3},{12,4},{6,5},{14,6},{1,15},{9,8},{3... | collective-permute-start | bytes 1474568 | tf_op jit(solution)/shard_map/ppermute | solution.py:528

commit v4 on v3

--- a/solution.py
+++ b/solution.py
@@ -222,13 +222,14 @@
     densify(zpool, ztab, zd, far_row, rows)
     near_in.wait()
     step = 6 if wide % 6 == 0 else 2
+    inner = (base >= 2 * rows) & (base < total - 2 * rows)
     for q in range(few // 2):
         r = here * (few // 2) + q
         k0 = window(base, rows, r, total)
-        kcols = pair_cols(k0, wide, tile)
-
-        def block(nb, carry, q=q, r=r, k0=k0, kcols=kcols):
+
+        def block(nb, carry, q=q, r=r, k0=k0, skipped=0, deep=wide):
             first = k0 + step * nb
+            kcols = pair_cols(k0 + skipped, deep, tile)
             acc = jnp.dot(
                 fd[2 * q * tile : (2 * q + 2) * tile, kcols],
                 zd[kcols, pair_cols(first, step, tile)],
@@ -241,7 +242,17 @@
                     tiles_of(pd, 2 * r + i, first + j, tile)[...] = piece.astype(pd.dtype)
             return carry
 
-        lax.fori_loop(0, wide // step, block, 0)
+        @pl.when(inner)
+        def _(block=block):
+            for nb in range(wide // step):
+                low = max(0, step * nb - H + 1) // 2 * 2
+                high = min(wide, (step * (nb + 1) + H + 1) // 2 * 2)
+                block(nb, 0, skipped=low, deep=high - low)
+
+        @pl.when(jnp.logical_not(inner))
+        def _(block=block):
+            lax.fori_loop(0, wide // step, block, 0)
+
     writes = [pltpu.make_async_copy(pd.at[mine], prod, psem.at[0])]
     for i, lent in enumerate((lent_0, lent_1)):
         cols = pl.ds(pl.multiple_of((1 - odd + i) * rows * tile, rows * tile), rows * tile)
@@ -306,16 +317,26 @@
     for copy in copies:
         copy.wait()
     step = 6 if wide % 6 == 0 else 2
-    for r in range(rows // 2):
+    inner = (base >= 2 * rows) & (base < total - 2 * rows)
+    for m in range(rows // 2):
+        r = jnp.where(odd == 0, m, rows // 2 - 1 - m)
         k0 = window(base, rows, r, total)
 
-        def block(nb, carry, r=r, k0=k0):
+        def block(nb, carry, r=r, k0=k0, deep=2 * rows):
             cols = pair_cols(k0 + step * nb, step, tile)
-            acc = jnp.dot(zt[2 * r * tile : (2 * r + 2) * tile, :], pd[:, cols], preferred_element_type=jnp.float32)
-            acc_ref[2 * r * tile : (2 * r + 2) * tile, cols] = acc.astype(acc_ref.dtype)
+            k_at = pl.ds(pl.multiple_of(jnp.where(odd == 0, 0, 2 * rows - deep) * tile, 2 * tile), deep * tile)
+            acc = jnp.dot(zt[pair_rows(2 * r, tile), k_at], pd[k_at, cols], preferred_element_type=jnp.float32)
+            acc_ref[pair_rows(2 * r, tile), cols] = acc.astype(acc_ref.dtype)
             return carry
 
-        lax.fori_loop(0, wide // step, block, 0)
+        @pl.when(inner)
+        def _(block=block, m=m):
+            lax.fori_loop(0, wide // step, functools.partial(block, deep=min(2 * rows, 2 * m + H + 2)), 0)
+
+        @pl.when(jnp.logical_not(inner))
+        def _(block=block):
+            lax.fori_loop(0, wide // step, block, 0)
+
 
     def one(t, carry):
         for s in range(slots):

time: 315 us -> 313 us (level)
  Pallas kernels: 84.5 us -> 80.1 us
    pallas_call x8, Pallas kernels: 84.5 us -> 80.1 us  [call(): pl.pallas_call(kernel, in_specs=[smem] * len(scalars) + [vmem if held_in...]
    ppermute x13, waiting for transfers between devices: 58.7 us -> 62 us  [permute(): return lax.ppermute(x, AXES, plan[name])]
  transfers between devices with their start and end apart: 21 -> 21, of which waited for: 15 -> 15; matrix products, arithmetic and copies ran while one was open for 3% -> 3% of each run, Pallas kernels for 19% -> 18%
where the time goes in v4:
time: 313 us
  waiting for transfers between devices  134 us (43%)
  starting transfers between devices  84 us (27%)
  Pallas kernels  80.1 us (26%)
  local copies, waits for them, and re-layouts  9.9 us (3%)
  other arithmetic  4.2 us (1%)
    pallas_call x8, Pallas kernels, call(): pl.pallas_call(kernel, in_specs=[smem] * len(scalars) + [vmem if held_in...  80.1 us
    ppermute x8, waiting for transfers between devices, body(): lax.ppermute(out, AXES, plan['shifts'][s])  71.9 us
    ppermute x13, waiting for transfers between devices, permute(): return lax.ppermute(x, AXES, plan[name])  62 us
    ppermute x8, starting transfers between devices, body(): lax.ppermute(out, AXES, plan['shifts'][s])  59.9 us
    ppermute x13, starting transfers between devices, permute(): return lax.ppermute(x, AXES, plan[name])  24.1 us
    unnamed x33, local copies, waits for them, and re-layouts  7.81 us
  transfers between devices with their start and end apart: 21, of which 15 were waited for; matrix products, arithmetic and copies ran while one was open for 3% of the time, Pallas kernels for 18%

profile of v4, /device:TPU:14, one launch (start us, length us, event | category | flops | bytes accessed | tf_op | source)
XLA Modules:
  0.0 312.9 jit_solution(11754139247968637175)
XLA Ops:
  0.0 1.9 collective-permute-start
  1.9 0.8 copy.39.pattern
  2.8 5.0 %pack.2 = bf16[92,128,128]{2,1,0:T(8,128)(2,1)S(1)} custom-call(s32[2]{0:T(128)S(1)} %pad_add_fusion.7.first, s32[256,15]{1,0:T(8,128)S(1)} %copy.39.pattern, bf16[120,128,128]{2,1,0:T(8,128)(2,1)} %bitcast.11.tiles.z_home), custom_call_target="tpu_custom_call" | custom-call | bytes 12000000 | tf_op jit(solution)/shard_map/pack/pallas_call | solution.py:393
  7.9 1.3 collective-permute-start.1
  9.2 1.3 collective-permute-start.2
  10.5 34.6 %collective-permute-done.1.far_a = bf16[92,128,128]{2,1,0:T(8,128)(2,1)S(1)} collective-permute-done((bf16[92,128,128]{2,1,0:T(8,128)(2,1)S(1)}, bf16[92,128,128]{2,1,0:T(8,128)(2,1)S(1)}, u32[]{:S(2)}, u32[]{:S(2)}) %collective-permute-start.1) | collective-permute-done | bytes 3014688 | tf_op jit(solution)/shard_map/ppermute | solution.py:455
  45.0 1.6 copy-done.5
  46.7 0.6 collective-permute-done.z_came.tiles
  47.3 3.2 %collective-permute-start.3 = (bf16[120,128,128]{2,1,0:T(8,128)(2,1)}, bf16[120,128,128]{2,1,0:T(8,128)(2,1)}, u32[]{:S(2)}, u32[]{:S(2)}) collective-permute-start(bf16[120,128,128]{2,1,0:T(8,128)(2,1)} %collective-permute-done.z_came.tiles), channel_id=1, source_target_pairs={{8,0},{10,2},{12,4},{14,6},{1,9},{3,11},{5,13},{7,15},{24,16},{26,... | collective-permute-start | bytes 11796488 | tf_op jit(solution)/shard_map/ppermute | solution.py:455
  50.6 3.0 collective-permute-start.4
  53.7 0.1 copy.41
  53.8 0.1 copy.42
  53.9 0.8 copy.40
  54.7 1.1 pad_add_fusion
  56.4 0.1 copy.54
  56.6 0.1 copy.49
  56.8 0.1 copy.58
  56.9 0.1 copy.52
  57.8 0.2 select_reduce_fusion.1
  58.0 6.6 %pack.3 = bf16[92,128,128]{2,1,0:T(8,128)(2,1)} custom-call(s32[2]{0:T(128)S(1)} %pad_add_fusion.8.first, s32[256,15]{1,0:T(8,128)S(1)} %copy.39.pattern, bf16[120,128,128]{2,1,0:T(8,128)(2,1)} %collective-permute-done.z_came.tiles), custom_call_target="tpu_custom_call" | custom-call | bytes 12000000 | tf_op jit(solution)/shard_map/pack/pallas_call | solution.py:393
  64.7 3.1 collective-permute-start.5
  67.8 13.0 %near.1 = (bf16[2048,3072]{1,0:T(8,128)(2,1)}, bf16[1024,1024]{1,0:T(8,128)(2,1)S(1)}, bf16[1024,2048]{1,0:T(8,128)(2,1)}) custom-call(s32[4]{0:T(128)S(1)} %pad_add_fusion.6.meta, s32[16,24]{1,0:T(8,128)S(1)} %compare_select_fusion.table, bf16[120,128,128]{2,1,0:T(8,128)(2,1)} %bitcast.11.tiles.z_home, ...), custom_call_target="tpu_custom_call" | custom-call | bytes 42000000 | tf_op jit(solution)/shard_map/near/pallas_call | solution.py:393
  80.9 1.3 copy-done.1
  82.2 2.2 collective-permute-start.6
  84.4 0.1 copy.46
  84.6 0.9 convert_reduce_fusion
  85.7 0.1 copy.59
  86.1 0.1 select_reduce_fusion.2
  86.2 0.1 select_reduce_fusion.4
  86.5 0.1 select_reduce_fusion
  86.6 0.1 select_reduce_fusion.3
  86.8 11.1 %collective-permute-done.4.f_came = bf16[120,128,128]{2,1,0:T(8,128)(2,1)} collective-permute-done((bf16[120,128,128]{2,1,0:T(8,128)(2,1)}, bf16[120,128,128]{2,1,0:T(8,128)(2,1)}, u32[]{:S(2)}, u32[]{:S(2)}) %collective-permute-start.4) | collective-permute-done | bytes 3932192 | tf_op jit(solution)/shard_map/ppermute | solution.py:455
  97.9 2.0 collective-permute-done.5.far_b
  99.8 15.5 %product.2 = (bf16[512,3072]{1,0:T(8,128)(2,1)}, bf16[512,1024]{1,0:T(8,128)(2,1)}, bf16[512,1024]{1,0:T(8,128)(2,1)}, bf16[38,128,128]{2,1,0:T(8,128)(2,1)S(1)}) custom-call(s32[4]{0:T(128)S(1)} %pad_add_fusion.6.meta, s32[4,24]{1,0:T(4,128)S(1)} %get-tuple-element.77.ftab, s32[8,24]{1,0:T(8,128)S(1)} %compare_select_fusion.2.ztab, ...), custom_call_target="tpu_custom_call" | custom-call | bytes 45000000 | tf_op jit(solution)/shard_map/product/pallas_call | solution.py:393
  115.3 3.8 %collective-permute-start.11 = (bf16[38,128,128]{2,1,0:T(8,128)(2,1)S(1)}, bf16[38,128,128]{2,1,0:T(8,128)(2,1)S(1)}, u32[]{:S(2)}, u32[]{:S(2)}) collective-permute-start(bf16[38,128,128]{2,1,0:T(8,128)(2,1)S(1)} %get-tuple-element.44), channel_id=1, source_target_pairs={{8,2},{2,8},{10,4},{4,10},{12,6},{6,12},{14,1},{1,14},{9,3},{3,9},... | collective-permute-start | bytes 3735560 | tf_op jit(solution)/shard_map/ppermute | solution.py:455
  119.2 16.5 %product.3 = (bf16[512,3072]{1,0:T(8,128)(2,1)}, bf16[512,1024]{1,0:T(8,128)(2,1)}, bf16[512,1024]{1,0:T(8,128)(2,1)}, bf16[54,128,128]{2,1,0:T(8,128)(2,1)}) custom-call(s32[4]{0:T(128)S(1)} %pad_add_fusion.6.meta, s32[4,24]{1,0:T(4,128)S(1)} %get-tuple-element.76.ftab, s32[8,24]{1,0:T(8,128)S(1)} %compare_select_fusion.2.ztab, ...), custom_call_target="tpu_custom_call" | custom-call | bytes 45000000 | tf_op jit(solution)/shard_map/product/pallas_call | solution.py:393
  135.7 1.1 copy-done.3
  136.8 1.9 collective-permute-start.12
  138.7 1.7 collective-permute-start.7
  140.5 0.4 collective-permute-start.9
  141.2 0.1 select_reduce_fusion.6.where
  141.3 1.7 collective-permute-done.7.rest_0_
  143.1 1.5 collective-permute-done.8.rest_1_
  144.6 1.5 collective-permute-done.9.rest_2_
  146.1 1.5 collective-permute-done.10.rest_3_
  147.6 1.9 copy-done.2
  149.5 16.0 %own.1.near = bf16[120,128,128]{2,1,0:T(8,128)(2,1)S(1)} custom-call(s32[4]{0:T(128)S(1)} %pad_add_fusion.6.meta, s32[8,15]{1,0:T(8,128)S(1)} %get-tuple-element.63.col_of, bf16[1024,2048]{1,0:T(8,128)(2,1)} %get-tuple-element.31.turned, bf16[512,3072]{1,0:T(8,128)(2,1)S(1)} %copy-done, bf16[512,3072]{1,0:T(8,128)(2,1)S(1)} %copy-done.2, ...), custom_call_target="tpu_custom_call" | custom-call | bytes 300000 | tf_op jit(solution)/shard_map/own/pallas_call | solution.py:393
  165.4 7.5 %collective-permute-done.12.far_1 = bf16[54,128,128]{2,1,0:T(8,128)(2,1)} collective-permute-done((bf16[54,128,128]{2,1,0:T(8,128)(2,1)}, bf16[54,128,128]{2,1,0:T(8,128)(2,1)}, u32[]{:S(2)}, u32[]{:S(2)}) %collective-permute-start.12) | collective-permute-done | bytes 1769504 | tf_op jit(solution)/shard_map/ppermute | solution.py:455
  172.9 5.1 %join.1 = (bf16[15,128,128]{2,1,0:T(8,128)(2,1)S(1)}, bf16[15,128,128]{2,1,0:T(8,128)(2,1)S(1)}, bf16[15,128,128]{2,1,0:T(8,128)(2,1)S(1)}, bf16[15,128,128]{2,1...) custom-call(s32[8,15]{1,0:T(8,128)S(1)} %compare_select_fusion.5.pla, ...), custom_call_target="tpu_custom_call" | custom-call | bytes 12000000 | tf_op jit(solution)/shard_map/join/pallas_call | solution.py:393
  178.0 37.3 %collective-permute-start.13 = (bf16[15,128,128]{2,1,0:T(8,128)(2,1)S(1)}, bf16[15,128,128]{2,1,0:T(8,128)(2,1)S(1)}, u32[]{:S(2)}, u32[]{:S(2)}) collective-permute-start(bf16[15,128,128]{2,1,0:T(8,128)(2,1)S(1)} %get-tuple-element.47), channel_id=1, source_target_pairs={{0,0},{8,1},{2,2},{10,3},{4,4},{12,5},{6,6},{14,7},{1,8},{9,9},{3,... | collective-permute-start | bytes 1474568 | tf_op jit(solution)/shard_map/ppermute | solution.py:549
  215.4 0.1 collective-permute-start.15
  215.5 6.9 %collective-permute-start.16 = (bf16[15,128,128]{2,1,0:T(8,128)(2,1)S(1)}, bf16[15,128,128]{2,1,0:T(8,128)(2,1)S(1)}, u32[]{:S(2)}, u32[]{:S(2)}) collective-permute-start(bf16[15,128,128]{2,1,0:T(8,128)(2,1)S(1)} %get-tuple-element.50), channel_id=1, source_target_pairs={{0,3},{8,4},{2,5},{10,6},{4,7},{12,0},{6,1},{14,2},{1,11},{9,12},{... | collective-permute-start | bytes 1474568 | tf_op jit(solution)/shard_map/ppermute | solution.py:549
  222.3 3.1 %collective-permute-start.17 = (bf16[15,128,128]{2,1,0:T(8,128)(2,1)S(1)}, bf16[15,128,128]{2,1,0:T(8,128)(2,1)S(1)}, u32[]{:S(2)}, u32[]{:S(2)}) collective-permute-start(bf16[15,128,128]{2,1,0:T(8,128)(2,1)S(1)} %get-tuple-element.51), channel_id=1, source_target_pairs={{0,4},{8,5},{2,6},{10,7},{4,0},{12,1},{6,2},{14,3},{1,12},{9,13},{... | collective-permute-start | bytes 1474568 | tf_op jit(solution)/shard_map/ppermute | solution.py:549
  225.5 6.7 %collective-permute-done.13.rest_0_ = bf16[15,128,128]{2,1,0:T(8,128)(2,1)S(1)} collective-permute-done((bf16[15,128,128]{2,1,0:T(8,128)(2,1)S(1)}, bf16[15,128,128]{2,1,0:T(8,128)(2,1)S(1)}, u32[]{:S(2)}, u32[]{:S(2)}) %collective-permute-start.13) | collective-permute-done | bytes 491552 | tf_op jit(solution)/shard_map/ppermute | solution.py:549
  232.2 5.8 %collective-permute-start.19 = (bf16[15,128,128]{2,1,0:T(8,128)(2,1)S(1)}, bf16[15,128,128]{2,1,0:T(8,128)(2,1)S(1)}, u32[]{:S(2)}, u32[]{:S(2)}) collective-permute-start(bf16[15,128,128]{2,1,0:T(8,128)(2,1)S(1)} %get-tuple-element.53), channel_id=1, source_target_pairs={{0,6},{8,7},{2,0},{10,1},{4,2},{12,3},{6,4},{14,5},{1,14},{9,15},{... | collective-permute-start | bytes 1474568 | tf_op jit(solution)/shard_map/ppermute | solution.py:549
  237.9 6.7 %collective-permute-start.20 = (bf16[15,128,128]{2,1,0:T(8,128)(2,1)S(1)}, bf16[15,128,128]{2,1,0:T(8,128)(2,1)S(1)}, u32[]{:S(2)}, u32[]{:S(2)}) collective-permute-start(bf16[15,128,128]{2,1,0:T(8,128)(2,1)S(1)} %get-tuple-element.54), channel_id=1, source_target_pairs={{0,7},{8,0},{2,1},{10,2},{4,3},{12,4},{6,5},{14,6},{1,15},{9,8},{3... | collective-permute-start | bytes 1474568 | tf_op jit(solution)/shard_map/ppermute | solution.py:549
  244.6 0.2 select_reduce_fusion.5
  244.8 0.1 convert_reduce_fusion.1
  245.0 1.1 collective-permute-done.16.rest_3_
  246.1 44.2 %collective-permute-done.17.rest_4_ = bf16[15,128,128]{2,1,0:T(8,128)(2,1)S(1)} collective-permute-done((bf16[15,128,128]{2,1,0:T(8,128)(2,1)S(1)}, bf16[15,128,128]{2,1,0:T(8,128)(2,1)S(1)}, u32[]{:S(2)}, u32[]{:S(2)}) %collective-permute-start.17) | collective-permute-done | bytes 491552 | tf_op jit(solution)/shard_map/ppermute | solution.py:549
  290.3 10.0 %collective-permute-done.18.rest_5_ = bf16[15,128,128]{2,1,0:T(8,128)(2,1)S(1)} collective-permute-done((bf16[15,128,128]{2,1,0:T(8,128)(2,1)S(1)}, bf16[15,128,128]{2,1,0:T(8,128)(2,1)S(1)}, u32[]{:S(2)}, u32[]{:S(2)}) %collective-permute-start.18) | collective-permute-done | bytes 491552 | tf_op jit(solution)/shard_map/ppermute | solution.py:549
  300.2 9.4 %collective-permute-done.19.rest_6_ = bf16[15,128,128]{2,1,0:T(8,128)(2,1)S(1)} collective-permute-done((bf16[15,128,128]{2,1,0:T(8,128)(2,1)S(1)}, bf16[15,128,128]{2,1,0:T(8,128)(2,1)S(1)}, u32[]{:S(2)}, u32[]{:S(2)}) %collective-permute-start.19) | collective-permute-done | bytes 491552 | tf_op jit(solution)/shard_map/ppermute | solution.py:549
  309.6 0.6 collective-permute-done.20.rest_7_
  310.2 2.5 gather.1
  (86 shorter events, 3.0 us)
Async XLA Ops:
  0.0 47.3 %collective-permute-start = (bf16[120,128,128]{2,1,0:T(8,128)(2,1)}, bf16[120,128,128]{2,1,0:T(8,128)(2,1)}, u32[]{:S(2)}, u32[]{:S(2)}) collective-permute-start(bf16[120,128,128]{2,1,0:T(8,128)(2,1)} %bitcast.11.tiles.z_home), channel_id=1, source_target_pairs={{1,8},{3,10},{5,12},{7,14},{8,1},{10,3},{12,5},{14,7},{17,24},{19,... | collective-permute-start | bytes 11796488 | tf_op jit(solution)/shard_map/ppermute | solution.py:455
  2.8 50.8 %copy-start.6 = (s32[256,15]{0,1:T(8,128)S(1)}, s32[256,15]{0,1:T(8,128)}, u32[]{:S(2)}) copy-start(s32[256,15]{0,1:T(8,128)} %param.12) | copy-start | bytes 46084
  2.8 50.9 %copy-start.7 = (s32[256,15]{0,1:T(8,128)S(1)}, s32[256,15]{0,1:T(8,128)}, u32[]{:S(2)}) copy-start(s32[256,15]{0,1:T(8,128)} %param.15) | copy-start | bytes 46084
  2.8 51.1 %copy-start.8 = (s32[256,15]{0,1:T(8,128)S(1)}, s32[256,15]{0,1:T(8,128)}, u32[]{:S(2)}) copy-start(s32[256,15]{0,1:T(8,128)} %param.16) | copy-start | bytes 46084
  7.9 37.2 %collective-permute-start.1 = (bf16[92,128,128]{2,1,0:T(8,128)(2,1)S(1)}, bf16[92,128,128]{2,1,0:T(8,128)(2,1)S(1)}, u32[]{:S(2)}, u32[]{:S(2)}) collective-permute-start(bf16[92,128,128]{2,1,0:T(8,128)(2,1)S(1)} %pack.2), channel_id=1, source_target_pairs={{2,8},{4,10},{6,12},{7,1},{8,14},{9,3},{11,5},{13,7},{18,24},{20,2... | collective-permute-start | bytes 9043976 | tf_op jit(solution)/shard_map/ppermute | solution.py:455
  9.2 58.6 %collective-permute-start.2 = (bf16[120,128,128]{2,1,0:T(8,128)(2,1)}, bf16[120,128,128]{2,1,0:T(8,128)(2,1)}, u32[]{:S(2)}, u32[]{:S(2)}) collective-permute-start(bf16[120,128,128]{2,1,0:T(8,128)(2,1)} %bitcast.11.tiles.z_home), channel_id=1, source_target_pairs={{0,8},{2,10},{4,12},{6,14},{9,1},{11,3},{13,5},{15,7},{16,24},{18,... | collective-permute-start | bytes 11796488 | tf_op jit(solution)/shard_map/ppermute | solution.py:455
  45.0 1.6 copy-start.5
  47.3 20.5 %collective-permute-start.3 = (bf16[120,128,128]{2,1,0:T(8,128)(2,1)}, bf16[120,128,128]{2,1,0:T(8,128)(2,1)}, u32[]{:S(2)}, u32[]{:S(2)}) collective-permute-start(bf16[120,128,128]{2,1,0:T(8,128)(2,1)} %collective-permute-done.z_came.tiles), channel_id=1, source_target_pairs={{8,0},{10,2},{12,4},{14,6},{1,9},{3,11},{5,13},{7,15},{24,16},{26,... | collective-permute-start | bytes 11796488 | tf_op jit(solution)/shard_map/ppermute | solution.py:455
  50.6 47.3 %collective-permute-start.4 = (bf16[120,128,128]{2,1,0:T(8,128)(2,1)}, bf16[120,128,128]{2,1,0:T(8,128)(2,1)}, u32[]{:S(2)}, u32[]{:S(2)}) collective-permute-start(bf16[120,128,128]{2,1,0:T(8,128)(2,1)} %bitcast.16.f_home), channel_id=1, source_target_pairs={{1,8},{3,10},{5,12},{7,14},{8,1},{10,3},{12,5},{14,7},{17,24},{19,... | collective-permute-start | bytes 11796488 | tf_op jit(solution)/shard_map/ppermute | solution.py:455
  64.7 20.8 %copy-start.10 = (s32[3,8]{1,0:T(4,128)S(1)}, s32[3,8]{1,0:T(4,128)}, u32[]{:S(2)}) copy-start(s32[3,8]{1,0:T(4,128)} %constant.148.clone) | copy-start | bytes 292
  64.7 20.8 %copy-start.11 = (s32[3,8]{1,0:T(4,128)S(1)}, s32[3,8]{1,0:T(4,128)}, u32[]{:S(2)}) copy-start(s32[3,8]{1,0:T(4,128)} %constant.147.clone) | copy-start | bytes 292
  64.7 20.8 %copy-start.12 = (s32[8]{0:T(128)S(1)}, s32[8]{0:T(128)}, u32[]{:S(2)}) copy-start(s32[8]{0:T(128)} %constant.146.clone) | copy-start | bytes 100
  64.7 20.8 %copy-start.13 = (s32[8]{0:T(128)S(1)}, s32[8]{0:T(128)}, u32[]{:S(2)}) copy-start(s32[8]{0:T(128)} %constant.145.clone) | copy-start | bytes 100
  64.7 35.1 %collective-permute-start.5 = (bf16[92,128,128]{2,1,0:T(8,128)(2,1)}, bf16[92,128,128]{2,1,0:T(8,128)(2,1)}, u32[]{:S(2)}, u32[]{:S(2)}) collective-permute-start(bf16[92,128,128]{2,1,0:T(8,128)(2,1)} %pack.3), channel_id=1, source_target_pairs={{8,2},{10,4},{12,6},{3,9},{5,11},{7,13},{24,18},{26,20},{28,22},{1... | collective-permute-start | bytes 9043976 | tf_op jit(solution)/shard_map/ppermute | solution.py:455
  80.9 1.3 copy-start.1
  82.2 17.7 %collective-permute-start.6 = (bf16[92,128,128]{2,1,0:T(8,128)(2,1)S(1)}, bf16[92,128,128]{2,1,0:T(8,128)(2,1)}, u32[]{:S(2)}, u32[]{:S(2)}) collective-permute-start(bf16[92,128,128]{2,1,0:T(8,128)(2,1)S(1)} %pack.2), channel_id=1, source_target_pairs={{15,16},{16,15}} | collective-permute-start | bytes 9043976 | tf_op jit(solution)/shard_map/ppermute | solution.py:455
  115.3 20.4 %collective-permute-start.11 = (bf16[38,128,128]{2,1,0:T(8,128)(2,1)S(1)}, bf16[38,128,128]{2,1,0:T(8,128)(2,1)S(1)}, u32[]{:S(2)}, u32[]{:S(2)}) collective-permute-start(bf16[38,128,128]{2,1,0:T(8,128)(2,1)S(1)} %get-tuple-element.44), channel_id=1, source_target_pairs={{8,2},{2,8},{10,4},{4,10},{12,6},{6,12},{14,1},{1,14},{9,3},{3,9},... | collective-permute-start | bytes 3735560 | tf_op jit(solution)/shard_map/ppermute | solution.py:455
  119.2 21.9 %copy-start.9 = (s32[256]{0:T(256)S(1)}, s32[256]{0:T(256)}, u32[]{:S(2)}) copy-start(s32[256]{0:T(256)} %param.17) | copy-start | bytes 3076
  119.2 28.4 %copy-start = (bf16[512,3072]{1,0:T(8,128)(2,1)S(1)}, bf16[512,3072]{1,0:T(8,128)(2,1)}, u32[]{:S(2)}) copy-start(bf16[512,3072]{1,0:T(8,128)(2,1)} %get-tuple-element.37.rest_0_.prod_0) | copy-start | bytes 9437188
  135.7 1.1 copy-start.3
  136.8 36.1 %collective-permute-start.12 = (bf16[54,128,128]{2,1,0:T(8,128)(2,1)}, bf16[54,128,128]{2,1,0:T(8,128)(2,1)}, u32[]{:S(2)}, u32[]{:S(2)}) collective-permute-start(bf16[54,128,128]{2,1,0:T(8,128)(2,1)} %get-tuple-element.46), channel_id=1, source_target_pairs={{8,2},{2,8},{10,4},{4,10},{12,6},{6,12},{14,1},{1,14},{9,3},{3,9},... | collective-permute-start | bytes 5308424 | tf_op jit(solution)/shard_map/ppermute | solution.py:455
  138.7 4.4 %collective-permute-start.7 = (bf16[512,1024]{1,0:T(8,128)(2,1)}, bf16[512,1024]{1,0:T(8,128)(2,1)}, u32[]{:S(2)}, u32[]{:S(2)}) collective-permute-start(bf16[512,1024]{1,0:T(8,128)(2,1)} %get-tuple-element.39), channel_id=1, source_target_pairs={{0,8},{8,0},{2,10},{10,2},{4,12},{12,4},{6,14},{14,6},{1,9},{9,1},... | collective-permute-start | bytes 3145736 | tf_op jit(solution)/shard_map/ppermute | solution.py:455
  140.4 4.1 %collective-permute-start.8 = (bf16[512,1024]{1,0:T(8,128)(2,1)}, bf16[512,1024]{1,0:T(8,128)(2,1)}, u32[]{:S(2)}, u32[]{:S(2)}) collective-permute-start(bf16[512,1024]{1,0:T(8,128)(2,1)} %get-tuple-element.40), channel_id=1, source_target_pairs={{0,8},{8,0},{2,10},{10,2},{4,12},{12,4},{6,14},{14,6},{1,9},{9,1},... | collective-permute-start | bytes 3145736 | tf_op jit(solution)/shard_map/ppermute | solution.py:455
  140.5 5.5 %collective-permute-start.9 = (bf16[512,1024]{1,0:T(8,128)(2,1)}, bf16[512,1024]{1,0:T(8,128)(2,1)}, u32[]{:S(2)}, u32[]{:S(2)}) collective-permute-start(bf16[512,1024]{1,0:T(8,128)(2,1)} %get-tuple-element.41), channel_id=1, source_target_pairs={{0,8},{8,0},{2,10},{10,2},{4,12},{12,4},{6,14},{14,6},{1,9},{9,1},... | collective-permute-start | bytes 3145736 | tf_op jit(solution)/shard_map/ppermute | solution.py:455
  141.0 6.6 %collective-permute-start.10 = (bf16[512,1024]{1,0:T(8,128)(2,1)}, bf16[512,1024]{1,0:T(8,128)(2,1)}, u32[]{:S(2)}, u32[]{:S(2)}) collective-permute-start(bf16[512,1024]{1,0:T(8,128)(2,1)} %get-tuple-element.42), channel_id=1, source_target_pairs={{0,8},{8,0},{2,10},{10,2},{4,12},{12,4},{6,14},{14,6},{1,9},{9,1},... | collective-permute-start | bytes 3145736 | tf_op jit(solution)/shard_map/ppermute | solution.py:455
  147.6 1.9 copy-start.2
  149.5 23.5 %copy-start.4 = (bf16[38,128,128]{2,1,0:T(8,128)(2,1)S(1)}, bf16[38,128,128]{2,1,0:T(8,128)(2,1)}, u32[]{:S(2)}) copy-start(bf16[38,128,128]{2,1,0:T(8,128)(2,1)} %copy-done.3) | copy-start | bytes 3735556
  178.0 54.1 %collective-permute-start.13 = (bf16[15,128,128]{2,1,0:T(8,128)(2,1)S(1)}, bf16[15,128,128]{2,1,0:T(8,128)(2,1)S(1)}, u32[]{:S(2)}, u32[]{:S(2)}) collective-permute-start(bf16[15,128,128]{2,1,0:T(8,128)(2,1)S(1)} %get-tuple-element.47), channel_id=1, source_target_pairs={{0,0},{8,1},{2,2},{10,3},{4,4},{12,5},{6,6},{14,7},{1,8},{9,9},{3,... | collective-permute-start | bytes 1474568 | tf_op jit(solution)/shard_map/ppermute | solution.py:549
  215.3 16.9 %collective-permute-start.14 = (bf16[15,128,128]{2,1,0:T(8,128)(2,1)S(1)}, bf16[15,128,128]{2,1,0:T(8,128)(2,1)S(1)}, u32[]{:S(2)}, u32[]{:S(2)}) collective-permute-start(bf16[15,128,128]{2,1,0:T(8,128)(2,1)S(1)} %get-tuple-element.48), channel_id=1, source_target_pairs={{0,1},{8,2},{2,3},{10,4},{4,5},{12,6},{6,7},{14,0},{1,9},{9,10},{3... | collective-permute-start | bytes 1474568 | tf_op jit(solution)/shard_map/ppermute | solution.py:549
  215.4 22.6 %collective-permute-start.15 = (bf16[15,128,128]{2,1,0:T(8,128)(2,1)S(1)}, bf16[15,128,128]{2,1,0:T(8,128)(2,1)S(1)}, u32[]{:S(2)}, u32[]{:S(2)}) collective-permute-start(bf16[15,128,128]{2,1,0:T(8,128)(2,1)S(1)} %get-tuple-element.49), channel_id=1, source_target_pairs={{0,2},{8,3},{2,4},{10,5},{4,6},{12,7},{6,0},{14,1},{1,10},{9,11},{... | collective-permute-start | bytes 1474568 | tf_op jit(solution)/shard_map/ppermute | solution.py:549
  215.5 30.6 %collective-permute-start.16 = (bf16[15,128,128]{2,1,0:T(8,128)(2,1)S(1)}, bf16[15,128,128]{2,1,0:T(8,128)(2,1)S(1)}, u32[]{:S(2)}, u32[]{:S(2)}) collective-permute-start(bf16[15,128,128]{2,1,0:T(8,128)(2,1)S(1)} %get-tuple-element.50), channel_id=1, source_target_pairs={{0,3},{8,4},{2,5},{10,6},{4,7},{12,0},{6,1},{14,2},{1,11},{9,12},{... | collective-permute-start | bytes 1474568 | tf_op jit(solution)/shard_map/ppermute | solution.py:549
  222.3 67.9 %collective-permute-start.17 = (bf16[15,128,128]{2,1,0:T(8,128)(2,1)S(1)}, bf16[15,128,128]{2,1,0:T(8,128)(2,1)S(1)}, u32[]{:S(2)}, u32[]{:S(2)}) collective-permute-start(bf16[15,128,128]{2,1,0:T(8,128)(2,1)S(1)} %get-tuple-element.51), channel_id=1, source_target_pairs={{0,4},{8,5},{2,6},{10,7},{4,0},{12,1},{6,2},{14,3},{1,12},{9,13},{... | collective-permute-start | bytes 1474568 | tf_op jit(solution)/shard_map/ppermute | solution.py:549
  232.1 68.1 %collective-permute-start.18 = (bf16[15,128,128]{2,1,0:T(8,128)(2,1)S(1)}, bf16[15,128,128]{2,1,0:T(8,128)(2,1)S(1)}, u32[]{:S(2)}, u32[]{:S(2)}) collective-permute-start(bf16[15,128,128]{2,1,0:T(8,128)(2,1)S(1)} %get-tuple-element.52), channel_id=1, source_target_pairs={{0,5},{8,6},{2,7},{10,0},{4,1},{12,2},{6,3},{14,4},{1,13},{9,14},{... | collective-permute-start | bytes 1474568 | tf_op jit(solution)/shard_map/ppermute | solution.py:549
  232.2 77.5 %collective-permute-start.19 = (bf16[15,128,128]{2,1,0:T(8,128)(2,1)S(1)}, bf16[15,128,128]{2,1,0:T(8,128)(2,1)S(1)}, u32[]{:S(2)}, u32[]{:S(2)}) collective-permute-start(bf16[15,128,128]{2,1,0:T(8,128)(2,1)S(1)} %get-tuple-element.53), channel_id=1, source_target_pairs={{0,6},{8,7},{2,0},{10,1},{4,2},{12,3},{6,4},{14,5},{1,14},{9,15},{... | collective-permute-start | bytes 1474568 | tf_op jit(solution)/shard_map/ppermute | solution.py:549
  237.9 72.3 %collective-permute-start.20 = (bf16[15,128,128]{2,1,0:T(8,128)(2,1)S(1)}, bf16[15,128,128]{2,1,0:T(8,128)(2,1)S(1)}, u32[]{:S(2)}, u32[]{:S(2)}) collective-permute-start(bf16[15,128,128]{2,1,0:T(8,128)(2,1)S(1)} %get-tuple-element.54), channel_id=1, source_target_pairs={{0,7},{8,0},{2,1},{10,2},{4,3},{12,4},{6,5},{14,6},{1,15},{9,8},{3... | collective-permute-start | bytes 1474568 | tf_op jit(solution)/shard_map/ppermute | solution.py:549
